TPU v7x, 128 devices: a whole 4x4x4 slice. The times are simulated.
128 devices in a mesh: blk: 16 (over x_lo, y, core), layer: 8 (over z, x_hi).
Axes of the slice: x: 4 (x_hi: 2, x_lo: 2; x = x_hi * 2 + x_lo), y: 4, z: 4, core: 2. Of those that a mesh axis runs over, the one named last changes fastest.
Arguments:
- points: float32 [16384, 128], P('blk'), may hold values from -6 to 6
- inv_scale: float32 [128], replicated, may hold values from 0.01 to 0.25
- vectors: float32 [16384, 64], P('blk'), may hold values from -6 to 6
- noise: float32 [16384], P(('blk', 'layer')), may hold values from 0.1 to 1
Outputs:
- result: float32 [16384, 64], P(('blk', 'layer'))
All inputs are finite; a program needn't handle non-finite values.
Results may differ from a plain program's by a relative error of at most 0.0001.
Values sent between devices are 32-bit elements; how exact they have to be, the bound alone decides.
No kernel may reach another device: no remote copies, remote signals or barrier semaphores. Data moves between devices by JAX's collectives and lax.ppermute only.
A program may use at most 64 MiB of HBM per device.

v0:
```python
import jax
import jax.numpy as jnp
from jax import lax
from jax.sharding import PartitionSpec as P

ROOT_FIVE = 5.0**0.5
FIVE_THIRDS = 5.0 / 3.0


def passed_along(value, axis, steps):
    count = lax.axis_size(axis)
    pairs = [(source, (source + steps) % count) for source in range(count)]
    return lax.ppermute(value, axis, pairs)


def in_blocks(x, dim, count):
    before, after = (x.shape[:dim], x.shape[dim + 1 :])
    return jnp.moveaxis(x.reshape(*before, count, -1, *after), dim, 0)


def summed_on_arrival(x, axis, dim):
    count = lax.axis_size(axis)
    tiles = lax.all_to_all(in_blocks(x, dim, count), axis, 0, 0, tiled=True)
    return jnp.sum(tiles, axis=0)


def matern(left_scaled, right_scaled, right_norms):
    left_norms = jnp.sum(left_scaled * left_scaled, axis=1)
    cross = jnp.dot(
        left_scaled,
        right_scaled.T,
        precision=lax.Precision.HIGHEST,
        preferred_element_type=jnp.float32,
    )
    distance_sq = jnp.maximum(left_norms[:, None] + right_norms[None, :] - 2.0 * cross, 0.0)
    radius = jnp.sqrt(distance_sq)
    return (1.0 + ROOT_FIVE * radius + FIVE_THIRDS * distance_sq) * jnp.exp(-ROOT_FIVE * radius)


def per_device(points, inv_scale, vectors, noise):
    layers = lax.axis_size("layer")
    layer_index = lax.axis_index("layer")
    block_rows = points.shape[0]
    feature_count = points.shape[1]
    column_count = vectors.shape[1]
    piece_rows = block_rows // layers
    scaled = points * inv_scale[None, :]
    packed = jnp.concatenate([scaled, vectors], axis=1)
    own_piece = lax.dynamic_slice_in_dim(packed, layer_index * piece_rows, piece_rows, 0)
    arrived = [own_piece]
    for distance in range(1, layers):
        arrived.append(passed_along(own_piece, "blk", -distance))
    outgoing = jnp.stack(arrived, axis=0)
    partner = lax.all_to_all(outgoing, "layer", split_axis=0, concat_axis=0, tiled=True).reshape(
        block_rows, -1
    )
    partner_scaled = partner[:, :feature_count]
    partner_vectors = partner[:, feature_count:]
    partner_norms = jnp.sum(partner_scaled * partner_scaled, axis=1)
    tile_rows = min(512, block_rows)
    tile_count = block_rows // tile_rows
    query_scaled = scaled.reshape(tile_count, tile_rows, feature_count)
    query_vectors = vectors.reshape(tile_count, tile_rows, column_count)

    def visit(carry_sum, block_item):
        left_scaled, left_vectors = block_item
        kernel = matern(left_scaled, partner_scaled, partner_norms)
        direct = jnp.dot(
            kernel,
            partner_vectors,
            precision=lax.Precision.HIGHEST,
            preferred_element_type=jnp.float32,
        )
        carry_sum = carry_sum + lax.dot_general(
            kernel,
            left_vectors,
            (((0,), (0,)), ((), ())),
            precision=lax.Precision.HIGHEST,
            preferred_element_type=jnp.float32,
        )
        return (carry_sum, direct)

    mirrored, direct = lax.scan(
        visit, jnp.zeros((block_rows, column_count), jnp.float32), (query_scaled, query_vectors)
    )
    direct = direct.reshape(block_rows, column_count)
    mirrored = mirrored * (layer_index > 0).astype(jnp.float32)
    spread = lax.all_to_all(
        mirrored.reshape(layers, piece_rows, column_count),
        "layer",
        split_axis=0,
        concat_axis=0,
        tiled=True,
    )
    returned = jnp.zeros((piece_rows, column_count), jnp.float32)
    for distance in range(1, layers):
        returned = returned + passed_along(spread[distance], "blk", distance)
    own_sum = summed_on_arrival(direct, "layer", 0) + returned
    own_vectors = lax.dynamic_slice_in_dim(vectors, layer_index * piece_rows, piece_rows, 0)
    normalizer = float(block_rows * (2 * layers - 1)) ** (-0.5)
    return own_sum * normalizer + noise[:, None] * own_vectors


def solution(mesh):
    placed = (P("blk", None), P(), P("blk", None), P(("blk", "layer")))
    return jax.shard_map(
        per_device, mesh=mesh, in_specs=placed, out_specs=P(("blk", "layer"), None), check_vma=False
    )
```

profile of v0, /device:TPU:0, one launch (start us, length us, event | category | flops | bytes accessed | tf_op | source)
XLA Modules:
  0.0 105.8 jit_solution(9900573701751353240)
XLA Ops:
  0.0 1.3 %copy.22 = f32[1024,128]{0,1:T(8,128)S(1)} copy(f32[1024,128]{1,0:T(8,128)} %param.6) | data formatting | bytes 1048576 | tf_op args[0]
  2.7 3.5 %collective-permute-start = (f32[128,192]{0,1:T(8,128)S(1)}, f32[128,192]{0,1:T(8,128)S(1)}, u32[]{:S(2)}, u32[]{:S(2)}) collective-permute-start(f32[128,192]{0,1:T(8,128)S(1)} %get-tuple-element.110), channel_id=1, source_target_pairs={{0,120},{8,0},{16,8},{24,16},{32,24},{40,32},{48,40},{56,48},{64,5... | collective-permute-start | bytes 294920 | tf_op jit(solution)/shard_map/ppermute | solution.py:13
  7.2 2.9 %collective-permute-start.3 = (f32[128,192]{0,1:T(8,128)S(1)}, f32[128,192]{0,1:T(8,128)S(1)}, u32[]{:S(2)}, u32[]{:S(2)}) collective-permute-start(f32[128,192]{0,1:T(8,128)S(1)} %get-tuple-element.110), channel_id=1, source_target_pairs={{0,96},{8,104},{16,112},{24,120},{32,0},{40,8},{48,16},{56,24},{64... | collective-permute-start | bytes 294920 | tf_op jit(solution)/shard_map/ppermute | solution.py:13
  10.1 1.3 %collective-permute-start.5 = (f32[128,192]{0,1:T(8,128)S(1)}, f32[128,192]{0,1:T(8,128)S(1)}, u32[]{:S(2)}, u32[]{:S(2)}) collective-permute-start(f32[128,192]{0,1:T(8,128)S(1)} %get-tuple-element.110), channel_id=1, source_target_pairs={{0,80},{8,88},{16,96},{24,104},{32,112},{40,120},{48,0},{56,8},{64... | collective-permute-start | bytes 294920 | tf_op jit(solution)/shard_map/ppermute | solution.py:13
  12.0 3.2 %collective-permute-done.1 = f32[128,192]{0,1:T(8,128)S(1)} collective-permute-done((f32[128,192]{0,1:T(8,128)S(1)}, f32[128,192]{0,1:T(8,128)S(1)}, u32[]{:S(2)}, u32[]{:S(2)}) %collective-permute-start.1) | collective-permute-done | bytes 98336 | tf_op jit(solution)/shard_map/ppermute | solution.py:13
  16.5 2.4 %collective-permute-done.3 = f32[128,192]{0,1:T(8,128)S(1)} collective-permute-done((f32[128,192]{0,1:T(8,128)S(1)}, f32[128,192]{0,1:T(8,128)S(1)}, u32[]{:S(2)}, u32[]{:S(2)}) %collective-permute-start.3) | collective-permute-done | bytes 98336 | tf_op jit(solution)/shard_map/ppermute | solution.py:13
  19.5 2.3 %collective-permute-done.4 = f32[128,192]{0,1:T(8,128)S(1)} collective-permute-done((f32[128,192]{0,1:T(8,128)S(1)}, f32[128,192]{0,1:T(8,128)S(1)}, u32[]{:S(2)}, u32[]{:S(2)}) %collective-permute-start.4) | collective-permute-done | bytes 98336 | tf_op jit(solution)/shard_map/ppermute | solution.py:13
  22.4 1.5 %collective-permute-done.5 = f32[128,192]{0,1:T(8,128)S(1)} collective-permute-done((f32[128,192]{0,1:T(8,128)S(1)}, f32[128,192]{0,1:T(8,128)S(1)}, u32[]{:S(2)}, u32[]{:S(2)}) %collective-permute-start.5) | collective-permute-done | bytes 98336 | tf_op jit(solution)/shard_map/ppermute | solution.py:13
  25.7 7.5 %all-to-all-start = ((f32[8,128,192]{1,2,0:T(8,128)}), f32[8,128,192]{1,2,0:T(8,128)S(1)}, u32[]{:S(2)}, u32[]{:S(2)}) async-start(f32[8,128,192]{1,2,0:T(8,128)} %bitcast_dynamic-update-slice_fusion), calls=%async_computation | async-start | bytes 1572864 | tf_op jit(solution)/shard_map/all_to_all | solution.py:54
  33.4 1.0 copy.24
  34.4 14.4 %all-to-all-done = f32[8,128,192]{1,2,0:T(8,128)S(1)} async-done(((f32[8,128,192]{1,2,0:T(8,128)}), f32[8,128,192]{1,2,0:T(8,128)S(1)}, u32[]{:S(2)}, u32[]{:S(2)}) %all-to-all-start) | async-done | bytes 786464 | tf_op jit(solution)/shard_map/all_to_all | solution.py:54
  49.0 1.0 copy.26
  50.2 24.8 %while.13 = (s32[]{:T(128)}, f32[1024,64]{0,1:T(8,128)S(1)}, f32[2,512,64]{1,0,2:T(2,128)}, f32[2,512,128]{2,1,0:T(8,128)S(1)}, f32[1024]{0:T(1024)S(1)}, /*inde...) while((s32[]{:T(128)}, f32[1024,64]{0,1:T(8,128)S(1)}, ...), condition=%wide.region_3.4_spmd.clone, body=%wide.region_1.3_spmd.clone.sunk | while | flops 1616117248 | bytes 9052795 | solution.py:83
  50.4 4.1 %exponential_multiply_fusion.2 = f32[512,1024]{1,0:T(8,128)S(1)} fusion(f32[1024,128]{1,0:T(8,128)} %get-tuple-element.194, f32[1024]{0:T(1024)S(1)} %get-tuple-element.193, f32[512]{0:T(512)S(1)} %fusion.28, f32[2,512,128]{2,1,0:T(8,128)S(1)} %get-tuple-element.192, s32[]{:T(128)} %get-tuple-element.179), kind=kOutput, calls=%fused_computation.clone.1 | convolution fusion | flops 810549248 | bytes 2889732 | tf_op jit(solution)/shard_map/while/body/eval_jaxpr/dot_general | solution.py:29
  54.4 2.5 %convolution_add_fusion.2 = f32[1024,64]{0,1:T(8,128)S(1)} fusion(f32[512,1024]{1,0:T(8,128)S(1)} %exponential_multiply_fusion.2, f32[1024,64]{0,1:T(8,128)S(1)} %get-tuple-element.180, f32[2,512,64]{2,1,0:T(8,128)} %get-tuple-element.195, s32[]{:T(128)} %get-tuple-element.179, pred[]{:T(512)S(6)} %compare.3), kind=kOutput, calls=%fused_computation.1.clone.1 | convolution fusion | flops 402784256 | bytes 2884097 | tf_op jit(solution)/shard_map/while/body/eval_jaxpr/dot_general | solution.py:74
  56.9 2.2 %convolution_bitcast_fusion.2 = f32[1,512,64]{1,2,0:T(8,128)S(1)} fusion(f32[512,1024]{1,0:T(8,128)S(1)} %exponential_multiply_fusion.2, f32[1024,64]{1,0:T(8,128)S(1)} %get-tuple-element.196), kind=kOutput, calls=%fused_computation.2.clone.1 | convolution fusion | flops 402653184 | bytes 2490368 | tf_op jit(solution)/shard_map/while/body/eval_jaxpr/dot_general | solution.py:68
  59.2 3.4 %dynamic_update_slice.6 = f32[2,512,64]{1,0,2:T(2,128)} dynamic-update-slice(f32[2,512,64]{1,0,2:T(2,128)} %get-tuple-element.181, f32[1,512,64]{1,0,2:T(1,128)S(1)} %copy.41, s32[]{:T(128)} %get-tuple-element.179, s32[]{:T(128)} %constant.7.clone.1..sunk, s32[]{:T(128)} %constant.7.clone.1..sunk) | dynamic-update-slice | bytes 262148 | tf_op jit(solution)/shard_map/while/body/jit(dynamic_update_index_in_dim)/dynamic_update_slice | solution.py:83
  62.8 4.1 %exponential_multiply_fusion.2 = f32[512,1024]{1,0:T(8,128)S(1)} fusion(f32[1024,128]{1,0:T(8,128)} %get-tuple-element.194, f32[1024]{0:T(1024)S(1)} %get-tuple-element.193, f32[512]{0:T(512)S(1)} %fusion.28, f32[2,512,128]{2,1,0:T(8,128)S(1)} %get-tuple-element.192, s32[]{:T(128)} %get-tuple-element.179), kind=kOutput, calls=%fused_computation.clone.1 | convolution fusion | flops 810549248 | bytes 2889732 | tf_op jit(solution)/shard_map/while/body/eval_jaxpr/dot_general | solution.py:29
  66.9 2.5 %convolution_add_fusion.2 = f32[1024,64]{0,1:T(8,128)S(1)} fusion(f32[512,1024]{1,0:T(8,128)S(1)} %exponential_multiply_fusion.2, f32[1024,64]{0,1:T(8,128)S(1)} %get-tuple-element.180, f32[2,512,64]{2,1,0:T(8,128)} %get-tuple-element.195, s32[]{:T(128)} %get-tuple-element.179, pred[]{:T(512)S(6)} %compare.3), kind=kOutput, calls=%fused_computation.1.clone.1 | convolution fusion | flops 402784256 | bytes 2884097 | tf_op jit(solution)/shard_map/while/body/eval_jaxpr/dot_general | solution.py:74
  69.3 2.2 %convolution_bitcast_fusion.2 = f32[1,512,64]{1,2,0:T(8,128)S(1)} fusion(f32[512,1024]{1,0:T(8,128)S(1)} %exponential_multiply_fusion.2, f32[1024,64]{1,0:T(8,128)S(1)} %get-tuple-element.196), kind=kOutput, calls=%fused_computation.2.clone.1 | convolution fusion | flops 402653184 | bytes 2490368 | tf_op jit(solution)/shard_map/while/body/eval_jaxpr/dot_general | solution.py:68
  71.6 3.4 %dynamic_update_slice.6 = f32[2,512,64]{1,0,2:T(2,128)} dynamic-update-slice(f32[2,512,64]{1,0,2:T(2,128)} %get-tuple-element.181, f32[1,512,64]{1,0,2:T(1,128)S(1)} %copy.41, s32[]{:T(128)} %get-tuple-element.179, s32[]{:T(128)} %constant.7.clone.1..sunk, s32[]{:T(128)} %constant.7.clone.1..sunk) | dynamic-update-slice | bytes 262148 | tf_op jit(solution)/shard_map/while/body/jit(dynamic_update_index_in_dim)/dynamic_update_slice | solution.py:83
  75.8 3.4 %all-to-all-start.2 = ((f32[8,128,64]{1,2,0:T(8,128)}), f32[8,128,64]{1,2,0:T(8,128)S(1)}, u32[]{:S(2)}, u32[]{:S(2)}) async-start(f32[8,128,64]{1,2,0:T(8,128)} %copy_bitcast_fusion.1), calls=%async_computation.2 | async-start | bytes 524288 | tf_op jit(solution)/shard_map/all_to_all | solution.py:88
  79.2 1.2 %reshape_reshape.3 = f32[8,128,64]{1,0,2:T(8,128)S(1)} reshape(f32[2,512,64]{1,0,2:T(2,128)} %get-tuple-element.48) | data formatting | bytes 524288 | tf_op jit(solution)/shard_map/reshape;reshape | solution.py:18
  81.1 7.2 %all-to-all-done.2 = f32[8,128,64]{1,2,0:T(8,128)S(1)} async-done(((f32[8,128,64]{1,2,0:T(8,128)}), f32[8,128,64]{1,2,0:T(8,128)S(1)}, u32[]{:S(2)}, u32[]{:S(2)}) %all-to-all-start.2) | async-done | bytes 262176 | tf_op jit(solution)/shard_map/all_to_all | solution.py:88
  88.3 3.4 %all-to-all-start.1 = ((f32[8,128,64]{1,2,0:T(8,128)}), f32[8,128,64]{1,2,0:T(8,128)S(1)}, u32[]{:S(2)}, u32[]{:S(2)}) async-start(f32[8,128,64]{1,2,0:T(8,128)} %copy.29), calls=%async_computation.1 | async-start | bytes 524288 | tf_op jit(solution)/shard_map/all_to_all | solution.py:23
  91.8 1.9 %collective-permute-start.11 = (f32[128,64]{0,1:T(8,128)S(1)}, f32[128,64]{0,1:T(8,128)S(1)}, u32[]{:S(2)}, u32[]{:S(2)}) collective-permute-start(f32[128,64]{0,1:T(8,128)S(1)} %get-tuple-element.116), channel_id=1, source_target_pairs={{0,40},{8,48},{16,56},{24,64},{32,72},{40,80},{48,88},{56,96},{64,... | collective-permute-start | bytes 98312 | tf_op jit(solution)/shard_map/ppermute | solution.py:13
  93.7 2.8 %collective-permute-start.13 = (f32[128,64]{0,1:T(8,128)S(1)}, f32[128,64]{0,1:T(8,128)S(1)}, u32[]{:S(2)}, u32[]{:S(2)}) collective-permute-start(f32[128,64]{0,1:T(8,128)S(1)} %get-tuple-element.114), channel_id=1, source_target_pairs={{0,56},{8,64},{16,72},{24,80},{32,88},{40,96},{48,104},{56,112},{6... | collective-permute-start | bytes 98312 | tf_op jit(solution)/shard_map/ppermute | solution.py:13
  96.6 1.7 %collective-permute-done.10 = f32[128,64]{0,1:T(8,128)S(1)} collective-permute-done((f32[128,64]{0,1:T(8,128)S(1)}, f32[128,64]{0,1:T(8,128)S(1)}, u32[]{:S(2)}, u32[]{:S(2)}) %collective-permute-start.10) | collective-permute-done | bytes 32800 | tf_op jit(solution)/shard_map/ppermute | solution.py:13
  98.4 2.1 %all-to-all-done.1 = f32[8,128,64]{1,2,0:T(8,128)S(1)} async-done(((f32[8,128,64]{1,2,0:T(8,128)}), f32[8,128,64]{1,2,0:T(8,128)S(1)}, u32[]{:S(2)}, u32[]{:S(2)}) %all-to-all-start.1) | async-done | bytes 262176 | tf_op jit(solution)/shard_map/all_to_all | solution.py:23
  100.5 1.5 %collective-permute-done.7 = f32[128,64]{0,1:T(8,128)S(1)} collective-permute-done((f32[128,64]{0,1:T(8,128)S(1)}, f32[128,64]{0,1:T(8,128)S(1)}, u32[]{:S(2)}, u32[]{:S(2)}) %collective-permute-start.7) | collective-permute-done | bytes 32800 | tf_op jit(solution)/shard_map/ppermute | solution.py:13
  102.0 2.4 %collective-permute-done.8 = f32[128,64]{0,1:T(8,128)S(1)} collective-permute-done((f32[128,64]{0,1:T(8,128)S(1)}, f32[128,64]{0,1:T(8,128)S(1)}, u32[]{:S(2)}, u32[]{:S(2)}) %collective-permute-start.8) | collective-permute-done | bytes 32800 | tf_op jit(solution)/shard_map/ppermute | solution.py:13
  104.5 1.4 %multiply_add_fusion = f32[128,64]{0,1:T(8,128)} fusion(f32[1024,64]{0,1:T(8,128)} %param.8, s32[]{:T(128)S(6)} %select_n.4, f32[128,64]{0,1:T(8,128)S(1)} %reduce_sum.28, f32[128,64]{0,1:T(8,128)S(1)} %collective-permute-done.13, f32[128,64]{0,1:T(8,128)S(1)} %collective-permute-done.12, f32[128,64]{0,1:T(8,128)S(1)} %collective-permute-done.11, ...), kind=kLoop, calls=%fused_computation.34 | loop fusion | flops 81920 | bytes 328196 | tf_op jit(solution)/shard_map/add | solution.py:101
  (44 shorter events, 10.3 us)
Async XLA Ops:
  0.0 2.1 %copy-start = (f32[1024,64]{0,1:T(8,128)S(1)}, f32[1024,64]{0,1:T(8,128)}, u32[]{:S(2)}) copy-start(f32[1024,64]{0,1:T(8,128)} %param.8) | copy-start | bytes 786436
  2.7 7.4 %collective-permute-start = (f32[128,192]{0,1:T(8,128)S(1)}, f32[128,192]{0,1:T(8,128)S(1)}, u32[]{:S(2)}, u32[]{:S(2)}) collective-permute-start(f32[128,192]{0,1:T(8,128)S(1)} %get-tuple-element.110), channel_id=1, source_target_pairs={{0,120},{8,0},{16,8},{24,16},{32,24},{40,32},{48,40},{56,48},{64,5... | collective-permute-start | bytes 294920 | tf_op jit(solution)/shard_map/ppermute | solution.py:13
  6.2 9.0 %collective-permute-start.1 = (f32[128,192]{0,1:T(8,128)S(1)}, f32[128,192]{0,1:T(8,128)S(1)}, u32[]{:S(2)}, u32[]{:S(2)}) collective-permute-start(f32[128,192]{0,1:T(8,128)S(1)} %get-tuple-element.110), channel_id=1, source_target_pairs={{0,112},{8,120},{16,0},{24,8},{32,16},{40,24},{48,32},{56,40},{64,... | collective-permute-start | bytes 294920 | tf_op jit(solution)/shard_map/ppermute | solution.py:13
  6.9 8.9 %collective-permute-start.2 = (f32[128,192]{0,1:T(8,128)S(1)}, f32[128,192]{0,1:T(8,128)S(1)}, u32[]{:S(2)}, u32[]{:S(2)}) collective-permute-start(f32[128,192]{0,1:T(8,128)S(1)} %get-tuple-element.110), channel_id=1, source_target_pairs={{0,104},{8,112},{16,120},{24,0},{32,8},{40,16},{48,24},{56,32},{64... | collective-permute-start | bytes 294920 | tf_op jit(solution)/shard_map/ppermute | solution.py:13
  7.2 11.7 %collective-permute-start.3 = (f32[128,192]{0,1:T(8,128)S(1)}, f32[128,192]{0,1:T(8,128)S(1)}, u32[]{:S(2)}, u32[]{:S(2)}) collective-permute-start(f32[128,192]{0,1:T(8,128)S(1)} %get-tuple-element.110), channel_id=1, source_target_pairs={{0,96},{8,104},{16,112},{24,120},{32,0},{40,8},{48,16},{56,24},{64... | collective-permute-start | bytes 294920 | tf_op jit(solution)/shard_map/ppermute | solution.py:13
  10.1 11.7 %collective-permute-start.4 = (f32[128,192]{0,1:T(8,128)S(1)}, f32[128,192]{0,1:T(8,128)S(1)}, u32[]{:S(2)}, u32[]{:S(2)}) collective-permute-start(f32[128,192]{0,1:T(8,128)S(1)} %get-tuple-element.110), channel_id=1, source_target_pairs={{0,88},{8,96},{16,104},{24,112},{32,120},{40,0},{48,8},{56,16},{64... | collective-permute-start | bytes 294920 | tf_op jit(solution)/shard_map/ppermute | solution.py:13
  10.1 13.8 %collective-permute-start.5 = (f32[128,192]{0,1:T(8,128)S(1)}, f32[128,192]{0,1:T(8,128)S(1)}, u32[]{:S(2)}, u32[]{:S(2)}) collective-permute-start(f32[128,192]{0,1:T(8,128)S(1)} %get-tuple-element.110), channel_id=1, source_target_pairs={{0,80},{8,88},{16,96},{24,104},{32,112},{40,120},{48,0},{56,8},{64... | collective-permute-start | bytes 294920 | tf_op jit(solution)/shard_map/ppermute | solution.py:13
  15.2 9.8 %collective-permute-start.6 = (f32[128,192]{0,1:T(8,128)S(1)}, f32[128,192]{0,1:T(8,128)S(1)}, u32[]{:S(2)}, u32[]{:S(2)}) collective-permute-start(f32[128,192]{0,1:T(8,128)S(1)} %get-tuple-element.110), channel_id=1, source_target_pairs={{0,72},{8,80},{16,88},{24,96},{32,104},{40,112},{48,120},{56,0},{6... | collective-permute-start | bytes 294920 | tf_op jit(solution)/shard_map/ppermute | solution.py:13
  25.7 23.1 %all-to-all-start = ((f32[8,128,192]{1,2,0:T(8,128)}), f32[8,128,192]{1,2,0:T(8,128)S(1)}, u32[]{:S(2)}, u32[]{:S(2)}) async-start(f32[8,128,192]{1,2,0:T(8,128)} %bitcast_dynamic-update-slice_fusion), calls=%async_computation | async-start | bytes 1572864 | tf_op jit(solution)/shard_map/all_to_all | solution.py:54
  75.0 29.4 %copy-start.1 = (f32[128]{0:T(128)S(1)}, f32[128]{0:T(128)}, u32[]{:S(2)}) copy-start(f32[128]{0:T(128)} %param.9) | copy-start | bytes 1540
  75.8 12.5 %all-to-all-start.2 = ((f32[8,128,64]{1,2,0:T(8,128)}), f32[8,128,64]{1,2,0:T(8,128)S(1)}, u32[]{:S(2)}, u32[]{:S(2)}) async-start(f32[8,128,64]{1,2,0:T(8,128)} %copy_bitcast_fusion.1), calls=%async_computation.2 | async-start | bytes 524288 | tf_op jit(solution)/shard_map/all_to_all | solution.py:88
  88.3 12.1 %all-to-all-start.1 = ((f32[8,128,64]{1,2,0:T(8,128)}), f32[8,128,64]{1,2,0:T(8,128)S(1)}, u32[]{:S(2)}, u32[]{:S(2)}) async-start(f32[8,128,64]{1,2,0:T(8,128)} %copy.29), calls=%async_computation.1 | async-start | bytes 524288 | tf_op jit(solution)/shard_map/all_to_all | solution.py:23
  91.7 6.6 %collective-permute-start.10 = (f32[128,64]{0,1:T(8,128)S(1)}, f32[128,64]{0,1:T(8,128)S(1)}, u32[]{:S(2)}, u32[]{:S(2)}) collective-permute-start(f32[128,64]{0,1:T(8,128)S(1)} %get-tuple-element.117), channel_id=1, source_target_pairs={{0,32},{8,40},{16,48},{24,56},{32,64},{40,72},{48,80},{56,88},{64,... | collective-permute-start | bytes 98312 | tf_op jit(solution)/shard_map/ppermute | solution.py:13
  91.8 6.5 %collective-permute-start.11 = (f32[128,64]{0,1:T(8,128)S(1)}, f32[128,64]{0,1:T(8,128)S(1)}, u32[]{:S(2)}, u32[]{:S(2)}) collective-permute-start(f32[128,64]{0,1:T(8,128)S(1)} %get-tuple-element.116), channel_id=1, source_target_pairs={{0,40},{8,48},{16,56},{24,64},{32,72},{40,80},{48,88},{56,96},{64,... | collective-permute-start | bytes 98312 | tf_op jit(solution)/shard_map/ppermute | solution.py:13
  93.7 6.8 %collective-permute-start.12 = (f32[128,64]{0,1:T(8,128)S(1)}, f32[128,64]{0,1:T(8,128)S(1)}, u32[]{:S(2)}, u32[]{:S(2)}) collective-permute-start(f32[128,64]{0,1:T(8,128)S(1)} %get-tuple-element.115), channel_id=1, source_target_pairs={{0,48},{8,56},{16,64},{24,72},{32,80},{40,88},{48,96},{56,104},{64... | collective-permute-start | bytes 98312 | tf_op jit(solution)/shard_map/ppermute | solution.py:13
  93.7 6.7 %collective-permute-start.13 = (f32[128,64]{0,1:T(8,128)S(1)}, f32[128,64]{0,1:T(8,128)S(1)}, u32[]{:S(2)}, u32[]{:S(2)}) collective-permute-start(f32[128,64]{0,1:T(8,128)S(1)} %get-tuple-element.114), channel_id=1, source_target_pairs={{0,56},{8,64},{16,72},{24,80},{32,88},{40,96},{48,104},{56,112},{6... | collective-permute-start | bytes 98312 | tf_op jit(solution)/shard_map/ppermute | solution.py:13
  96.6 5.4 %collective-permute-start.7 = (f32[128,64]{0,1:T(8,128)S(1)}, f32[128,64]{0,1:T(8,128)S(1)}, u32[]{:S(2)}, u32[]{:S(2)}) collective-permute-start(f32[128,64]{0,1:T(8,128)S(1)} %get-tuple-element.119), channel_id=1, source_target_pairs={{0,8},{8,16},{16,24},{24,32},{32,40},{40,48},{48,56},{56,64},{64,7... | collective-permute-start | bytes 98312 | tf_op jit(solution)/shard_map/ppermute | solution.py:13
  98.3 6.1 %collective-permute-start.8 = (f32[128,64]{0,1:T(8,128)S(1)}, f32[128,64]{0,1:T(8,128)S(1)}, u32[]{:S(2)}, u32[]{:S(2)}) collective-permute-start(f32[128,64]{0,1:T(8,128)S(1)} %get-tuple-element.113), channel_id=1, source_target_pairs={{0,16},{8,24},{16,32},{24,40},{32,48},{40,56},{48,64},{56,72},{64,... | collective-permute-start | bytes 98312 | tf_op jit(solution)/shard_map/ppermute | solution.py:13
  98.4 6.1 %collective-permute-start.9 = (f32[128,64]{0,1:T(8,128)S(1)}, f32[128,64]{0,1:T(8,128)S(1)}, u32[]{:S(2)}, u32[]{:S(2)}) collective-permute-start(f32[128,64]{0,1:T(8,128)S(1)} %get-tuple-element.118), channel_id=1, source_target_pairs={{0,24},{8,32},{16,40},{24,48},{32,56},{40,64},{48,72},{56,80},{64,... | collective-permute-start | bytes 98312 | tf_op jit(solution)/shard_map/ppermute | solution.py:13
where the time goes:
time: 108 us; the launch traced here: 106 us
  waiting for transfers between devices  39.3 us (36%)
  starting transfers between devices  27.8 us (26%)
  local copies, waits for them, and re-layouts  17.3 us (16%)
  matrix products  17.3 us (16%)
  other arithmetic  3.91 us (4%)
    ppermute x14, waiting for transfers between devices, passed_along(): return lax.ppermute(value, axis, pairs)  15.5 us
    all_to_all x1, waiting for transfers between devices, per_device(): lax.all_to_all(outgoing, 'layer', split_axis=0, concat_axis=0, tiled=True)  14.4 us
    ppermute x14, starting transfers between devices, passed_along(): return lax.ppermute(value, axis, pairs)  13.5 us
    dot_general x2, matrix products, matern(): jnp.dot(left_scaled, right_scaled.T, precision=lax.Precision.HIGHEST, pre...  8.12 us
    unnamed x15, local copies, waits for them, and re-layouts  7.51 us
    all_to_all x1, starting transfers between devices, per_device(): lax.all_to_all(outgoing, 'layer', split_axis=0, concat_axis=0, tiled=True)  7.46 us
    all_to_all x1, waiting for transfers between devices, per_device(): lax.all_to_all(mirrored.reshape(layers, piece_rows, column_count), 'layer...  7.21 us
    dynamic_update_slice x4, local copies, waits for them, and re-layouts, per_device(): lax.scan(visit, jnp.zeros((block_rows, column_count), jnp.float32), (quer...  7.13 us
  transfers between devices with their start and end apart: 17, of which 11 were waited for; matrix products, arithmetic and copies ran while one was open for 7% of the time, Pallas kernels for 0%

commit v1 on v0

v1 whole, which is shorter than its diff:
```python
import jax
import jax.numpy as jnp
from jax import lax
from jax.experimental import pallas as pl
from jax.experimental.pallas import tpu as pltpu
from jax.sharding import PartitionSpec as P

F32 = jnp.float32
BF16 = jnp.bfloat16
ROOT_THREE = 3.0**0.5
POINT_SCALE = (5.0 / 3.0) ** 0.5
EXP2_SCALE = -ROOT_THREE * 1.4426950408889634
TINY = 1e-30
LANES = 128
CHUNK = 256

SHIFTS = (1, 2, 7, 6, 3, 5, 4)
FIRST_GROUP = 3


def passed_along(value, axis, steps):
    count = lax.axis_size(axis)
    pairs = [(source, (source + steps) % count) for source in range(count)]
    return lax.ppermute(value, axis, pairs)


def two_parts(x):
    high = x.astype(BF16)
    return high, (x - high.astype(F32)).astype(BF16)


def three_parts(x):
    high = x.astype(BF16)
    rest = x - high.astype(F32)
    middle = rest.astype(BF16)
    return high, middle, (rest - middle.astype(F32)).astype(BF16)


def side_by_side(*parts):
    return jnp.concatenate(parts, axis=1)


def stacked(*parts):
    return jnp.concatenate(parts, axis=0)


def across(left, right):
    return lax.dot_general(left, right, (((1,), (1,)), ((), ())), preferred_element_type=F32)


def pair_kernel(count, final, with_total, *refs):
    inv_ref, points_ref, vectors_t_ref = refs[:3]
    pieces = refs[3 : 3 + count]
    rest = refs[3 + count :]
    if with_total:
        total_in, rest = rest[0], rest[1:]
    if final:
        direct_ref, mirrored_ref, total, left, left_norms, left_vectors = rest
    else:
        total, mirrored_ref, left, left_norms, left_vectors = rest
    rows, feats = points_ref.shape
    columns = vectors_t_ref.shape[0]
    inv = inv_ref[...] * POINT_SCALE
    x = points_ref[...] * inv
    left_norms[...] = jnp.broadcast_to(jnp.sum(x * x, axis=1, keepdims=True), (rows, LANES))
    high, middle, low = three_parts(x * (-2.0))
    for place, part in enumerate((high, middle, high, middle, high, low)):
        left[:, place * feats : (place + 1) * feats] = part
    high, low = two_parts(vectors_t_ref[...])
    left_vectors[:columns, :] = high
    left_vectors[columns:, :] = low
    zero = jnp.zeros((columns, CHUNK), BF16)
    for pair in range(count // 2):
        held = [pieces[2 * pair][...], pieces[2 * pair + 1][...]]
        y = stacked(held[0][:LANES], held[1][:LANES]) * inv
        right_norms = jnp.sum((y * y).T, axis=0, keepdims=True)
        high, middle, low = three_parts(y)
        right = side_by_side(high, high, middle, middle, low, high)
        high, low = two_parts(side_by_side(held[0][LANES:], held[1][LANES:]))
        right_vectors = side_by_side(
            stacked(high, low), stacked(high, jnp.zeros_like(high))
        )
        mirrored = jnp.zeros((2 * columns, 2 * LANES), F32)
        for chunk in range(rows // CHUNK):
            here = pl.ds(chunk * CHUNK, CHUNK)
            cross = across(left[here, :], right)
            norms = left_norms[here, :]
            square = jnp.maximum(cross + side_by_side(norms, norms) + right_norms, TINY)
            radius = square * lax.rsqrt(square)
            kernel = ((radius + ROOT_THREE) * radius + 1.0) * jnp.exp2(radius * EXP2_SCALE)
            high, low = two_parts(kernel)
            direct = across(side_by_side(high, low), right_vectors)
            if pair > 0:
                total[here, :] += direct
            elif with_total:
                total[here, :] = total_in[here, :] + direct
            else:
                total[here, :] = direct
            own = left_vectors[:columns, here]
            own_low = left_vectors[columns:, here]
            mirrored = mirrored + jnp.dot(
                stacked(side_by_side(own, own), side_by_side(own_low, zero)),
                stacked(high, low),
                preferred_element_type=F32,
            )
        mirrored = mirrored[:columns] + mirrored[columns:]
        mirrored_ref[2 * pair, :, :] = mirrored[:, :LANES]
        mirrored_ref[2 * pair + 1, :, :] = mirrored[:, LANES:]
    if final:
        for piece in range(rows // LANES):
            turned = total[piece * LANES : (piece + 1) * LANES, :].T
            direct_ref[piece, :, :] = turned[:columns] + turned[columns:]


def paired(inv, points, vectors_t, pieces, total=None, final=False):
    rows, feats = points.shape
    columns = vectors_t.shape[0]
    count = len(pieces)
    whole = pl.BlockSpec(memory_space=pltpu.VMEM)
    mirrored_shape = jax.ShapeDtypeStruct((count, columns, LANES), F32)
    total_shape = jax.ShapeDtypeStruct((rows, 2 * columns), F32)
    scratch = [
        pltpu.VMEM((rows, 6 * feats), BF16),
        pltpu.VMEM((rows, LANES), F32),
        pltpu.VMEM((2 * columns, rows), BF16),
    ]
    if final:
        out_shape = (
            jax.ShapeDtypeStruct((rows // LANES, columns, LANES), F32),
            mirrored_shape,
        )
        scratch = [pltpu.VMEM(total_shape.shape, F32)] + scratch
    else:
        out_shape = (total_shape, mirrored_shape)
    args = [inv, points, vectors_t, *pieces] + ([] if total is None else [total])

    def body(*refs):
        pair_kernel(count, final, total is not None, *refs)

    return pl.pallas_call(
        body,
        out_shape=out_shape,
        in_specs=[whole] * len(args),
        out_specs=(whole, whole),
        scratch_shapes=scratch,
        compiler_params=pltpu.CompilerParams(vmem_limit_bytes=32 * 1024 * 1024),
        cost_estimate=pl.CostEstimate(
            flops=2 * rows * LANES * count * (6 * feats + 8 * columns),
            bytes_accessed=4 * (rows * (feats + columns) + count * 2 * LANES * LANES),
            transcendentals=0,
        ),
    )(*args)


def per_device(points, inv_scale, vectors, noise):
    layers = lax.axis_size("layer")
    layer_index = lax.axis_index("layer")
    rows = points.shape[0]
    piece_rows = rows // layers
    inv = inv_scale[None, :]
    vectors_t = vectors.T
    own_points = lax.dynamic_slice_in_dim(points, layer_index * piece_rows, piece_rows, 0)
    own_vectors = lax.dynamic_slice_in_dim(vectors_t, layer_index * piece_rows, piece_rows, 1)
    own = stacked(own_points, own_vectors)
    arrived = [passed_along(own, "blk", -shift) for shift in SHIFTS]
    total, back_first = paired(inv, points, vectors_t, [own] + arrived[:FIRST_GROUP])
    direct, back_last = paired(
        inv, points, vectors_t, arrived[FIRST_GROUP:], total=total, final=True
    )
    back = [back_first[i + 1] for i in range(FIRST_GROUP)]
    back += [back_last[i] for i in range(len(SHIFTS) - FIRST_GROUP)]
    tiles = lax.all_to_all(direct, "layer", 0, 0, tiled=True)
    returned = [passed_along(part, "blk", shift) for part, shift in zip(back, SHIFTS)]
    own_sum = jnp.sum(tiles, axis=0)
    for part in returned:
        own_sum = own_sum + part
    normalizer = float(rows * (2 * layers - 1)) ** (-0.5)
    return (own_sum * normalizer + noise[None, :] * own_vectors).T


def solution(mesh):
    placed = (P("blk", None), P(), P("blk", None), P(("blk", "layer")))
    return jax.shard_map(
        per_device, mesh=mesh, in_specs=placed, out_specs=P(("blk", "layer"), None), check_vma=False
    )
```

time: 108 us -> 46.8 us (0.43)
  the two profiles are of different devices: /device:TPU:0 before, /device:TPU:5 now
where the time goes in v1:
time: 46.8 us; the launch traced here: 46.5 us
  starting transfers between devices  29.8 us (64%)
  Pallas kernels  6.65 us (14%)
  waiting for transfers between devices  5.89 us (13%)
  local copies, waits for them, and re-layouts  3.38 us (7%)
  other arithmetic  0.66 us (1%)
    ppermute x14, starting transfers between devices, passed_along(): return lax.ppermute(value, axis, pairs)  22.1 us
    all_to_all x1, starting transfers between devices, per_device(): tiles = lax.all_to_all(direct, 'layer', 0, 0, tiled=True)  7.72 us
    pallas_call x2, Pallas kernels, paired(): pl.pallas_call(body, out_shape=out_shape, in_specs=[whole] * len(args), o...  6.65 us
    ppermute x14, waiting for transfers between devices, passed_along(): return lax.ppermute(value, axis, pairs)  5.89 us
    unnamed x8, local copies, waits for them, and re-layouts  1.69 us
  transfers between devices with their start and end apart: 15, of which 4 were waited for; matrix products, arithmetic and copies ran while one was open for 0% of the time, Pallas kernels for 6%

profile of v1, /device:TPU:5, one launch (start us, length us, event | category | flops | bytes accessed | tf_op | source)
XLA Modules:
  0.0 46.5 jit_solution(12534200560063832085)
XLA Ops:
  0.0 0.8 %dynamic-slice_bitcast_fusion = f32[64,128]{1,0:T(8,128)S(1)} fusion(f32[1024,64]{0,1:T(8,128)} %param.6, s32[]{:T(128)S(6)} %select_n.4), kind=kLoop, calls=%fused_computation.9 | loop fusion | bytes 65540 | tf_op jit(solution)/shard_map/dynamic_slice | solution.py:163
  0.8 0.8 %constant_dynamic-slice_fusion = f32[128,128]{1,0:T(8,128)S(1)} fusion(f32[1024,128]{1,0:T(8,128)} %refs_1_.3, s32[]{:T(128)S(6)} %select_n.4), kind=kLoop, calls=%fused_computation.10 | loop fusion | bytes 131076 | tf_op jit(solution)/shard_map/dynamic_slice | solution.py:162
  1.7 2.6 %collective-permute-start.6 = (f32[192,128]{1,0:T(8,128)S(1)}, f32[192,128]{1,0:T(8,128)S(1)}, u32[]{:S(2)}, u32[]{:S(2)}) collective-permute-start(f32[192,128]{1,0:T(8,128)S(1)} %pad_maximum_fusion.refs_3_), channel_id=1, source_target_pairs={{0,72},{8,80},{16,88},{24,96},{32,104},{40,112},{48,120},{56,0},{6... | collective-permute-start | bytes 294920 | tf_op jit(solution)/shard_map/ppermute | solution.py:24
  4.2 1.4 %collective-permute-start.5 = (f32[192,128]{1,0:T(8,128)S(1)}, f32[192,128]{1,0:T(8,128)S(1)}, u32[]{:S(2)}, u32[]{:S(2)}) collective-permute-start(f32[192,128]{1,0:T(8,128)S(1)} %pad_maximum_fusion.refs_3_), channel_id=1, source_target_pairs={{0,112},{8,120},{16,0},{24,8},{32,16},{40,24},{48,32},{56,40},{64,... | collective-permute-start | bytes 294920 | tf_op jit(solution)/shard_map/ppermute | solution.py:24
  5.6 0.7 %collective-permute-start.4 = (f32[192,128]{1,0:T(8,128)S(1)}, f32[192,128]{1,0:T(8,128)S(1)}, u32[]{:S(2)}, u32[]{:S(2)}) collective-permute-start(f32[192,128]{1,0:T(8,128)S(1)} %pad_maximum_fusion.refs_3_), channel_id=1, source_target_pairs={{0,120},{8,0},{16,8},{24,16},{32,24},{40,32},{48,40},{56,48},{64,5... | collective-permute-start | bytes 294920 | tf_op jit(solution)/shard_map/ppermute | solution.py:24
  6.4 1.3 %collective-permute-start.3 = (f32[192,128]{1,0:T(8,128)S(1)}, f32[192,128]{1,0:T(8,128)S(1)}, u32[]{:S(2)}, u32[]{:S(2)}) collective-permute-start(f32[192,128]{1,0:T(8,128)S(1)} %pad_maximum_fusion.refs_3_), channel_id=1, source_target_pairs={{0,96},{8,104},{16,112},{24,120},{32,0},{40,8},{48,16},{56,24},{64... | collective-permute-start | bytes 294920 | tf_op jit(solution)/shard_map/ppermute | solution.py:24
  7.6 4.0 %collective-permute-start.2 = (f32[192,128]{1,0:T(8,128)S(1)}, f32[192,128]{1,0:T(8,128)S(1)}, u32[]{:S(2)}, u32[]{:S(2)}) collective-permute-start(f32[192,128]{1,0:T(8,128)S(1)} %pad_maximum_fusion.refs_3_), channel_id=1, source_target_pairs={{0,88},{8,96},{16,104},{24,112},{32,120},{40,0},{48,8},{56,16},{64... | collective-permute-start | bytes 294920 | tf_op jit(solution)/shard_map/ppermute | solution.py:24
  11.6 0.0 collective-permute-done.6.refs_6_
  11.6 0.1 collective-permute-start
  11.7 0.0 copy-start.2
  11.7 0.6 %copy-done.2 = f32[128]{0:T(128)S(1)} copy-done((f32[128]{0:T(128)S(1)}, f32[128]{0:T(128)}, u32[]{:S(2)}) %copy-start.2) | copy-done | bytes 536
  12.4 1.0 %copy-done.1 = f32[1024,128]{1,0:T(8,128)S(1)} copy-done((f32[1024,128]{1,0:T(8,128)S(1)}, f32[1024,128]{1,0:T(8,128)}, u32[]{:S(2)}) %copy-start.1) | copy-done | bytes 524312
  13.4 3.0 %shard_map.46 = (f32[1024,128]{1,0:T(8,128)S(1)}, f32[4,64,128]{2,1,0:T(8,128)S(1)}) custom-call(f32[1,128]{1,0:T(1,128)S(1)} %bitcast.24, f32[1024,128]{1,0:T(8,128)S(1)} %copy-done.1, f32[64,1024]{1,0:T(8,128)S(1)} %bitcast.22, f32[192,128]{1,0:T(8,128)S(1)} %pad_maximum_fusion.refs_3_, f32[192,128]{1,0:T(8,128)S(1)} %collective-permute-done.4.refs_4_, ...), custom_call_target="tpu_custom_call" | custom-call | flops 1342177280 | bytes 1310720 | tf_op jit(solution)/shard_map/pallas_call | solution.py:140
  16.4 0.0 collective-permute-done.2.refs_5_
  16.4 2.1 %collective-permute-done.1.refs_4_ = f32[192,128]{1,0:T(8,128)S(1)} collective-permute-done((f32[192,128]{1,0:T(8,128)S(1)}, f32[192,128]{1,0:T(8,128)S(1)}, u32[]{:S(2)}, u32[]{:S(2)}) %collective-permute-start.1) | collective-permute-done | bytes 98336 | tf_op jit(solution)/shard_map/ppermute | solution.py:24
  18.5 0.5 %collective-permute-done.refs_3_ = f32[192,128]{1,0:T(8,128)S(1)} collective-permute-done((f32[192,128]{1,0:T(8,128)S(1)}, f32[192,128]{1,0:T(8,128)S(1)}, u32[]{:S(2)}, u32[]{:S(2)}) %collective-permute-start) | collective-permute-done | bytes 98336 | tf_op jit(solution)/shard_map/ppermute | solution.py:24
  19.0 3.7 %shard_map.47 = (f32[8,64,128]{2,1,0:T(8,128)}, f32[4,64,128]{2,1,0:T(8,128)S(1)}) custom-call(f32[1,128]{1,0:T(1,128)S(1)} %bitcast.25, f32[1024,128]{1,0:T(8,128)S(1)} %copy-done.1, f32[64,1024]{1,0:T(8,128)S(1)} %bitcast.23, f32[192,128]{1,0:T(8,128)S(1)} %collective-permute-done.refs_3_, f32[192,128]{1,0:T(8,128)S(1)} %collective-permute-done.1.refs_4_, ...), custom_call_target="tpu_custom_call" | custom-call | flops 1342177280 | bytes 1310720 | tf_op jit(solution)/shard_map/pallas_call | solution.py:140
  22.7 7.7 %all-to-all-start = ((f32[8,64,128]{2,1,0:T(8,128)}), f32[8,64,128]{2,1,0:T(8,128)S(1)}, u32[]{:S(2)}, u32[]{:S(2)}) async-start(f32[8,64,128]{2,1,0:T(8,128)} %get-tuple-element.10), calls=%async_computation | async-start | bytes 524288 | tf_op jit(solution)/shard_map/all_to_all | solution.py:172
  30.4 1.9 %collective-permute-start.7 = (f32[64,128]{1,0:T(8,128)S(1)}, f32[64,128]{1,0:T(8,128)S(1)}, u32[]{:S(2)}, u32[]{:S(2)}) collective-permute-start(f32[64,128]{1,0:T(8,128)S(1)} %get-tuple-element.13), channel_id=1, source_target_pairs={{0,8},{8,16},{16,24},{24,32},{32,40},{40,48},{48,56},{56,64},{64,7... | collective-permute-start | bytes 98312 | tf_op jit(solution)/shard_map/ppermute | solution.py:24
  32.3 0.1 collective-permute-start.9
  32.4 0.6 %collective-permute-start.8 = (f32[64,128]{1,0:T(8,128)S(1)}, f32[64,128]{1,0:T(8,128)S(1)}, u32[]{:S(2)}, u32[]{:S(2)}) collective-permute-start(f32[64,128]{1,0:T(8,128)S(1)} %get-tuple-element.15), channel_id=1, source_target_pairs={{0,16},{8,24},{16,32},{24,40},{32,48},{40,56},{48,64},{56,72},{64,... | collective-permute-start | bytes 98312 | tf_op jit(solution)/shard_map/ppermute | solution.py:24
  33.0 2.8 %collective-permute-start.10 = (f32[64,128]{1,0:T(8,128)S(1)}, f32[64,128]{1,0:T(8,128)S(1)}, u32[]{:S(2)}, u32[]{:S(2)}) collective-permute-start(f32[64,128]{1,0:T(8,128)S(1)} %get-tuple-element.16), channel_id=1, source_target_pairs={{0,48},{8,56},{16,64},{24,72},{32,80},{40,88},{48,96},{56,104},{64... | collective-permute-start | bytes 98312 | tf_op jit(solution)/shard_map/ppermute | solution.py:24
  35.8 0.3 collective-permute-start.13
  36.1 0.0 collective-permute-done.7
  36.1 4.3 %collective-permute-start.12 = (f32[64,128]{1,0:T(8,128)S(1)}, f32[64,128]{1,0:T(8,128)S(1)}, u32[]{:S(2)}, u32[]{:S(2)}) collective-permute-start(f32[64,128]{1,0:T(8,128)S(1)} %get-tuple-element.18), channel_id=1, source_target_pairs={{0,40},{8,48},{16,56},{24,64},{32,72},{40,80},{48,88},{56,96},{64,... | collective-permute-start | bytes 98312 | tf_op jit(solution)/shard_map/ppermute | solution.py:24
  40.4 0.0 collective-permute-done.9
  40.4 2.1 %collective-permute-start.11 = (f32[64,128]{1,0:T(8,128)S(1)}, f32[64,128]{1,0:T(8,128)S(1)}, u32[]{:S(2)}, u32[]{:S(2)}) collective-permute-start(f32[64,128]{1,0:T(8,128)S(1)} %get-tuple-element.19), channel_id=1, source_target_pairs={{0,24},{8,32},{16,40},{24,48},{32,56},{40,64},{48,72},{56,80},{64,... | collective-permute-start | bytes 98312 | tf_op jit(solution)/shard_map/ppermute | solution.py:24
  42.6 0.0 collective-permute-done.8
  42.6 0.0 collective-permute-done.13
  42.6 2.6 %collective-permute-done.12 = f32[64,128]{1,0:T(8,128)S(1)} collective-permute-done((f32[64,128]{1,0:T(8,128)S(1)}, f32[64,128]{1,0:T(8,128)S(1)}, u32[]{:S(2)}, u32[]{:S(2)}) %collective-permute-start.12) | collective-permute-done | bytes 32800 | tf_op jit(solution)/shard_map/ppermute | solution.py:24
  45.2 0.7 %collective-permute-done.11 = f32[64,128]{1,0:T(8,128)S(1)} collective-permute-done((f32[64,128]{1,0:T(8,128)S(1)}, f32[64,128]{1,0:T(8,128)S(1)}, u32[]{:S(2)}, u32[]{:S(2)}) %collective-permute-start.11) | collective-permute-done | bytes 32800 | tf_op jit(solution)/shard_map/ppermute | solution.py:24
  45.9 0.6 %add_bitcast_fusion = f32[128,64]{0,1:T(8,128)} fusion(f32[64,128]{1,0:T(8,128)S(1)} %collective-permute-done.13, f32[64,128]{1,0:T(8,128)S(1)} %collective-permute-done.12, f32[64,128]{1,0:T(8,128)S(1)} %collective-permute-done.11, f32[64,128]{1,0:T(8,128)S(1)} %collective-permute-done.10, f32[64,128]{1,0:T(8,128)S(1)} %collective-permute-done.9, ...), kind=kLoop, calls=%fused_computation.1 | loop fusion | flops 81920 | bytes 328196 | tf_op jit(solution)/shard_map/transpose | solution.py:178
  (15 shorter events, 0.1 us)
Async XLA Ops:
  0.0 11.7 %copy-start = (f32[1024,64]{0,1:T(8,128)S(1)}, f32[1024,64]{0,1:T(8,128)}, u32[]{:S(2)}) copy-start(f32[1024,64]{0,1:T(8,128)} %param.6) | copy-start | bytes 786436
  1.7 9.9 %collective-permute-start.6 = (f32[192,128]{1,0:T(8,128)S(1)}, f32[192,128]{1,0:T(8,128)S(1)}, u32[]{:S(2)}, u32[]{:S(2)}) collective-permute-start(f32[192,128]{1,0:T(8,128)S(1)} %pad_maximum_fusion.refs_3_), channel_id=1, source_target_pairs={{0,72},{8,80},{16,88},{24,96},{32,104},{40,112},{48,120},{56,0},{6... | collective-permute-start | bytes 294920 | tf_op jit(solution)/shard_map/ppermute | solution.py:24
  4.2 7.3 %collective-permute-start.5 = (f32[192,128]{1,0:T(8,128)S(1)}, f32[192,128]{1,0:T(8,128)S(1)}, u32[]{:S(2)}, u32[]{:S(2)}) collective-permute-start(f32[192,128]{1,0:T(8,128)S(1)} %pad_maximum_fusion.refs_3_), channel_id=1, source_target_pairs={{0,112},{8,120},{16,0},{24,8},{32,16},{40,24},{48,32},{56,40},{64,... | collective-permute-start | bytes 294920 | tf_op jit(solution)/shard_map/ppermute | solution.py:24
  5.6 6.1 %collective-permute-start.4 = (f32[192,128]{1,0:T(8,128)S(1)}, f32[192,128]{1,0:T(8,128)S(1)}, u32[]{:S(2)}, u32[]{:S(2)}) collective-permute-start(f32[192,128]{1,0:T(8,128)S(1)} %pad_maximum_fusion.refs_3_), channel_id=1, source_target_pairs={{0,120},{8,0},{16,8},{24,16},{32,24},{40,32},{48,40},{56,48},{64,5... | collective-permute-start | bytes 294920 | tf_op jit(solution)/shard_map/ppermute | solution.py:24
  6.4 10.0 %collective-permute-start.3 = (f32[192,128]{1,0:T(8,128)S(1)}, f32[192,128]{1,0:T(8,128)S(1)}, u32[]{:S(2)}, u32[]{:S(2)}) collective-permute-start(f32[192,128]{1,0:T(8,128)S(1)} %pad_maximum_fusion.refs_3_), channel_id=1, source_target_pairs={{0,96},{8,104},{16,112},{24,120},{32,0},{40,8},{48,16},{56,24},{64... | collective-permute-start | bytes 294920 | tf_op jit(solution)/shard_map/ppermute | solution.py:24
  7.6 8.8 %collective-permute-start.2 = (f32[192,128]{1,0:T(8,128)S(1)}, f32[192,128]{1,0:T(8,128)S(1)}, u32[]{:S(2)}, u32[]{:S(2)}) collective-permute-start(f32[192,128]{1,0:T(8,128)S(1)} %pad_maximum_fusion.refs_3_), channel_id=1, source_target_pairs={{0,88},{8,96},{16,104},{24,112},{32,120},{40,0},{48,8},{56,16},{64... | collective-permute-start | bytes 294920 | tf_op jit(solution)/shard_map/ppermute | solution.py:24
  11.6 6.9 %collective-permute-start.1 = (f32[192,128]{1,0:T(8,128)S(1)}, f32[192,128]{1,0:T(8,128)S(1)}, u32[]{:S(2)}, u32[]{:S(2)}) collective-permute-start(f32[192,128]{1,0:T(8,128)S(1)} %pad_maximum_fusion.refs_3_), channel_id=1, source_target_pairs={{0,104},{8,112},{16,120},{24,0},{32,8},{40,16},{48,24},{56,32},{64... | collective-permute-start | bytes 294920 | tf_op jit(solution)/shard_map/ppermute | solution.py:24
  11.6 7.4 %collective-permute-start = (f32[192,128]{1,0:T(8,128)S(1)}, f32[192,128]{1,0:T(8,128)S(1)}, u32[]{:S(2)}, u32[]{:S(2)}) collective-permute-start(f32[192,128]{1,0:T(8,128)S(1)} %pad_maximum_fusion.refs_3_), channel_id=1, source_target_pairs={{0,80},{8,88},{16,96},{24,104},{32,112},{40,120},{48,0},{56,8},{64... | collective-permute-start | bytes 294920 | tf_op jit(solution)/shard_map/ppermute | solution.py:24
  11.7 0.7 %copy-start.2 = (f32[128]{0:T(128)S(1)}, f32[128]{0:T(128)}, u32[]{:S(2)}) copy-start(f32[128]{0:T(128)} %param.5) | copy-start | bytes 1540
  12.3 1.0 %copy-start.1 = (f32[1024,128]{1,0:T(8,128)S(1)}, f32[1024,128]{1,0:T(8,128)}, u32[]{:S(2)}) copy-start(f32[1024,128]{1,0:T(8,128)} %refs_1_.3) | copy-start | bytes 1572868
  22.7 19.9 %all-to-all-start = ((f32[8,64,128]{2,1,0:T(8,128)}), f32[8,64,128]{2,1,0:T(8,128)S(1)}, u32[]{:S(2)}, u32[]{:S(2)}) async-start(f32[8,64,128]{2,1,0:T(8,128)} %get-tuple-element.10), calls=%async_computation | async-start | bytes 524288 | tf_op jit(solution)/shard_map/all_to_all | solution.py:172
  30.4 5.7 %collective-permute-start.7 = (f32[64,128]{1,0:T(8,128)S(1)}, f32[64,128]{1,0:T(8,128)S(1)}, u32[]{:S(2)}, u32[]{:S(2)}) collective-permute-start(f32[64,128]{1,0:T(8,128)S(1)} %get-tuple-element.13), channel_id=1, source_target_pairs={{0,8},{8,16},{16,24},{24,32},{32,40},{40,48},{48,56},{56,64},{64,7... | collective-permute-start | bytes 98312 | tf_op jit(solution)/shard_map/ppermute | solution.py:24
  32.3 8.1 %collective-permute-start.9 = (f32[64,128]{1,0:T(8,128)S(1)}, f32[64,128]{1,0:T(8,128)S(1)}, u32[]{:S(2)}, u32[]{:S(2)}) collective-permute-start(f32[64,128]{1,0:T(8,128)S(1)} %get-tuple-element.14), channel_id=1, source_target_pairs={{0,56},{8,64},{16,72},{24,80},{32,88},{40,96},{48,104},{56,112},{6... | collective-permute-start | bytes 98312 | tf_op jit(solution)/shard_map/ppermute | solution.py:24
  32.4 10.2 %collective-permute-start.8 = (f32[64,128]{1,0:T(8,128)S(1)}, f32[64,128]{1,0:T(8,128)S(1)}, u32[]{:S(2)}, u32[]{:S(2)}) collective-permute-start(f32[64,128]{1,0:T(8,128)S(1)} %get-tuple-element.15), channel_id=1, source_target_pairs={{0,16},{8,24},{16,32},{24,40},{32,48},{40,56},{48,64},{56,72},{64,... | collective-permute-start | bytes 98312 | tf_op jit(solution)/shard_map/ppermute | solution.py:24
  33.0 9.6 %collective-permute-start.10 = (f32[64,128]{1,0:T(8,128)S(1)}, f32[64,128]{1,0:T(8,128)S(1)}, u32[]{:S(2)}, u32[]{:S(2)}) collective-permute-start(f32[64,128]{1,0:T(8,128)S(1)} %get-tuple-element.16), channel_id=1, source_target_pairs={{0,48},{8,56},{16,64},{24,72},{32,80},{40,88},{48,96},{56,104},{64... | collective-permute-start | bytes 98312 | tf_op jit(solution)/shard_map/ppermute | solution.py:24
  35.8 6.8 %collective-permute-start.13 = (f32[64,128]{1,0:T(8,128)S(1)}, f32[64,128]{1,0:T(8,128)S(1)}, u32[]{:S(2)}, u32[]{:S(2)}) collective-permute-start(f32[64,128]{1,0:T(8,128)S(1)} %get-tuple-element.17), channel_id=1, source_target_pairs={{0,32},{8,40},{16,48},{24,56},{32,64},{40,72},{48,80},{56,88},{64,... | collective-permute-start | bytes 98312 | tf_op jit(solution)/shard_map/ppermute | solution.py:24
  36.1 9.1 %collective-permute-start.12 = (f32[64,128]{1,0:T(8,128)S(1)}, f32[64,128]{1,0:T(8,128)S(1)}, u32[]{:S(2)}, u32[]{:S(2)}) collective-permute-start(f32[64,128]{1,0:T(8,128)S(1)} %get-tuple-element.18), channel_id=1, source_target_pairs={{0,40},{8,48},{16,56},{24,64},{32,72},{40,80},{48,88},{56,96},{64,... | collective-permute-start | bytes 98312 | tf_op jit(solution)/shard_map/ppermute | solution.py:24
  40.4 5.5 %copy-start.3 = (f32[128]{0:T(128)S(1)}, f32[128]{0:T(128)}, u32[]{:S(2)}) copy-start(f32[128]{0:T(128)} %param.7) | copy-start | bytes 1540
  40.4 5.5 %collective-permute-start.11 = (f32[64,128]{1,0:T(8,128)S(1)}, f32[64,128]{1,0:T(8,128)S(1)}, u32[]{:S(2)}, u32[]{:S(2)}) collective-permute-start(f32[64,128]{1,0:T(8,128)S(1)} %get-tuple-element.19), channel_id=1, source_target_pairs={{0,24},{8,32},{16,40},{24,48},{32,56},{40,64},{48,72},{56,80},{64,... | collective-permute-start | bytes 98312 | tf_op jit(solution)/shard_map/ppermute | solution.py:24

commit v2 on v0

v2 whole, which is shorter than its diff:
```python
import jax
import jax.numpy as jnp
from jax import lax
from jax.experimental import pallas as pl
from jax.experimental.pallas import tpu as pltpu
from jax.sharding import PartitionSpec as P

F32 = jnp.float32
BF16 = jnp.bfloat16
ROOT_THREE = 3.0**0.5
POINT_SCALE = (5.0 / 3.0) ** 0.5
EXP2_SCALE = -ROOT_THREE * 1.4426950408889634
TINY = 1e-30
LANES = 128
CHUNK = 256
VMEM_BYTES = 32 * 1024 * 1024

STEPS = ((0, 2), (4, 1), (-3, -5), (7, 6))
PARTS = len(STEPS)


def moved(value, which, back):
    blocks, layers = lax.axis_size("blk"), lax.axis_size("layer")
    pairs = []
    for block in range(blocks):
        for layer in range(layers):
            step = STEPS[which][layer % 2]
            if step:
                source = block * layers + layer
                target = (block + step) % blocks * layers + layer
                pairs.append((target, source) if back else (source, target))
    return lax.ppermute(value, ("blk", "layer"), pairs)


def two_parts(x):
    high = x.astype(BF16)
    return high, (x - high.astype(F32)).astype(BF16)


def three_parts(x):
    high = x.astype(BF16)
    rest = x - high.astype(F32)
    middle = rest.astype(BF16)
    return high, middle, (rest - middle.astype(F32)).astype(BF16)


def side_by_side(*parts):
    return jnp.concatenate(parts, axis=1)


def stacked(*parts):
    return jnp.concatenate(parts, axis=0)


def across(left, right):
    return lax.dot_general(left, right, (((1,), (1,)), ((), ())), preferred_element_type=F32)


def local_call(
    body, outs, args, scratch=(), aliases=None, flops=0, moved_bytes=0,
    space=pltpu.VMEM,
):
    whole = pl.BlockSpec(memory_space=pltpu.VMEM)
    return pl.pallas_call(
        body,
        out_shape=tuple(jax.ShapeDtypeStruct(shape, kind) for shape, kind in outs),
        in_specs=[pl.BlockSpec(memory_space=space)] * len(args),
        out_specs=(whole,) * len(outs),
        scratch_shapes=list(scratch),
        input_output_aliases=aliases or {},
        compiler_params=pltpu.CompilerParams(vmem_limit_bytes=VMEM_BYTES),
        cost_estimate=pl.CostEstimate(flops=flops, bytes_accessed=moved_bytes, transcendentals=0),
    )(*(pltpu.with_memory_space_constraint(arg, space) for arg in args))


def prepare(points, inv, vectors_t, noise):
    rows, feats = points.shape
    columns = vectors_t.shape[0]
    part_rows = rows // PARTS

    def body(points_hbm, vectors_hbm, inv_hbm, noise_hbm, own_ref, x_ref, v_ref, term_ref, raw, inv_ref, noise_ref, sems):
        layer = lax.axis_index("layer")
        copies = [
            pltpu.make_async_copy(source, target, sems.at[which])
            for which, (source, target) in enumerate(
                ((points_hbm, raw), (inv_hbm, inv_ref), (vectors_hbm, v_ref), (noise_hbm, noise_ref))
            )
        ]
        for copy in copies:
            copy.start()
        copies[1].wait()
        inv_row = inv_ref[...] * POINT_SCALE
        copies[0].wait()
        start = pl.multiple_of(layer // 2 * part_rows, part_rows)
        own_ref[:part_rows, :] = raw[pl.ds(start, part_rows), :] * inv_row
        x_ref[...] = raw[...] * inv_row
        copies[2].wait()
        for half in range(part_rows // LANES):
            place = pl.multiple_of(start + half * LANES, LANES)
            own_ref[part_rows + half * columns : part_rows + (half + 1) * columns, :] = v_ref[
                :, pl.ds(place, LANES)
            ]
        copies[3].wait()
        place = pl.multiple_of(layer * LANES, LANES)
        term_ref[...] = v_ref[:, pl.ds(place, LANES)] * noise_ref[...]

    outs = (
        ((part_rows + part_rows // LANES * columns, feats), F32),
        ((rows, feats), F32),
        ((columns, rows), F32),
        ((columns, LANES), F32),
    )
    scratch = (
        pltpu.VMEM((rows, feats), F32),
        pltpu.VMEM((1, feats), F32),
        pltpu.VMEM((1, LANES), F32),
        pltpu.SemaphoreType.DMA((4,)),
    )
    return local_call(
        body, outs, (points, vectors_t, inv, noise), scratch, moved_bytes=2 << 20,
        space=pltpu.HBM,
    )


def load_right(held, columns):
    part_rows = 2 * LANES
    y = held[:part_rows]
    right_norms = jnp.sum((y * y).T, axis=0, keepdims=True)
    high, middle, low = three_parts(y)
    right = side_by_side(high, high, middle, middle, low, high)
    vectors = side_by_side(
        held[part_rows : part_rows + columns], held[part_rows + columns : part_rows + 2 * columns]
    )
    high, low = two_parts(vectors)
    right_vectors = side_by_side(stacked(high, low), stacked(high, jnp.zeros_like(high)))
    return right, right_norms, right_vectors


def tile(held, left, left_norms, left_vectors, total, add, mirrored_ref):
    rows = left.shape[0]
    columns = left_vectors.shape[0] // 2
    right, right_norms, right_vectors = load_right(held, columns)
    zero = jnp.zeros((columns, CHUNK), BF16)
    mirrored = jnp.zeros((2 * columns, 2 * LANES), F32)
    for chunk in range(rows // CHUNK):
        here = pl.ds(chunk * CHUNK, CHUNK)
        cross = across(left[here, :], right)
        norms = left_norms[here, :]
        square = jnp.maximum(cross + side_by_side(norms, norms) + right_norms, TINY)
        radius = square * lax.rsqrt(square)
        kernel = ((radius + ROOT_THREE) * radius + 1.0) * jnp.exp2(radius * EXP2_SCALE)
        high, low = two_parts(kernel)
        direct = across(side_by_side(high, low), right_vectors)
        if add:
            total[here, :] += direct
        else:
            total[here, :] = direct
        own = left_vectors[:columns, here]
        own_low = left_vectors[columns:, here]
        mirrored = mirrored + jnp.dot(
            stacked(side_by_side(own, own), side_by_side(own_low, zero)),
            stacked(high, low),
            preferred_element_type=F32,
        )
    mirrored = mirrored[:columns] + mirrored[columns:]
    mirrored_ref[:columns, :] = mirrored[:, :LANES]
    mirrored_ref[columns:, :] = mirrored[:, LANES:]


def tile_flops(rows, feats, columns):
    return 2 * rows * 2 * LANES * (6 * feats + 8 * columns)


def first_tile(x, vectors_t, own, piece):
    rows, feats = x.shape
    columns = vectors_t.shape[0]

    def body(x_ref, v_ref, own_ref, piece_ref, total, mirrored_ref, left, left_norms, left_vectors):
        x = x_ref[...]
        left_norms[...] = jnp.broadcast_to(jnp.sum(x * x, axis=1, keepdims=True), (rows, LANES))
        high, middle, low = three_parts(x * (-2.0))
        for place, part in enumerate((high, middle, high, middle, high, low)):
            left[:, place * feats : (place + 1) * feats] = part
        high, low = two_parts(v_ref[...])
        left_vectors[:columns, :] = high
        left_vectors[columns:, :] = low
        local = lax.axis_index("layer") % 2 == 0
        held = jnp.where(local, own_ref[...], piece_ref[...])
        tile(held, left, left_norms, left_vectors, total, False, mirrored_ref)

    outs = (
        ((rows, 2 * columns), F32),
        ((2 * columns, LANES), F32),
        ((rows, 6 * feats), BF16),
        ((rows, LANES), F32),
        ((2 * columns, rows), BF16),
    )
    return local_call(
        body, outs, (x, vectors_t, own, piece),
        flops=tile_flops(rows, feats, columns), moved_bytes=2 << 20,
    )


def next_tile(total, left, left_norms, left_vectors, piece, last):
    rows = left.shape[0]
    columns = left_vectors.shape[0] // 2
    feats = left.shape[1] // 6

    def plain(total_in, left, left_norms, left_vectors, piece_ref, total, mirrored_ref):
        tile(piece_ref[...], left, left_norms, left_vectors, total, True, mirrored_ref)

    def closing(total_in, left, left_norms, left_vectors, piece_ref, turned_ref, mirrored_ref, total):
        total[...] = total_in[...]
        tile(piece_ref[...], left, left_norms, left_vectors, total, True, mirrored_ref)
        for place in range(rows // LANES):
            turned = total[place * LANES : (place + 1) * LANES, :].T
            turned_ref[place, :, :] = turned[:columns] + turned[columns:]

    args = (total, left, left_norms, left_vectors, piece)
    cost = dict(flops=tile_flops(rows, feats, columns), moved_bytes=2 << 20)
    mirrored = ((2 * columns, LANES), F32)
    if last:
        outs = (((rows // LANES, columns, LANES), F32), mirrored)
        return local_call(closing, outs, args, (pltpu.VMEM((rows, 2 * columns), F32),), **cost)
    return local_call(plain, ((total.shape, F32), mirrored), args, aliases={0: 0}, **cost)


def joined(tiles, returned):
    columns = tiles.shape[1]

    def body(tiles_in, *refs):
        parts, tiles = refs[:-1], refs[-1]
        total = parts[0][...]
        for part in parts[1:]:
            total = total + part[...]
        tiles[...] = tiles_in[...]
        place = lax.axis_index("layer") // 2 * 2
        tiles[place, :, :] += total[:columns]
        tiles[place + 1, :, :] += total[columns:]

    return local_call(
        body, ((tiles.shape, F32),), (tiles, *returned), moved_bytes=1 << 19
    )[0]


def per_device(points, inv_scale, vectors, noise):
    layers = lax.axis_size("layer")
    rows = points.shape[0]
    own, x, vectors_t, noise_term = prepare(
        points, inv_scale[None, :], vectors.T, noise[None, :]
    )
    arrived = [moved(own, which, False) for which in range(PARTS)]
    total, back, left, left_norms, left_vectors = first_tile(x, vectors_t, own, arrived[0])
    returned = [moved(back, 0, True)]
    for which in range(1, PARTS):
        total, back = next_tile(
            total, left, left_norms, left_vectors, arrived[which], which == PARTS - 1
        )
        returned.append(moved(back, which, True))
    tiles = lax.all_to_all(joined(total, returned), "layer", 0, 0, tiled=True)
    normalizer = float(rows * (2 * layers - 1)) ** (-0.5)
    return (jnp.sum(tiles, axis=0) * normalizer + noise_term).T


def solution(mesh):
    placed = (P("blk", None), P(), P("blk", None), P(("blk", "layer")))
    return jax.shard_map(
        per_device, mesh=mesh, in_specs=placed, out_specs=P(("blk", "layer"), None), check_vma=False
    )
```

time: 108 us -> 51 us (0.47); the launches traced: 106 us -> 50.9 us
  waiting for transfers between devices: 39.3 us -> 10.9 us
  blocking collectives: 0 us -> 18.5 us
  matrix products: 17.3 us -> 0 us
  local copies, waits for them, and re-layouts: 17.3 us -> 0 us
  starting transfers between devices: 27.8 us -> 12.3 us
  Pallas kernels: 0 us -> 8.46 us
  other arithmetic: 3.91 us -> 0.64 us
    all_to_all x3 -> x0, waiting for transfers between devices: 23.7 us -> none  [the longest x1 14.4 us: per_device(): lax.all_to_all(outgoing, 'layer', split_axis=0, concat_axis=0, tiled=True)]
    all_to_all x0 -> x1, blocking collectives: none -> 18.5 us  [per_device(): tiles = lax.all_to_all(joined(total, returned), 'layer', 0, 0, tiled=True)]
    dot_general x6 -> x0, matrix products: 17.3 us -> none  [the longest x2 8.12 us: matern(): jnp.dot(left_scaled, right_scaled.T, precision=lax.Precision.HIGHEST, pre...]
    all_to_all x3 -> x0, starting transfers between devices: 14.3 us -> none  [the longest x1 7.46 us: per_device(): lax.all_to_all(outgoing, 'layer', split_axis=0, concat_axis=0, tiled=True)]
    pallas_call x0 -> x6, Pallas kernels: none -> 8.46 us  [local_call(): pl.pallas_call(body, out_shape=tuple((jax.ShapeDtypeStruct(shape, kind) f...]
    unnamed x15 -> x0, local copies, waits for them, and re-layouts: 7.51 us -> none
    dynamic_update_slice x4 -> x0, local copies, waits for them, and re-layouts: 7.13 us -> none  [per_device(): lax.scan(visit, jnp.zeros((block_rows, column_count), jnp.float32), (quer...]
    ppermute x14 -> x8, waiting for transfers between devices: 15.5 us -> 10.9 us  [moved(): return lax.ppermute(value, ('blk', 'layer'), pairs)]
  transfers between devices with their start and end apart: 17 -> 8, of which waited for: 11 -> 3; matrix products, arithmetic and copies ran while one was open for 7% -> 0% of each run, Pallas kernels for 0% -> 14%
where the time goes in v2:
time: 51 us; the launch traced here: 50.9 us
  blocking collectives  18.5 us (36%)
  starting transfers between devices  12.3 us (24%)
  waiting for transfers between devices  10.9 us (21%)
  Pallas kernels  8.46 us (17%)
  other arithmetic  0.64 us (1%)
    all_to_all x1, blocking collectives, per_device(): tiles = lax.all_to_all(joined(total, returned), 'layer', 0, 0, tiled=True)  18.5 us
    ppermute x8, starting transfers between devices, moved(): return lax.ppermute(value, ('blk', 'layer'), pairs)  12.3 us
    ppermute x8, waiting for transfers between devices, moved(): return lax.ppermute(value, ('blk', 'layer'), pairs)  10.9 us
    pallas_call x6, Pallas kernels, local_call(): pl.pallas_call(body, out_shape=tuple((jax.ShapeDtypeStruct(shape, kind) f...  8.46 us
  transfers between devices with their start and end apart: 8, of which 3 were waited for; matrix products, arithmetic and copies ran while one was open for 0% of the time, Pallas kernels for 14%

profile of v2, /device:TPU:0, one launch (start us, length us, event | category | flops | bytes accessed | tf_op | source)
XLA Modules:
  0.0 50.9 jit_solution(5442805602094503340)
XLA Ops:
  0.0 1.2 %shard_map.46 = (f32[384,128]{1,0:T(8,128)S(1)}, f32[1024,128]{1,0:T(8,128)S(1)}, f32[64,1024]{1,0:T(8,128)S(1)}, f32[64,128]{1,0:T(8,128)S(1)}) custom-call(f32[1024,128]{1,0:T(8,128)} %points_hbm.1, f32[64,1024]{1,0:T(8,128)} %bitcast.5, f32[1,128]{1,0:T(1,128)} %bitcast.6, f32[1,128]{1,0:T(1,128)} %bitcast.7), custom_call_target="tpu_custom_call" | custom-call | bytes 2097152 | tf_op jit(solution)/shard_map/pallas_call | solution.py:64
  1.2 0.7 %collective-permute-start = (f32[384,128]{1,0:T(8,128)S(1)}, f32[384,128]{1,0:T(8,128)S(1)}, u32[]{:S(2)}, u32[]{:S(2)}) collective-permute-start(f32[384,128]{1,0:T(8,128)S(1)} %get-tuple-element.22.own_ref), channel_id=1, source_target_pairs={{1,17},{3,19},{5,21},{7,23},{9,25},{11,27},{13,29},{15,31},{17,33}... | collective-permute-start | bytes 589832 | tf_op jit(solution)/shard_map/ppermute | solution.py:32
  1.9 3.3 %collective-permute-start.1 = (f32[384,128]{1,0:T(8,128)S(1)}, f32[384,128]{1,0:T(8,128)S(1)}, u32[]{:S(2)}, u32[]{:S(2)}) collective-permute-start(f32[384,128]{1,0:T(8,128)S(1)} %get-tuple-element.22.own_ref), channel_id=1, source_target_pairs={{0,32},{1,9},{2,34},{3,11},{4,36},{5,13},{6,38},{7,15},{8,40},{9,1... | collective-permute-start | bytes 589832 | tf_op jit(solution)/shard_map/ppermute | solution.py:32
  5.2 0.4 collective-permute-start.2
  5.7 1.1 %collective-permute-start.3 = (f32[384,128]{1,0:T(8,128)S(1)}, f32[384,128]{1,0:T(8,128)S(1)}, u32[]{:S(2)}, u32[]{:S(2)}) collective-permute-start(f32[384,128]{1,0:T(8,128)S(1)} %get-tuple-element.22.own_ref), channel_id=1, source_target_pairs={{0,56},{1,49},{2,58},{3,51},{4,60},{5,53},{6,62},{7,55},{8,64},{9,... | collective-permute-start | bytes 589832 | tf_op jit(solution)/shard_map/ppermute | solution.py:32
  6.8 0.0 collective-permute-done.piece_ref
  6.8 1.8 %shard_map.47 = (f32[1024,128]{1,0:T(8,128)S(1)}, f32[128,128]{1,0:T(8,128)S(1)}, bf16[1024,768]{1,0:T(8,128)(2,1)S(1)}, f32[1024,128]{1,0:T(8,128)S(1)}, bf16[128,1024]{1,0:T(8,128)(2,1)S(1)}) custom-call(f32[1024,128]{1,0:T(8,128)S(1)} %get-tuple-element.20.x_ref, f32[64,1024]{1,0:T(8,128)S(1)} %get-tuple-element.21.v_ref, ...), custom_call_target="tpu_custom_call" | custom-call | flops 671088640 | bytes 2097152 | tf_op jit(solution)/shard_map/pallas_call | solution.py:64
  8.6 0.7 %collective-permute-start.4 = (f32[128,128]{1,0:T(8,128)S(1)}, f32[128,128]{1,0:T(8,128)S(1)}, u32[]{:S(2)}, u32[]{:S(2)}) collective-permute-start(f32[128,128]{1,0:T(8,128)S(1)} %get-tuple-element.30), channel_id=1, source_target_pairs={{17,1},{19,3},{21,5},{23,7},{25,9},{27,11},{29,13},{31,15},{33,17}... | collective-permute-start | bytes 196616 | tf_op jit(solution)/shard_map/ppermute | solution.py:32
  9.3 2.4 %collective-permute-done.1.piece_ref = f32[384,128]{1,0:T(8,128)S(1)} collective-permute-done((f32[384,128]{1,0:T(8,128)S(1)}, f32[384,128]{1,0:T(8,128)S(1)}, u32[]{:S(2)}, u32[]{:S(2)}) %collective-permute-start.1) | collective-permute-done | bytes 196640 | tf_op jit(solution)/shard_map/ppermute | solution.py:32
  11.7 1.8 %shard_map.48 = (f32[1024,128]{1,0:T(8,128)S(1)}, f32[128,128]{1,0:T(8,128)S(1)}) custom-call(f32[1024,128]{1,0:T(8,128)S(1)} %get-tuple-element.23.total_in, bf16[1024,768]{1,0:T(8,128)(2,1)S(1)} %get-tuple-element.24.left, f32[1024,128]{1,0:T(8,128)S(1)} %get-tuple-element.25.left_norms, ...), custom_call_target="tpu_custom_call", output_to_operand_aliasing={{0}: (0, {})} | custom-call | flops 671088640 | bytes 2097152 | tf_op jit(solution)/shard_map/pallas_call | solution.py:64
  13.5 4.8 %collective-permute-start.5 = (f32[128,128]{1,0:T(8,128)S(1)}, f32[128,128]{1,0:T(8,128)S(1)}, u32[]{:S(2)}, u32[]{:S(2)}) collective-permute-start(f32[128,128]{1,0:T(8,128)S(1)} %get-tuple-element.31), channel_id=1, source_target_pairs={{32,0},{9,1},{34,2},{11,3},{36,4},{13,5},{38,6},{15,7},{40,8},{17,... | collective-permute-start | bytes 196616 | tf_op jit(solution)/shard_map/ppermute | solution.py:32
  18.3 0.0 collective-permute-done.2.piece_ref
  18.3 1.8 %shard_map.49 = (f32[1024,128]{1,0:T(8,128)S(1)}, f32[128,128]{1,0:T(8,128)S(1)}) custom-call(f32[1024,128]{1,0:T(8,128)S(1)} %get-tuple-element.27.total_in, bf16[1024,768]{1,0:T(8,128)(2,1)S(1)} %get-tuple-element.24.left, f32[1024,128]{1,0:T(8,128)S(1)} %get-tuple-element.25.left_norms, ...), custom_call_target="tpu_custom_call", output_to_operand_aliasing={{0}: (0, {})} | custom-call | flops 671088640 | bytes 2097152 | tf_op jit(solution)/shard_map/pallas_call | solution.py:64
  20.1 0.9 %collective-permute-start.6 = (f32[128,128]{1,0:T(8,128)S(1)}, f32[128,128]{1,0:T(8,128)S(1)}, u32[]{:S(2)}, u32[]{:S(2)}) collective-permute-start(f32[128,128]{1,0:T(8,128)S(1)} %get-tuple-element.32), channel_id=1, source_target_pairs={{104,0},{89,1},{106,2},{91,3},{108,4},{93,5},{110,6},{95,7},{112,8... | collective-permute-start | bytes 196616 | tf_op jit(solution)/shard_map/ppermute | solution.py:32
  21.0 0.0 collective-permute-done.3.piece_ref
  21.0 1.8 %shard_map.50 = (f32[8,64,128]{2,1,0:T(8,128)S(1)}, f32[128,128]{1,0:T(8,128)S(1)}) custom-call(f32[1024,128]{1,0:T(8,128)S(1)} %get-tuple-element.28.total_in, bf16[1024,768]{1,0:T(8,128)(2,1)S(1)} %get-tuple-element.24.left, f32[1024,128]{1,0:T(8,128)S(1)} %get-tuple-element.25.left_norms, bf16[128,1024]{1,0:T(8,128)(2,1)S(1)} %get-tuple-element.26.left_vectors, ...), custom_call_target="tpu_custom_call" | custom-call | flops 671088640 | bytes 2097152 | tf_op jit(solution)/shard_map/pallas_call | solution.py:64
  22.8 0.3 collective-permute-start.7
  23.2 0.0 collective-permute-done.4.refs_0_
  23.2 0.0 collective-permute-done.5.refs_1_
  23.2 3.6 %collective-permute-done.6.refs_2_ = f32[128,128]{1,0:T(8,128)S(1)} collective-permute-done((f32[128,128]{1,0:T(8,128)S(1)}, f32[128,128]{1,0:T(8,128)S(1)}, u32[]{:S(2)}, u32[]{:S(2)}) %collective-permute-start.6) | collective-permute-done | bytes 65568 | tf_op jit(solution)/shard_map/ppermute | solution.py:32
  26.8 4.9 %collective-permute-done.7.refs_3_ = f32[128,128]{1,0:T(8,128)S(1)} collective-permute-done((f32[128,128]{1,0:T(8,128)S(1)}, f32[128,128]{1,0:T(8,128)S(1)}, u32[]{:S(2)}, u32[]{:S(2)}) %collective-permute-start.7) | collective-permute-done | bytes 65568 | tf_op jit(solution)/shard_map/ppermute | solution.py:32
  31.7 18.5 %all_to_all.5 = f32[8,64,128]{2,1,0:T(8,128)S(1)} all-to-all(f32[8,64,128]{2,1,0:T(8,128)S(1)} %shard_map.51), channel_id=1, replica_groups=mesh['blk'=16,'layer'=8] {'layer'}, dimensions={0} | all-to-all | bytes 524288 | tf_op jit(solution)/shard_map/all_to_all | solution.py:260
  50.2 0.6 %add_bitcast_fusion = f32[128,64]{0,1:T(8,128)} fusion(f32[64,128]{1,0:T(8,128)S(1)} %get-tuple-element.34, f32[64,128]{1,0:T(8,128)S(1)} %reduce_sum.9), kind=kLoop, calls=%fused_computation | loop fusion | flops 16384 | bytes 98304 | tf_op jit(solution)/shard_map/transpose | solution.py:262
  (2 shorter events, 0.1 us)
Async XLA Ops:
  1.2 5.6 %collective-permute-start = (f32[384,128]{1,0:T(8,128)S(1)}, f32[384,128]{1,0:T(8,128)S(1)}, u32[]{:S(2)}, u32[]{:S(2)}) collective-permute-start(f32[384,128]{1,0:T(8,128)S(1)} %get-tuple-element.22.own_ref), channel_id=1, source_target_pairs={{1,17},{3,19},{5,21},{7,23},{9,25},{11,27},{13,29},{15,31},{17,33}... | collective-permute-start | bytes 589832 | tf_op jit(solution)/shard_map/ppermute | solution.py:32
  1.9 9.8 %collective-permute-start.1 = (f32[384,128]{1,0:T(8,128)S(1)}, f32[384,128]{1,0:T(8,128)S(1)}, u32[]{:S(2)}, u32[]{:S(2)}) collective-permute-start(f32[384,128]{1,0:T(8,128)S(1)} %get-tuple-element.22.own_ref), channel_id=1, source_target_pairs={{0,32},{1,9},{2,34},{3,11},{4,36},{5,13},{6,38},{7,15},{8,40},{9,1... | collective-permute-start | bytes 589832 | tf_op jit(solution)/shard_map/ppermute | solution.py:32
  5.2 13.1 %collective-permute-start.2 = (f32[384,128]{1,0:T(8,128)S(1)}, f32[384,128]{1,0:T(8,128)S(1)}, u32[]{:S(2)}, u32[]{:S(2)}) collective-permute-start(f32[384,128]{1,0:T(8,128)S(1)} %get-tuple-element.22.own_ref), channel_id=1, source_target_pairs={{0,104},{1,89},{2,106},{3,91},{4,108},{5,93},{6,110},{7,95},{8,112... | collective-permute-start | bytes 589832 | tf_op jit(solution)/shard_map/ppermute | solution.py:32
  5.7 15.4 %collective-permute-start.3 = (f32[384,128]{1,0:T(8,128)S(1)}, f32[384,128]{1,0:T(8,128)S(1)}, u32[]{:S(2)}, u32[]{:S(2)}) collective-permute-start(f32[384,128]{1,0:T(8,128)S(1)} %get-tuple-element.22.own_ref), channel_id=1, source_target_pairs={{0,56},{1,49},{2,58},{3,51},{4,60},{5,53},{6,62},{7,55},{8,64},{9,... | collective-permute-start | bytes 589832 | tf_op jit(solution)/shard_map/ppermute | solution.py:32
  8.6 14.5 %collective-permute-start.4 = (f32[128,128]{1,0:T(8,128)S(1)}, f32[128,128]{1,0:T(8,128)S(1)}, u32[]{:S(2)}, u32[]{:S(2)}) collective-permute-start(f32[128,128]{1,0:T(8,128)S(1)} %get-tuple-element.30), channel_id=1, source_target_pairs={{17,1},{19,3},{21,5},{23,7},{25,9},{27,11},{29,13},{31,15},{33,17}... | collective-permute-start | bytes 196616 | tf_op jit(solution)/shard_map/ppermute | solution.py:32
  13.5 9.7 %collective-permute-start.5 = (f32[128,128]{1,0:T(8,128)S(1)}, f32[128,128]{1,0:T(8,128)S(1)}, u32[]{:S(2)}, u32[]{:S(2)}) collective-permute-start(f32[128,128]{1,0:T(8,128)S(1)} %get-tuple-element.31), channel_id=1, source_target_pairs={{32,0},{9,1},{34,2},{11,3},{36,4},{13,5},{38,6},{15,7},{40,8},{17,... | collective-permute-start | bytes 196616 | tf_op jit(solution)/shard_map/ppermute | solution.py:32
  20.1 6.7 %collective-permute-start.6 = (f32[128,128]{1,0:T(8,128)S(1)}, f32[128,128]{1,0:T(8,128)S(1)}, u32[]{:S(2)}, u32[]{:S(2)}) collective-permute-start(f32[128,128]{1,0:T(8,128)S(1)} %get-tuple-element.32), channel_id=1, source_target_pairs={{104,0},{89,1},{106,2},{91,3},{108,4},{93,5},{110,6},{95,7},{112,8... | collective-permute-start | bytes 196616 | tf_op jit(solution)/shard_map/ppermute | solution.py:32
  22.8 8.8 %collective-permute-start.7 = (f32[128,128]{1,0:T(8,128)S(1)}, f32[128,128]{1,0:T(8,128)S(1)}, u32[]{:S(2)}, u32[]{:S(2)}) collective-permute-start(f32[128,128]{1,0:T(8,128)S(1)} %get-tuple-element.33), channel_id=1, source_target_pairs={{56,0},{49,1},{58,2},{51,3},{60,4},{53,5},{62,6},{55,7},{64,8},{57... | collective-permute-start | bytes 196616 | tf_op jit(solution)/shard_map/ppermute | solution.py:32

commit v3 on v2

v3 whole, which is shorter than its diff:
```python
import jax
import jax.numpy as jnp
from jax import lax
from jax.experimental import pallas as pl
from jax.experimental.pallas import tpu as pltpu
from jax.sharding import PartitionSpec as P

F32 = jnp.float32
BF16 = jnp.bfloat16
ROOT_THREE = 3.0**0.5
POINT_SCALE = (5.0 / 3.0) ** 0.5
EXP2_SCALE = -ROOT_THREE * 1.4426950408889634
TINY = 1e-30
LANES = 128
CHUNK = 256
VMEM_BYTES = 32 * 1024 * 1024

CHIP_STEPS = (-1, -2, 3)


def permuted(value, target_of):
    count = lax.axis_size("blk")
    pairs = [(block, target_of(block) % count) for block in range(count)]
    return lax.ppermute(value, "blk", pairs)


def swapped(value):
    return permuted(value, lambda block: block ^ 1)


def stepped(value, chips):
    return permuted(value, lambda block: block + 2 * chips)


def across_the_ring(value):
    count = lax.axis_size("blk")
    pairs = [(block, (block + count // 2) % count) for block in range(0, count, 2)]
    return lax.ppermute(value, "blk", pairs)


def two_parts(x):
    high = x.astype(BF16)
    return high, (x - high.astype(F32)).astype(BF16)


def three_parts(x):
    high = x.astype(BF16)
    rest = x - high.astype(F32)
    middle = rest.astype(BF16)
    return high, middle, (rest - middle.astype(F32)).astype(BF16)


def side_by_side(*parts):
    return jnp.concatenate(parts, axis=1)


def stacked(*parts):
    return jnp.concatenate(parts, axis=0)


def across(left, right):
    return lax.dot_general(left, right, (((1,), (1,)), ((), ())), preferred_element_type=F32)


def local_call(body, outs, args, scratch=(), aliases=None, macs=0, space=pltpu.VMEM):
    whole = pl.BlockSpec(memory_space=pltpu.VMEM)
    return pl.pallas_call(
        body,
        out_shape=tuple(jax.ShapeDtypeStruct(shape, kind) for shape, kind in outs),
        in_specs=[pl.BlockSpec(memory_space=space)] * len(args),
        out_specs=(whole,) * len(outs),
        scratch_shapes=list(scratch),
        input_output_aliases=aliases or {},
        compiler_params=pltpu.CompilerParams(vmem_limit_bytes=VMEM_BYTES),
        cost_estimate=pl.CostEstimate(flops=2 * macs, bytes_accessed=1 << 20, transcendentals=0),
    )(*(pltpu.with_memory_space_constraint(arg, space) for arg in args))


def prepare(points, inv, vectors_t, noise):
    rows, feats = points.shape
    columns = vectors_t.shape[0]
    tiles = rows // LANES

    def body(
        points_hbm, vectors_hbm, inv_hbm, noise_hbm, packed_ref, piece_ref, term_ref,
        raw, raw_vectors, inv_ref, noise_ref, sems,
    ):
        layer = lax.axis_index("layer")
        copies = [
            pltpu.make_async_copy(source, target, sems.at[which])
            for which, (source, target) in enumerate(
                (
                    (points_hbm, raw),
                    (inv_hbm, inv_ref),
                    (vectors_hbm, raw_vectors),
                    (noise_hbm, noise_ref),
                )
            )
        ]
        for copy in copies:
            copy.start()
        copies[1].wait()
        inv_row = inv_ref[...] * POINT_SCALE
        copies[0].wait()
        start = pl.multiple_of(layer * LANES, LANES)
        piece_ref[:LANES, :] = raw[pl.ds(start, LANES), :] * inv_row
        packed_ref[:rows, :] = raw[...] * inv_row
        copies[2].wait()
        for tile in range(tiles):
            packed_ref[rows + tile * columns : rows + (tile + 1) * columns, :] = raw_vectors[
                :, tile * LANES : (tile + 1) * LANES
            ]
        own_vectors = raw_vectors[:, pl.ds(start, LANES)]
        piece_ref[LANES:, :] = own_vectors
        copies[3].wait()
        term_ref[...] = own_vectors * noise_ref[...]

    outs = (
        ((rows + tiles * columns, feats), F32),
        ((LANES + columns, feats), F32),
        ((columns, LANES), F32),
    )
    scratch = (
        pltpu.VMEM((rows, feats), F32),
        pltpu.VMEM((columns, rows), F32),
        pltpu.VMEM((1, feats), F32),
        pltpu.VMEM((1, LANES), F32),
        pltpu.SemaphoreType.DMA((4,)),
    )
    return local_call(body, outs, (points, vectors_t, inv, noise), scratch, space=pltpu.HBM)


def load_left(packed, left, left_norms, left_vectors):
    rows = left.shape[0]
    columns = left_vectors.shape[0] // 2
    x = packed[:rows, :]
    left_norms[...] = jnp.broadcast_to(jnp.sum(x * x, axis=1, keepdims=True), (rows, LANES))
    high, middle, low = three_parts(x * (-2.0))
    feats = x.shape[1]
    for place, part in enumerate((high, middle, high, middle, high, low)):
        left[:, place * feats : (place + 1) * feats] = part
    for tile in range(rows // LANES):
        high, low = two_parts(packed[rows + tile * columns : rows + (tile + 1) * columns, :])
        left_vectors[:columns, tile * LANES : (tile + 1) * LANES] = high
        left_vectors[columns:, tile * LANES : (tile + 1) * LANES] = low


def load_right(pieces):
    held = [piece[...] for piece in pieces]
    y = stacked(*(piece[:LANES] for piece in held))
    right_norms = jnp.sum((y * y).T, axis=0, keepdims=True)
    high, middle, low = three_parts(y)
    right = side_by_side(high, high, middle, middle, low, high)
    high, low = two_parts(side_by_side(*(piece[LANES:] for piece in held)))
    right_vectors = side_by_side(stacked(high, low), stacked(high, jnp.zeros_like(high)))
    return right, right_norms, right_vectors


def tile_products(side, loaded, total_in, total, mirrored):
    left, left_norms, left_vectors = side
    right, right_norms, right_vectors = loaded
    rows = left.shape[0]
    columns = left_vectors.shape[0] // 2
    count = right.shape[0] // LANES
    zero = jnp.zeros((columns, CHUNK), BF16)
    for chunk in range(rows // CHUNK):
        here = pl.ds(chunk * CHUNK, CHUNK)
        cross = across(left[here, :], right)
        norms = left_norms[here, :]
        square = jnp.maximum(cross + side_by_side(*(norms,) * count) + right_norms, TINY)
        radius = square * lax.rsqrt(square)
        kernel = ((radius + ROOT_THREE) * radius + 1.0) * jnp.exp2(radius * EXP2_SCALE)
        high, low = two_parts(kernel)
        direct = across(side_by_side(high, low), right_vectors)
        total[here, :] = direct if total_in is None else total_in[here, :] + direct
        own = left_vectors[:columns, here]
        own_low = left_vectors[columns:, here]
        part = jnp.dot(
            stacked(side_by_side(own, own), side_by_side(own_low, zero)),
            stacked(high, low),
            preferred_element_type=F32,
        )
        mirrored = part if mirrored is None else mirrored + part
    return mirrored


def folded(mirrored):
    columns = mirrored.shape[0] // 2
    return mirrored[:columns] + mirrored[columns:]


def write_turned(total, turned_ref):
    columns = total.shape[1] // 2
    for place in range(turned_ref.shape[0]):
        turned = total[place * LANES : (place + 1) * LANES, :].T
        turned_ref[place, :, :] = turned[:columns] + turned[columns:]


def macs_of(rows, feats, columns, count):
    return rows * count * LANES * (6 * feats + 8 * columns)


def early_tiles(packed, other_packed, piece, arrived):
    feats = packed.shape[1]
    columns = piece.shape[0] - LANES
    rows = packed.shape[0] * LANES // (LANES + columns)

    def body(
        packed, other_packed, piece, arrived,
        total, left, norms, vectors, other_total, other_left, other_norms, other_vectors, back_ref,
    ):
        load_left(packed, left, norms, vectors)
        load_left(other_packed, other_left, other_norms, other_vectors)
        loaded = load_right((piece, arrived))
        mirrored = tile_products((left, norms, vectors), loaded, None, total, None)
        other = (other_left, other_norms, other_vectors)
        mirrored = tile_products(other, loaded, None, other_total, mirrored)
        back_ref[...] = folded(mirrored)[:, LANES:]

    side = (
        ((rows, 2 * columns), F32),
        ((rows, 6 * feats), BF16),
        ((rows, LANES), F32),
        ((2 * columns, rows), BF16),
    )
    outs = side + side + (((columns, LANES), F32),)
    args = (packed, other_packed, piece, arrived)
    out = local_call(body, outs, args, macs=macs_of(2 * rows, feats, columns, 2))
    return out[:4], out[4:8], out[8]


def other_tiles(side, pieces):
    total, left, norms, vectors = side
    rows, columns = left.shape[0], vectors.shape[0] // 2

    def body(total_in, left, norms, vectors, *refs):
        arrived, turned_ref, shared_ref, back_ref, total = refs[:3], *refs[3:]
        loaded = load_right(arrived)
        mirrored = tile_products((left, norms, vectors), loaded, total_in, total, None)
        shared_ref[...] = mirrored[:, : 2 * LANES]
        back_ref[...] = folded(mirrored[:, 2 * LANES :])
        write_turned(total, turned_ref)

    outs = (
        ((rows // LANES, columns, LANES), F32),
        ((2 * columns, 2 * LANES), F32),
        ((columns, LANES), F32),
    )
    scratch = (pltpu.VMEM((rows, 2 * columns), F32),)
    macs = macs_of(rows, left.shape[1] // 6, columns, 3)
    return local_call(body, outs, (total, left, norms, vectors, *pieces), scratch, macs=macs)


def own_tiles(side, shared, pieces):
    total, left, norms, vectors = side
    rows, columns = left.shape[0], vectors.shape[0] // 2

    def body(total_in, left, norms, vectors, shared_ref, *refs):
        arrived, turned_ref, first_ref, second_ref, total = refs[:2], *refs[2:]
        loaded = load_right(arrived)
        mirrored = tile_products((left, norms, vectors), loaded, total_in, total, shared_ref[...])
        mirrored = folded(mirrored)
        first_ref[...] = mirrored[:, :LANES]
        second_ref[...] = mirrored[:, LANES:]
        write_turned(total, turned_ref)

    back = ((columns, LANES), F32)
    outs = (((rows // LANES, columns, LANES), F32), back, back)
    scratch = (pltpu.VMEM((rows, 2 * columns), F32),)
    macs = macs_of(rows, left.shape[1] // 6, columns, 2)
    return local_call(body, outs, (total, left, norms, vectors, shared, *pieces), scratch, macs=macs)


def per_device(points, inv_scale, vectors, noise):
    layers = lax.axis_size("layer")
    rows = points.shape[0]
    packed, piece, noise_term = prepare(points, inv_scale[None, :], vectors.T, noise[None, :])
    near, middle, far = CHIP_STEPS
    near_piece = stepped(piece, near)
    other_packed = swapped(packed)
    middle_piece = stepped(piece, middle)
    far_piece = stepped(piece, far)
    ring_piece = across_the_ring(piece)
    own, other, near_back = early_tiles(packed, other_packed, piece, near_piece)
    near_back = stepped(near_back, -near)
    for_other, shared, ring_back = other_tiles(other, (middle_piece, far_piece, ring_piece))
    from_other = swapped(for_other)
    direct, middle_back, far_back = own_tiles(own, shared, (middle_piece, far_piece))
    tiles = lax.all_to_all(direct + from_other, "layer", 0, 0, tiled=True)
    returned = (
        near_back
        + across_the_ring(ring_back)
        + stepped(middle_back, -middle)
        + stepped(far_back, -far)
    )
    normalizer = float(rows * (2 * layers - 1)) ** (-0.5)
    return ((jnp.sum(tiles, axis=0) + returned) * normalizer + noise_term).T


def solution(mesh):
    placed = (P("blk", None), P(), P("blk", None), P(("blk", "layer")))
    return jax.shard_map(
        per_device, mesh=mesh, in_specs=placed, out_specs=P(("blk", "layer"), None), check_vma=False
    )
```

time: 51 us -> 38.4 us (0.75)
  the two profiles are of different devices: /device:TPU:0 before, /device:TPU:30 now
where the time goes in v3:
time: 38.4 us; the launch traced here: 38.1 us
  starting transfers between devices  24.5 us (64%)
  Pallas kernels  7.81 us (20%)
  waiting for transfers between devices  4.27 us (11%)
  other arithmetic  1.37 us (4%)
    ppermute x8, starting transfers between devices, permuted(): return lax.ppermute(value, 'blk', pairs)  10.8 us
    all_to_all x1, starting transfers between devices, per_device(): tiles = lax.all_to_all(direct + from_other, 'layer', 0, 0, tiled=True)  8.28 us
    pallas_call x4, Pallas kernels, local_call(): pl.pallas_call(body, out_shape=tuple((jax.ShapeDtypeStruct(shape, kind) f...  7.81 us
    ppermute x2, starting transfers between devices, across_the_ring(): return lax.ppermute(value, 'blk', pairs)  5.43 us
    ppermute x2, waiting for transfers between devices, across_the_ring(): return lax.ppermute(value, 'blk', pairs)  3.01 us
    ppermute x8, waiting for transfers between devices, permuted(): return lax.ppermute(value, 'blk', pairs)  1.26 us
  transfers between devices with their start and end apart: 11, of which 3 were waited for; matrix products, arithmetic and copies ran while one was open for 0% of the time, Pallas kernels for 11%

profile of v3, /device:TPU:30, one launch (start us, length us, event | category | flops | bytes accessed | tf_op | source)
XLA Modules:
  0.0 38.1 jit_solution(5114120754260241403)
XLA Ops:
  0.0 1.2 %shard_map.46 = (f32[1536,128]{1,0:T(8,128)S(1)}, f32[192,128]{1,0:T(8,128)S(1)}, f32[64,128]{1,0:T(8,128)S(1)}) custom-call(f32[1024,128]{1,0:T(8,128)} %points_hbm.1, f32[64,1024]{1,0:T(8,128)} %bitcast.5, f32[1,128]{1,0:T(1,128)} %bitcast.6, f32[1,128]{1,0:T(1,128)} %bitcast.7), custom_call_target="tpu_custom_call" | custom-call | bytes 1048576 | tf_op jit(solution)/shard_map/pallas_call | solution.py:67
  1.2 0.1 collective-permute-start
  1.3 0.8 %collective-permute-start.1 = (f32[192,128]{1,0:T(8,128)S(1)}, f32[192,128]{1,0:T(8,128)S(1)}, u32[]{:S(2)}, u32[]{:S(2)}) collective-permute-start(f32[192,128]{1,0:T(8,128)S(1)} %get-tuple-element.24.piece), channel_id=1, source_target_pairs={{0,112},{8,120},{16,0},{24,8},{32,16},{40,24},{48,32},{56,40},{64,... | collective-permute-start | bytes 294920 | tf_op jit(solution)/shard_map/ppermute | solution.py:24
  2.1 0.9 %collective-permute-start.2 = (f32[192,128]{1,0:T(8,128)S(1)}, f32[192,128]{1,0:T(8,128)S(1)}, u32[]{:S(2)}, u32[]{:S(2)}) collective-permute-start(f32[192,128]{1,0:T(8,128)S(1)} %get-tuple-element.24.piece), channel_id=1, source_target_pairs={{0,96},{8,104},{16,112},{24,120},{32,0},{40,8},{48,16},{56,24},{64... | collective-permute-start | bytes 294920 | tf_op jit(solution)/shard_map/ppermute | solution.py:24
  3.0 3.3 %collective-permute-start.3 = (f32[192,128]{1,0:T(8,128)S(1)}, f32[192,128]{1,0:T(8,128)S(1)}, u32[]{:S(2)}, u32[]{:S(2)}) collective-permute-start(f32[192,128]{1,0:T(8,128)S(1)} %get-tuple-element.24.piece), channel_id=1, source_target_pairs={{0,48},{8,56},{16,64},{24,72},{32,80},{40,88},{48,96},{56,104},{64... | collective-permute-start | bytes 294920 | tf_op jit(solution)/shard_map/ppermute | solution.py:24
  6.3 2.7 %collective-permute-start.4 = (f32[192,128]{1,0:T(8,128)S(1)}, f32[192,128]{1,0:T(8,128)S(1)}, u32[]{:S(2)}, u32[]{:S(2)}) collective-permute-start(f32[192,128]{1,0:T(8,128)S(1)} %get-tuple-element.24.piece), channel_id=1, source_target_pairs={{0,64},{16,80},{32,96},{48,112},{64,0},{80,16},{96,32},{112,48},{1... | collective-permute-start | bytes 294920 | tf_op jit(solution)/shard_map/ppermute | solution.py:38
  9.1 1.1 %collective-permute-done.1.arrived = f32[192,128]{1,0:T(8,128)S(1)} collective-permute-done((f32[192,128]{1,0:T(8,128)S(1)}, f32[192,128]{1,0:T(8,128)S(1)}, u32[]{:S(2)}, u32[]{:S(2)}) %collective-permute-start.1) | collective-permute-done | bytes 98336 | tf_op jit(solution)/shard_map/ppermute | solution.py:24
  10.2 0.0 collective-permute-done.other_packed
  10.2 2.9 %shard_map.47 = (f32[1024,128]{1,0:T(8,128)S(1)}, bf16[1024,768]{1,0:T(8,128)(2,1)S(1)}, f32[1024,128]{1,0:T(8,128)S(1)}, bf16[128,1024]{1,0:T(8,128)(2,1)S(1)},...) custom-call(f32[1536,128]{1,0:T(8,128)S(1)} %get-tuple-element.23.pa, ...), custom_call_target="tpu_custom_call" | custom-call | flops 1342177280 | bytes 1048576 | tf_op jit(solution)/shard_map/pallas_call | solution.py:67
  13.0 0.0 collective-permute-done.2.refs_0_
  13.1 0.0 collective-permute-done.3.refs_1_
  13.1 0.0 collective-permute-done.4.refs_2_
  13.1 2.4 %shard_map.48 = (f32[8,64,128]{2,1,0:T(8,128)S(1)}, f32[128,256]{1,0:T(8,128)S(1)}, f32[64,128]{1,0:T(8,128)S(1)}) custom-call(f32[1024,128]{1,0:T(8,128)S(1)} %get-tuple-element.29.total_in, bf16[1024,768]{1,0:T(8,128)(2,1)S(1)} %get-tuple-element.30.left, f32[1024,128]{1,0:T(8,128)S(1)} %get-tuple-element.31.norms, ...), custom_call_target="tpu_custom_call" | custom-call | flops 1006632960 | bytes 1048576 | tf_op jit(solution)/shard_map/pallas_call | solution.py:67
  15.5 0.1 collective-permute-start.5
  15.6 1.4 %shard_map.49 = (f32[8,64,128]{2,1,0:T(8,128)S(1)}, f32[64,128]{1,0:T(8,128)S(1)}, f32[64,128]{1,0:T(8,128)S(1)}) custom-call(f32[1024,128]{1,0:T(8,128)S(1)} %get-tuple-element.25.total_in, bf16[1024,768]{1,0:T(8,128)(2,1)S(1)} %get-tuple-element.26.left, f32[1024,128]{1,0:T(8,128)S(1)} %get-tuple-element.27.norms, ...), custom_call_target="tpu_custom_call" | custom-call | flops 671088640 | bytes 1048576 | tf_op jit(solution)/shard_map/pallas_call | solution.py:67
  16.9 0.2 collective-permute-done.5
  17.1 0.7 %add.18 = f32[8,64,128]{2,1,0:T(8,128)} add(f32[8,64,128]{2,1,0:T(8,128)S(1)} %get-tuple-element.34, f32[8,64,128]{2,1,0:T(8,128)S(1)} %collective-permute-done.5) | non-fusion elementwise | flops 65536 | bytes 786432 | tf_op jit(solution)/shard_map/add | solution.py:289
  17.8 8.3 %all-to-all-start = ((f32[8,64,128]{2,1,0:T(8,128)}), f32[8,64,128]{2,1,0:T(8,128)S(1)}, u32[]{:S(2)}, u32[]{:S(2)}) async-start(f32[8,64,128]{2,1,0:T(8,128)} %add.18), calls=%async_computation | async-start | bytes 524288 | tf_op jit(solution)/shard_map/all_to_all | solution.py:289
  26.1 0.0 collective-permute-start.9
  26.1 2.9 %collective-permute-start.8 = (f32[64,128]{1,0:T(8,128)S(1)}, f32[64,128]{1,0:T(8,128)S(1)}, u32[]{:S(2)}, u32[]{:S(2)}) collective-permute-start(f32[64,128]{1,0:T(8,128)S(1)} %get-tuple-element.38), channel_id=1, source_target_pairs={{0,32},{8,40},{16,48},{24,56},{32,64},{40,72},{48,80},{56,88},{64,... | collective-permute-start | bytes 98312 | tf_op jit(solution)/shard_map/ppermute | solution.py:24
  29.0 2.7 %collective-permute-start.6 = (f32[64,128]{1,0:T(8,128)S(1)}, f32[64,128]{1,0:T(8,128)S(1)}, u32[]{:S(2)}, u32[]{:S(2)}) collective-permute-start(f32[64,128]{1,0:T(8,128)S(1)} %get-tuple-element.36), channel_id=1, source_target_pairs={{0,16},{8,24},{16,32},{24,40},{32,48},{40,56},{48,64},{56,72},{64,... | collective-permute-start | bytes 98312 | tf_op jit(solution)/shard_map/ppermute | solution.py:24
  31.7 2.7 %collective-permute-start.7 = (f32[64,128]{1,0:T(8,128)S(1)}, f32[64,128]{1,0:T(8,128)S(1)}, u32[]{:S(2)}, u32[]{:S(2)}) collective-permute-start(f32[64,128]{1,0:T(8,128)S(1)} %get-tuple-element.37), channel_id=1, source_target_pairs={{0,64},{16,80},{32,96},{48,112},{64,0},{80,16},{96,32},{112,48},{1... | collective-permute-start | bytes 98312 | tf_op jit(solution)/shard_map/ppermute | solution.py:38
  34.4 0.0 all-to-all-done
  34.5 0.0 collective-permute-done.9
  34.5 0.0 collective-permute-done.8
  34.5 0.0 collective-permute-done.6
  34.5 3.0 %collective-permute-done.7 = f32[64,128]{1,0:T(8,128)S(1)} collective-permute-done((f32[64,128]{1,0:T(8,128)S(1)}, f32[64,128]{1,0:T(8,128)S(1)}, u32[]{:S(2)}, u32[]{:S(2)}) %collective-permute-start.7) | collective-permute-done | bytes 32800 | tf_op jit(solution)/shard_map/ppermute | solution.py:38
  37.5 0.6 %add_bitcast_fusion = f32[128,64]{0,1:T(8,128)} fusion(f32[64,128]{1,0:T(8,128)S(1)} %get-tuple-element.40, f32[64,128]{1,0:T(8,128)S(1)} %reduce_sum.9, f32[64,128]{1,0:T(8,128)S(1)} %collective-permute-done.9, f32[64,128]{1,0:T(8,128)S(1)} %collective-permute-done.8, f32[64,128]{1,0:T(8,128)S(1)} %collective-permute-done.6, ...), kind=kLoop, calls=%fused_computation | loop fusion | flops 49152 | bytes 229376 | tf_op jit(solution)/shard_map/transpose | solution.py:297
  (1 shorter events, 0.0 us)
Async XLA Ops:
  1.2 9.0 %collective-permute-start = (f32[1536,128]{1,0:T(8,128)S(1)}, f32[1536,128]{1,0:T(8,128)S(1)}, u32[]{:S(2)}, u32[]{:S(2)}) collective-permute-start(f32[1536,128]{1,0:T(8,128)S(1)} %get-tuple-element.23.packed), channel_id=1, source_target_pairs={{0,8},{8,0},{16,24},{24,16},{32,40},{40,32},{48,56},{56,48},{64,72... | collective-permute-start | bytes 2359304 | tf_op jit(solution)/shard_map/ppermute | solution.py:24
  1.3 8.9 %collective-permute-start.1 = (f32[192,128]{1,0:T(8,128)S(1)}, f32[192,128]{1,0:T(8,128)S(1)}, u32[]{:S(2)}, u32[]{:S(2)}) collective-permute-start(f32[192,128]{1,0:T(8,128)S(1)} %get-tuple-element.24.piece), channel_id=1, source_target_pairs={{0,112},{8,120},{16,0},{24,8},{32,16},{40,24},{48,32},{56,40},{64,... | collective-permute-start | bytes 294920 | tf_op jit(solution)/shard_map/ppermute | solution.py:24
  2.1 11.0 %collective-permute-start.2 = (f32[192,128]{1,0:T(8,128)S(1)}, f32[192,128]{1,0:T(8,128)S(1)}, u32[]{:S(2)}, u32[]{:S(2)}) collective-permute-start(f32[192,128]{1,0:T(8,128)S(1)} %get-tuple-element.24.piece), channel_id=1, source_target_pairs={{0,96},{8,104},{16,112},{24,120},{32,0},{40,8},{48,16},{56,24},{64... | collective-permute-start | bytes 294920 | tf_op jit(solution)/shard_map/ppermute | solution.py:24
  3.0 10.0 %collective-permute-start.3 = (f32[192,128]{1,0:T(8,128)S(1)}, f32[192,128]{1,0:T(8,128)S(1)}, u32[]{:S(2)}, u32[]{:S(2)}) collective-permute-start(f32[192,128]{1,0:T(8,128)S(1)} %get-tuple-element.24.piece), channel_id=1, source_target_pairs={{0,48},{8,56},{16,64},{24,72},{32,80},{40,88},{48,96},{56,104},{64... | collective-permute-start | bytes 294920 | tf_op jit(solution)/shard_map/ppermute | solution.py:24
  6.3 6.7 %collective-permute-start.4 = (f32[192,128]{1,0:T(8,128)S(1)}, f32[192,128]{1,0:T(8,128)S(1)}, u32[]{:S(2)}, u32[]{:S(2)}) collective-permute-start(f32[192,128]{1,0:T(8,128)S(1)} %get-tuple-element.24.piece), channel_id=1, source_target_pairs={{0,64},{16,80},{32,96},{48,112},{64,0},{80,16},{96,32},{112,48},{1... | collective-permute-start | bytes 294920 | tf_op jit(solution)/shard_map/ppermute | solution.py:38
  15.5 1.6 %collective-permute-start.5 = (f32[8,64,128]{2,1,0:T(8,128)S(1)}, f32[8,64,128]{2,1,0:T(8,128)S(1)}, u32[]{:S(2)}, u32[]{:S(2)}) collective-permute-start(f32[8,64,128]{2,1,0:T(8,128)S(1)} %get-tuple-element.35), channel_id=1, source_target_pairs={{0,8},{8,0},{16,24},{24,16},{32,40},{40,32},{48,56},{56,48},{64,72... | collective-permute-start | bytes 786440 | tf_op jit(solution)/shard_map/ppermute | solution.py:24
  17.8 16.6 %all-to-all-start = ((f32[8,64,128]{2,1,0:T(8,128)}), f32[8,64,128]{2,1,0:T(8,128)S(1)}, u32[]{:S(2)}, u32[]{:S(2)}) async-start(f32[8,64,128]{2,1,0:T(8,128)} %add.18), calls=%async_computation | async-start | bytes 524288 | tf_op jit(solution)/shard_map/all_to_all | solution.py:289
  26.1 8.4 %collective-permute-start.9 = (f32[64,128]{1,0:T(8,128)S(1)}, f32[64,128]{1,0:T(8,128)S(1)}, u32[]{:S(2)}, u32[]{:S(2)}) collective-permute-start(f32[64,128]{1,0:T(8,128)S(1)} %get-tuple-element.39), channel_id=1, source_target_pairs={{0,80},{8,88},{16,96},{24,104},{32,112},{40,120},{48,0},{56,8},{64... | collective-permute-start | bytes 98312 | tf_op jit(solution)/shard_map/ppermute | solution.py:24
  26.1 8.4 %collective-permute-start.8 = (f32[64,128]{1,0:T(8,128)S(1)}, f32[64,128]{1,0:T(8,128)S(1)}, u32[]{:S(2)}, u32[]{:S(2)}) collective-permute-start(f32[64,128]{1,0:T(8,128)S(1)} %get-tuple-element.38), channel_id=1, source_target_pairs={{0,32},{8,40},{16,48},{24,56},{32,64},{40,72},{48,80},{56,88},{64,... | collective-permute-start | bytes 98312 | tf_op jit(solution)/shard_map/ppermute | solution.py:24
  29.0 5.5 %collective-permute-start.6 = (f32[64,128]{1,0:T(8,128)S(1)}, f32[64,128]{1,0:T(8,128)S(1)}, u32[]{:S(2)}, u32[]{:S(2)}) collective-permute-start(f32[64,128]{1,0:T(8,128)S(1)} %get-tuple-element.36), channel_id=1, source_target_pairs={{0,16},{8,24},{16,32},{24,40},{32,48},{40,56},{48,64},{56,72},{64,... | collective-permute-start | bytes 98312 | tf_op jit(solution)/shard_map/ppermute | solution.py:24
  31.7 5.8 %collective-permute-start.7 = (f32[64,128]{1,0:T(8,128)S(1)}, f32[64,128]{1,0:T(8,128)S(1)}, u32[]{:S(2)}, u32[]{:S(2)}) collective-permute-start(f32[64,128]{1,0:T(8,128)S(1)} %get-tuple-element.37), channel_id=1, source_target_pairs={{0,64},{16,80},{32,96},{48,112},{64,0},{80,16},{96,32},{112,48},{1... | collective-permute-start | bytes 98312 | tf_op jit(solution)/shard_map/ppermute | solution.py:38

commit v4 on v3

--- a/solution.py
+++ b/solution.py
@@ -34,8 +34,7 @@
 
 def across_the_ring(value):
     count = lax.axis_size("blk")
-    pairs = [(block, (block + count // 2) % count) for block in range(0, count, 2)]
-    return lax.ppermute(value, "blk", pairs)
+    return permuted(value, lambda block: block + count // 2)
 
 
 def two_parts(x):
@@ -156,7 +155,7 @@
     return right, right_norms, right_vectors
 
 
-def tile_products(side, loaded, total_in, total, mirrored):
+def tile_products(side, loaded, total_in, total, mirrored, both=True):
     left, left_norms, left_vectors = side
     right, right_norms, right_vectors = loaded
     rows = left.shape[0]
@@ -173,6 +172,8 @@
         high, low = two_parts(kernel)
         direct = across(side_by_side(high, low), right_vectors)
         total[here, :] = direct if total_in is None else total_in[here, :] + direct
+        if not both:
+            continue
         own = left_vectors[:columns, here]
         own_low = left_vectors[columns:, here]
         part = jnp.dot(
@@ -200,6 +201,15 @@
     return rows * count * LANES * (6 * feats + 8 * columns)
 
 
+def side_shapes(rows, feats, columns):
+    return (
+        ((rows, 2 * columns), F32),
+        ((rows, 6 * feats), BF16),
+        ((rows, LANES), F32),
+        ((2 * columns, rows), BF16),
+    )
+
+
 def early_tiles(packed, other_packed, piece, arrived):
     feats = packed.shape[1]
     columns = piece.shape[0] - LANES
@@ -207,8 +217,10 @@
 
     def body(
         packed, other_packed, piece, arrived,
-        total, left, norms, vectors, other_total, other_left, other_norms, other_vectors, back_ref,
+        total, left, norms, vectors, other_total, other_left, other_norms, other_vectors,
+        back_ref, again_ref,
     ):
+        again_ref[...] = piece[...]
         load_left(packed, left, norms, vectors)
         load_left(other_packed, other_left, other_norms, other_vectors)
         loaded = load_right((piece, arrived))
@@ -217,58 +229,60 @@
         mirrored = tile_products(other, loaded, None, other_total, mirrored)
         back_ref[...] = folded(mirrored)[:, LANES:]
 
-    side = (
-        ((rows, 2 * columns), F32),
-        ((rows, 6 * feats), BF16),
-        ((rows, LANES), F32),
-        ((2 * columns, rows), BF16),
-    )
-    outs = side + side + (((columns, LANES), F32),)
+    side = side_shapes(rows, feats, columns)
+    outs = side + side + (((columns, LANES), F32), (piece.shape, F32))
     args = (packed, other_packed, piece, arrived)
     out = local_call(body, outs, args, macs=macs_of(2 * rows, feats, columns, 2))
-    return out[:4], out[4:8], out[8]
-
-
-def other_tiles(side, pieces):
-    total, left, norms, vectors = side
-    rows, columns = left.shape[0], vectors.shape[0] // 2
-
-    def body(total_in, left, norms, vectors, *refs):
-        arrived, turned_ref, shared_ref, back_ref, total = refs[:3], *refs[3:]
+    return out[:4], out[4:8], out[8], out[9]
+
+
+def later_tiles(side, other_side, pieces):
+    rows, columns = side[1].shape[0], side[3].shape[0] // 2
+
+    def body(total_in, left, norms, vectors, other_in, other_left, other_norms, other_vectors, *refs):
+        arrived, total, other_total, first_ref, second_ref = refs[:2], *refs[2:]
         loaded = load_right(arrived)
         mirrored = tile_products((left, norms, vectors), loaded, total_in, total, None)
-        shared_ref[...] = mirrored[:, : 2 * LANES]
-        back_ref[...] = folded(mirrored[:, 2 * LANES :])
-        write_turned(total, turned_ref)
-
-    outs = (
-        ((rows // LANES, columns, LANES), F32),
-        ((2 * columns, 2 * LANES), F32),
-        ((columns, LANES), F32),
-    )
-    scratch = (pltpu.VMEM((rows, 2 * columns), F32),)
-    macs = macs_of(rows, left.shape[1] // 6, columns, 3)
-    return local_call(body, outs, (total, left, norms, vectors, *pieces), scratch, macs=macs)
-
-
-def own_tiles(side, shared, pieces):
-    total, left, norms, vectors = side
-    rows, columns = left.shape[0], vectors.shape[0] // 2
-
-    def body(total_in, left, norms, vectors, shared_ref, *refs):
-        arrived, turned_ref, first_ref, second_ref, total = refs[:2], *refs[2:]
-        loaded = load_right(arrived)
-        mirrored = tile_products((left, norms, vectors), loaded, total_in, total, shared_ref[...])
+        other = (other_left, other_norms, other_vectors)
+        mirrored = tile_products(other, loaded, other_in, other_total, mirrored)
         mirrored = folded(mirrored)
         first_ref[...] = mirrored[:, :LANES]
         second_ref[...] = mirrored[:, LANES:]
+
+    total_shape = ((rows, 2 * columns), F32)
+    back = ((columns, LANES), F32)
+    outs = (total_shape, total_shape, back, back)
+    macs = macs_of(2 * rows, side[1].shape[1] // 6, columns, 2)
+    return local_call(body, outs, (*side, *other_side, *pieces), macs=macs)
+
+
+def ring_tiles(side, piece):
+    total, left, norms, vectors = side
+    rows, columns = left.shape[0], vectors.shape[0] // 2
+
+    def body(total_in, left, norms, vectors, piece, turned_ref, total):
+        loaded = load_right((piece,))
+        tile_products((left, norms, vectors), loaded, total_in, total, None, both=False)
         write_turned(total, turned_ref)
 
-    back = ((columns, LANES), F32)
-    outs = (((rows // LANES, columns, LANES), F32), back, back)
+    outs = (((rows // LANES, columns, LANES), F32),)
     scratch = (pltpu.VMEM((rows, 2 * columns), F32),)
-    macs = macs_of(rows, left.shape[1] // 6, columns, 2)
-    return local_call(body, outs, (total, left, norms, vectors, shared, *pieces), scratch, macs=macs)
+    macs = macs_of(rows, left.shape[1] // 6, columns, 1)
+    return local_call(body, outs, (total, left, norms, vectors, piece), scratch, macs=macs)[0]
+
+
+def joined(total, from_other, returned):
+    def body(total, from_other, *refs):
+        parts, tiles = refs[:-1], refs[-1]
+        write_turned(total, tiles)
+        tiles[...] += from_other[...]
+        layer = lax.axis_index("layer")
+        returned = parts[0][...]
+        for part in parts[1:]:
+            returned = returned + part[...]
+        tiles[layer, :, :] += returned
+
+    return local_call(body, ((from_other.shape, F32),), (total, from_other, *returned))[0]
 
 
 def per_device(points, inv_scale, vectors, noise):
@@ -280,21 +294,15 @@
     other_packed = swapped(packed)
     middle_piece = stepped(piece, middle)
     far_piece = stepped(piece, far)
+    own, other, near_back, piece = early_tiles(packed, other_packed, piece, near_piece)
     ring_piece = across_the_ring(piece)
-    own, other, near_back = early_tiles(packed, other_packed, piece, near_piece)
     near_back = stepped(near_back, -near)
-    for_other, shared, ring_back = other_tiles(other, (middle_piece, far_piece, ring_piece))
-    from_other = swapped(for_other)
-    direct, middle_back, far_back = own_tiles(own, shared, (middle_piece, far_piece))
-    tiles = lax.all_to_all(direct + from_other, "layer", 0, 0, tiled=True)
-    returned = (
-        near_back
-        + across_the_ring(ring_back)
-        + stepped(middle_back, -middle)
-        + stepped(far_back, -far)
-    )
+    total, other_total, middle_back, far_back = later_tiles(own, other, (middle_piece, far_piece))
+    returned = (near_back, stepped(middle_back, -middle), stepped(far_back, -far))
+    from_other = swapped(ring_tiles((other_total, *other[1:]), ring_piece))
+    tiles = lax.all_to_all(joined(total, from_other, returned), "layer", 0, 0, tiled=True)
     normalizer = float(rows * (2 * layers - 1)) ** (-0.5)
-    return ((jnp.sum(tiles, axis=0) + returned) * normalizer + noise_term).T
+    return (jnp.sum(tiles, axis=0) * normalizer + noise_term).T
 
 
 def solution(mesh):

time: 38.4 us -> 46.1 us (1.20)
  the two profiles are of different devices: /device:TPU:30 before, /device:TPU:0 now
where the time goes in v4:
time: 46.1 us; the launch traced here: 45.9 us
  blocking collectives  16.3 us (35%)
  starting transfers between devices  12.2 us (26%)
  waiting for transfers between devices  8.63 us (19%)
  Pallas kernels  8.05 us (17%)
  other arithmetic  0.64 us (1%)
    all_to_all x1, blocking collectives, per_device(): lax.all_to_all(joined(total, from_other, returned), 'layer', 0, 0, tiled=...  16.3 us
    ppermute x9, starting transfers between devices, permuted(): return lax.ppermute(value, 'blk', pairs)  12.2 us
    ppermute x9, waiting for transfers between devices, permuted(): return lax.ppermute(value, 'blk', pairs)  8.63 us
    pallas_call x5, Pallas kernels, local_call(): pl.pallas_call(body, out_shape=tuple((jax.ShapeDtypeStruct(shape, kind) f...  8.05 us
  transfers between devices with their start and end apart: 9, of which 6 were waited for; matrix products, arithmetic and copies ran while one was open for 0% of the time, Pallas kernels for 12%

profile of v4, /device:TPU:0, one launch (start us, length us, event | category | flops | bytes accessed | tf_op | source)
XLA Modules:
  0.0 45.9 jit_solution(11875646473312604368)
XLA Ops:
  0.0 1.2 %shard_map.46 = (f32[1536,128]{1,0:T(8,128)S(1)}, f32[192,128]{1,0:T(8,128)S(1)}, f32[64,128]{1,0:T(8,128)S(1)}) custom-call(f32[1024,128]{1,0:T(8,128)} %points_hbm.1, f32[64,1024]{1,0:T(8,128)} %bitcast.5, f32[1,128]{1,0:T(1,128)} %bitcast.6, f32[1,128]{1,0:T(1,128)} %bitcast.7), custom_call_target="tpu_custom_call" | custom-call | bytes 1048576 | tf_op jit(solution)/shard_map/pallas_call | solution.py:66
  1.2 0.1 collective-permute-start
  1.3 4.1 %collective-permute-start.1 = (f32[192,128]{1,0:T(8,128)S(1)}, f32[192,128]{1,0:T(8,128)S(1)}, u32[]{:S(2)}, u32[]{:S(2)}) collective-permute-start(f32[192,128]{1,0:T(8,128)S(1)} %get-tuple-element.23.piece), channel_id=1, source_target_pairs={{0,112},{8,120},{16,0},{24,8},{32,16},{40,24},{48,32},{56,40},{64,... | collective-permute-start | bytes 294920 | tf_op jit(solution)/shard_map/ppermute | solution.py:24
  5.4 0.6 %collective-permute-start.2 = (f32[192,128]{1,0:T(8,128)S(1)}, f32[192,128]{1,0:T(8,128)S(1)}, u32[]{:S(2)}, u32[]{:S(2)}) collective-permute-start(f32[192,128]{1,0:T(8,128)S(1)} %get-tuple-element.23.piece), channel_id=1, source_target_pairs={{0,96},{8,104},{16,112},{24,120},{32,0},{40,8},{48,16},{56,24},{64... | collective-permute-start | bytes 294920 | tf_op jit(solution)/shard_map/ppermute | solution.py:24
  6.0 0.0 collective-permute-start.3
  6.1 2.4 %collective-permute-done.1.arrived = f32[192,128]{1,0:T(8,128)S(1)} collective-permute-done((f32[192,128]{1,0:T(8,128)S(1)}, f32[192,128]{1,0:T(8,128)S(1)}, u32[]{:S(2)}, u32[]{:S(2)}) %collective-permute-start.1) | collective-permute-done | bytes 98336 | tf_op jit(solution)/shard_map/ppermute | solution.py:24
  8.5 0.0 collective-permute-done.other_packed
  8.5 2.9 %shard_map.47 = (f32[1024,128]{1,0:T(8,128)S(1)}, bf16[1024,768]{1,0:T(8,128)(2,1)S(1)}, f32[1024,128]{1,0:T(8,128)S(1)}, bf16[128,1024]{1,0:T(8,128)(2,1)S(1)},...) custom-call(f32[1536,128]{1,0:T(8,128)S(1)} %get-tuple-element.22.pa, ...), custom_call_target="tpu_custom_call" | custom-call | flops 1342177280 | bytes 1048576 | tf_op jit(solution)/shard_map/pallas_call | solution.py:66
  11.4 0.6 %collective-permute-start.4 = (f32[192,128]{1,0:T(8,128)S(1)}, f32[192,128]{1,0:T(8,128)S(1)}, u32[]{:S(2)}, u32[]{:S(2)}) collective-permute-start(f32[192,128]{1,0:T(8,128)S(1)} %get-tuple-element.34), channel_id=1, source_target_pairs={{0,64},{8,72},{16,80},{24,88},{32,96},{40,104},{48,112},{56,120},{... | collective-permute-start | bytes 294920 | tf_op jit(solution)/shard_map/ppermute | solution.py:24
  12.0 0.0 collective-permute-done.2.refs_0_
  12.0 0.7 %collective-permute-done.3.refs_1_ = f32[192,128]{1,0:T(8,128)S(1)} collective-permute-done((f32[192,128]{1,0:T(8,128)S(1)}, f32[192,128]{1,0:T(8,128)S(1)}, u32[]{:S(2)}, u32[]{:S(2)}) %collective-permute-start.3) | collective-permute-done | bytes 98336 | tf_op jit(solution)/shard_map/ppermute | solution.py:24
  12.7 2.7 %shard_map.48 = (f32[1024,128]{1,0:T(8,128)S(1)}, f32[1024,128]{1,0:T(8,128)S(1)}, f32[64,128]{1,0:T(8,128)S(1)}, f32[64,128]{1,0:T(8,128)S(1)}) custom-call(f32[1024,128]{1,0:T(8,128)S(1)} %get-tuple-element.24.total_in, bf16[1024,768]{1,0:T(8,128)(2,1)S(1)} %get-tuple-element.25.left, f32[1024,128]{1,0:T(8,128)S(1)} %get-tuple-element.26.norms, ...), custom_call_target="tpu_custom_call" | custom-call | flops 1342177280 | bytes 1048576 | tf_op jit(solution)/shard_map/pallas_call | solution.py:66
  15.4 0.7 %collective-permute-done.4.piece = f32[192,128]{1,0:T(8,128)S(1)} collective-permute-done((f32[192,128]{1,0:T(8,128)S(1)}, f32[192,128]{1,0:T(8,128)S(1)}, u32[]{:S(2)}, u32[]{:S(2)}) %collective-permute-start.4) | collective-permute-done | bytes 98336 | tf_op jit(solution)/shard_map/ppermute | solution.py:24
  16.1 1.1 %shard_map.49 = f32[8,64,128]{2,1,0:T(8,128)S(1)} custom-call(f32[1024,128]{1,0:T(8,128)S(1)} %get-tuple-element.33.total_in, bf16[1024,768]{1,0:T(8,128)(2,1)S(1)} %get-tuple-element.29.other_left.left, f32[1024,128]{1,0:T(8,128)S(1)} %get-tuple-element.30.other_norms.norms, bf16[128,1024]{1,0:T(8,128)(2,1)S(1)} %get-tuple-element.31.other_vectors.vectors, ...), custom_call_target="tpu_custom_call" | custom-call | flops 335544320 | bytes 1048576 | tf_op jit(solution)/shard_map/pallas_call | solution.py:66
  17.2 0.1 collective-permute-start.5
  17.3 0.1 collective-permute-start.6
  17.4 6.3 %collective-permute-start.7 = (f32[64,128]{1,0:T(8,128)S(1)}, f32[64,128]{1,0:T(8,128)S(1)}, u32[]{:S(2)}, u32[]{:S(2)}) collective-permute-start(f32[64,128]{1,0:T(8,128)S(1)} %get-tuple-element.36), channel_id=1, source_target_pairs={{0,32},{8,40},{16,48},{24,56},{32,64},{40,72},{48,80},{56,88},{64,... | collective-permute-start | bytes 98312 | tf_op jit(solution)/shard_map/ppermute | solution.py:24
  23.6 0.4 collective-permute-start.8
  24.0 1.3 %collective-permute-done.6.refs_0_ = f32[64,128]{1,0:T(8,128)S(1)} collective-permute-done((f32[64,128]{1,0:T(8,128)S(1)}, f32[64,128]{1,0:T(8,128)S(1)}, u32[]{:S(2)}, u32[]{:S(2)}) %collective-permute-start.6) | collective-permute-done | bytes 32800 | tf_op jit(solution)/shard_map/ppermute | solution.py:24
  25.3 1.3 %collective-permute-done.7.refs_1_ = f32[64,128]{1,0:T(8,128)S(1)} collective-permute-done((f32[64,128]{1,0:T(8,128)S(1)}, f32[64,128]{1,0:T(8,128)S(1)}, u32[]{:S(2)}, u32[]{:S(2)}) %collective-permute-start.7) | collective-permute-done | bytes 32800 | tf_op jit(solution)/shard_map/ppermute | solution.py:24
  26.6 2.2 %collective-permute-done.8.refs_2_ = f32[64,128]{1,0:T(8,128)S(1)} collective-permute-done((f32[64,128]{1,0:T(8,128)S(1)}, f32[64,128]{1,0:T(8,128)S(1)}, u32[]{:S(2)}, u32[]{:S(2)}) %collective-permute-start.8) | collective-permute-done | bytes 32800 | tf_op jit(solution)/shard_map/ppermute | solution.py:24
  28.8 0.0 collective-permute-done.5.from_other
  28.8 0.2 shard_map.50
  29.0 16.3 %all_to_all.5 = f32[8,64,128]{2,1,0:T(8,128)S(1)} all-to-all(f32[8,64,128]{2,1,0:T(8,128)S(1)} %shard_map.50), channel_id=1, replica_groups=mesh['blk'=16,'layer'=8] {'layer'}, dimensions={0} | all-to-all | bytes 524288 | tf_op jit(solution)/shard_map/all_to_all | solution.py:303
  45.3 0.6 %add_bitcast_fusion = f32[128,64]{0,1:T(8,128)} fusion(f32[64,128]{1,0:T(8,128)S(1)} %get-tuple-element.38, f32[64,128]{1,0:T(8,128)S(1)} %reduce_sum.9), kind=kLoop, calls=%fused_computation | loop fusion | flops 16384 | bytes 98304 | tf_op jit(solution)/shard_map/transpose | solution.py:305
  (1 shorter events, 0.0 us)
Async XLA Ops:
  1.2 7.3 %collective-permute-start = (f32[1536,128]{1,0:T(8,128)S(1)}, f32[1536,128]{1,0:T(8,128)S(1)}, u32[]{:S(2)}, u32[]{:S(2)}) collective-permute-start(f32[1536,128]{1,0:T(8,128)S(1)} %get-tuple-element.22.packed), channel_id=1, source_target_pairs={{0,8},{8,0},{16,24},{24,16},{32,40},{40,32},{48,56},{56,48},{64,72... | collective-permute-start | bytes 2359304 | tf_op jit(solution)/shard_map/ppermute | solution.py:24
  1.3 7.2 %collective-permute-start.1 = (f32[192,128]{1,0:T(8,128)S(1)}, f32[192,128]{1,0:T(8,128)S(1)}, u32[]{:S(2)}, u32[]{:S(2)}) collective-permute-start(f32[192,128]{1,0:T(8,128)S(1)} %get-tuple-element.23.piece), channel_id=1, source_target_pairs={{0,112},{8,120},{16,0},{24,8},{32,16},{40,24},{48,32},{56,40},{64,... | collective-permute-start | bytes 294920 | tf_op jit(solution)/shard_map/ppermute | solution.py:24
  5.4 6.6 %collective-permute-start.2 = (f32[192,128]{1,0:T(8,128)S(1)}, f32[192,128]{1,0:T(8,128)S(1)}, u32[]{:S(2)}, u32[]{:S(2)}) collective-permute-start(f32[192,128]{1,0:T(8,128)S(1)} %get-tuple-element.23.piece), channel_id=1, source_target_pairs={{0,96},{8,104},{16,112},{24,120},{32,0},{40,8},{48,16},{56,24},{64... | collective-permute-start | bytes 294920 | tf_op jit(solution)/shard_map/ppermute | solution.py:24
  6.0 6.7 %collective-permute-start.3 = (f32[192,128]{1,0:T(8,128)S(1)}, f32[192,128]{1,0:T(8,128)S(1)}, u32[]{:S(2)}, u32[]{:S(2)}) collective-permute-start(f32[192,128]{1,0:T(8,128)S(1)} %get-tuple-element.23.piece), channel_id=1, source_target_pairs={{0,48},{8,56},{16,64},{24,72},{32,80},{40,88},{48,96},{56,104},{64... | collective-permute-start | bytes 294920 | tf_op jit(solution)/shard_map/ppermute | solution.py:24
  11.4 4.7 %collective-permute-start.4 = (f32[192,128]{1,0:T(8,128)S(1)}, f32[192,128]{1,0:T(8,128)S(1)}, u32[]{:S(2)}, u32[]{:S(2)}) collective-permute-start(f32[192,128]{1,0:T(8,128)S(1)} %get-tuple-element.34), channel_id=1, source_target_pairs={{0,64},{8,72},{16,80},{24,88},{32,96},{40,104},{48,112},{56,120},{... | collective-permute-start | bytes 294920 | tf_op jit(solution)/shard_map/ppermute | solution.py:24
  17.2 11.6 %collective-permute-start.5 = (f32[8,64,128]{2,1,0:T(8,128)S(1)}, f32[8,64,128]{2,1,0:T(8,128)S(1)}, u32[]{:S(2)}, u32[]{:S(2)}) collective-permute-start(f32[8,64,128]{2,1,0:T(8,128)S(1)} %shard_map.49), channel_id=1, source_target_pairs={{0,8},{8,0},{16,24},{24,16},{32,40},{40,32},{48,56},{56,48},{64,72... | collective-permute-start | bytes 786440 | tf_op jit(solution)/shard_map/ppermute | solution.py:24
  17.3 8.0 %collective-permute-start.6 = (f32[64,128]{1,0:T(8,128)S(1)}, f32[64,128]{1,0:T(8,128)S(1)}, u32[]{:S(2)}, u32[]{:S(2)}) collective-permute-start(f32[64,128]{1,0:T(8,128)S(1)} %get-tuple-element.35), channel_id=1, source_target_pairs={{0,16},{8,24},{16,32},{24,40},{32,48},{40,56},{48,64},{56,72},{64,... | collective-permute-start | bytes 98312 | tf_op jit(solution)/shard_map/ppermute | solution.py:24
  17.4 9.2 %collective-permute-start.7 = (f32[64,128]{1,0:T(8,128)S(1)}, f32[64,128]{1,0:T(8,128)S(1)}, u32[]{:S(2)}, u32[]{:S(2)}) collective-permute-start(f32[64,128]{1,0:T(8,128)S(1)} %get-tuple-element.36), channel_id=1, source_target_pairs={{0,32},{8,40},{16,48},{24,56},{32,64},{40,72},{48,80},{56,88},{64,... | collective-permute-start | bytes 98312 | tf_op jit(solution)/shard_map/ppermute | solution.py:24
  23.6 5.1 %collective-permute-start.8 = (f32[64,128]{1,0:T(8,128)S(1)}, f32[64,128]{1,0:T(8,128)S(1)}, u32[]{:S(2)}, u32[]{:S(2)}) collective-permute-start(f32[64,128]{1,0:T(8,128)S(1)} %get-tuple-element.37), channel_id=1, source_target_pairs={{0,80},{8,88},{16,96},{24,104},{32,112},{40,120},{48,0},{56,8},{64... | collective-permute-start | bytes 98312 | tf_op jit(solution)/shard_map/ppermute | solution.py:24

commit v5 on v4

--- a/solution.py
+++ b/solution.py
@@ -155,7 +155,7 @@
     return right, right_norms, right_vectors
 
 
-def tile_products(side, loaded, total_in, total, mirrored, both=True):
+def tile_products(side, loaded, total_in, total, mirrored, backs):
     left, left_norms, left_vectors = side
     right, right_norms, right_vectors = loaded
     rows = left.shape[0]
@@ -172,13 +172,14 @@
         high, low = two_parts(kernel)
         direct = across(side_by_side(high, low), right_vectors)
         total[here, :] = direct if total_in is None else total_in[here, :] + direct
-        if not both:
+        if backs == 0:
             continue
+        wide = backs * LANES
         own = left_vectors[:columns, here]
         own_low = left_vectors[columns:, here]
         part = jnp.dot(
             stacked(side_by_side(own, own), side_by_side(own_low, zero)),
-            stacked(high, low),
+            stacked(high[:, :wide], low[:, :wide]),
             preferred_element_type=F32,
         )
         mirrored = part if mirrored is None else mirrored + part
@@ -210,41 +211,35 @@
     )
 
 
-def early_tiles(packed, other_packed, piece, arrived):
+def first_tiles(packed, other_packed, piece):
     feats = packed.shape[1]
     columns = piece.shape[0] - LANES
     rows = packed.shape[0] * LANES // (LANES + columns)
 
-    def body(
-        packed, other_packed, piece, arrived,
-        total, left, norms, vectors, other_total, other_left, other_norms, other_vectors,
-        back_ref, again_ref,
-    ):
+    def body(packed, other_packed, piece, *refs):
+        own, other, again_ref = refs[:4], refs[4:8], refs[8]
         again_ref[...] = piece[...]
-        load_left(packed, left, norms, vectors)
-        load_left(other_packed, other_left, other_norms, other_vectors)
-        loaded = load_right((piece, arrived))
-        mirrored = tile_products((left, norms, vectors), loaded, None, total, None)
-        other = (other_left, other_norms, other_vectors)
-        mirrored = tile_products(other, loaded, None, other_total, mirrored)
-        back_ref[...] = folded(mirrored)[:, LANES:]
+        loaded = load_right((piece,))
+        for source, (total, *side) in ((packed, own), (other_packed, other)):
+            load_left(source, *side)
+            tile_products(side, loaded, None, total, None, 0)
 
     side = side_shapes(rows, feats, columns)
-    outs = side + side + (((columns, LANES), F32), (piece.shape, F32))
-    args = (packed, other_packed, piece, arrived)
-    out = local_call(body, outs, args, macs=macs_of(2 * rows, feats, columns, 2))
-    return out[:4], out[4:8], out[8], out[9]
-
-
-def later_tiles(side, other_side, pieces):
-    rows, columns = side[1].shape[0], side[3].shape[0] // 2
-
-    def body(total_in, left, norms, vectors, other_in, other_left, other_norms, other_vectors, *refs):
-        arrived, total, other_total, first_ref, second_ref = refs[:2], *refs[2:]
+    outs = side + side + ((piece.shape, F32),)
+    macs = macs_of(2 * rows, feats, columns, 1)
+    out = local_call(body, outs, (packed, other_packed, piece), macs=macs)
+    return out[:4], out[4:8], out[8]
+
+
+def shared_tiles(own, other, pieces):
+    rows, columns = own[1].shape[0], own[3].shape[0] // 2
+
+    def body(*refs):
+        (own_in, *own_side), (other_in, *other_side) = refs[:4], refs[4:8]
+        arrived, total, other_total, first_ref, second_ref = refs[8:10], *refs[10:]
         loaded = load_right(arrived)
-        mirrored = tile_products((left, norms, vectors), loaded, total_in, total, None)
-        other = (other_left, other_norms, other_vectors)
-        mirrored = tile_products(other, loaded, other_in, other_total, mirrored)
+        mirrored = tile_products(own_side, loaded, own_in, total, None, 2)
+        mirrored = tile_products(other_side, loaded, other_in, other_total, mirrored, 2)
         mirrored = folded(mirrored)
         first_ref[...] = mirrored[:, :LANES]
         second_ref[...] = mirrored[:, LANES:]
@@ -252,37 +247,43 @@
     total_shape = ((rows, 2 * columns), F32)
     back = ((columns, LANES), F32)
     outs = (total_shape, total_shape, back, back)
-    macs = macs_of(2 * rows, side[1].shape[1] // 6, columns, 2)
-    return local_call(body, outs, (*side, *other_side, *pieces), macs=macs)
-
-
-def ring_tiles(side, piece):
-    total, left, norms, vectors = side
-    rows, columns = left.shape[0], vectors.shape[0] // 2
-
-    def body(total_in, left, norms, vectors, piece, turned_ref, total):
-        loaded = load_right((piece,))
-        tile_products((left, norms, vectors), loaded, total_in, total, None, both=False)
+    macs = macs_of(2 * rows, own[1].shape[1] // 6, columns, 2)
+    return local_call(body, outs, (*own, *other, *pieces), macs=macs)
+
+
+def other_tiles(side, pieces):
+    rows, columns = side[1].shape[0], side[3].shape[0] // 2
+
+    def body(*refs):
+        (total_in, *side), arrived, turned_ref, part_ref, total = refs[:4], refs[4:6], *refs[6:]
+        part_ref[...] = tile_products(side, load_right(arrived), total_in, total, None, 1)
         write_turned(total, turned_ref)
 
-    outs = (((rows // LANES, columns, LANES), F32),)
+    outs = (((rows // LANES, columns, LANES), F32), ((2 * columns, LANES), F32))
     scratch = (pltpu.VMEM((rows, 2 * columns), F32),)
-    macs = macs_of(rows, left.shape[1] // 6, columns, 1)
-    return local_call(body, outs, (total, left, norms, vectors, piece), scratch, macs=macs)[0]
-
-
-def joined(total, from_other, returned):
-    def body(total, from_other, *refs):
-        parts, tiles = refs[:-1], refs[-1]
+    macs = macs_of(rows, side[1].shape[1] // 6, columns, 2)
+    return local_call(body, outs, (*side, *pieces), scratch, macs=macs)
+
+
+def own_tiles(side, part, piece):
+    rows, columns = side[1].shape[0], side[3].shape[0] // 2
+
+    def body(*refs):
+        (total_in, *side), part_ref, arrived, total, back_ref = refs[:4], *refs[4:]
+        loaded = load_right((arrived,))
+        back_ref[...] = folded(tile_products(side, loaded, total_in, total, part_ref[...], 1))
+
+    outs = (((rows, 2 * columns), F32), ((columns, LANES), F32))
+    macs = macs_of(rows, side[1].shape[1] // 6, columns, 1)
+    return local_call(body, outs, (*side, part, piece), macs=macs)
+
+
+def joined(total, from_other):
+    def body(total, from_other, tiles):
         write_turned(total, tiles)
         tiles[...] += from_other[...]
-        layer = lax.axis_index("layer")
-        returned = parts[0][...]
-        for part in parts[1:]:
-            returned = returned + part[...]
-        tiles[layer, :, :] += returned
-
-    return local_call(body, ((from_other.shape, F32),), (total, from_other, *returned))[0]
+
+    return local_call(body, ((from_other.shape, F32),), (total, from_other))[0]
 
 
 def per_device(points, inv_scale, vectors, noise):
@@ -294,15 +295,20 @@
     other_packed = swapped(packed)
     middle_piece = stepped(piece, middle)
     far_piece = stepped(piece, far)
-    own, other, near_back, piece = early_tiles(packed, other_packed, piece, near_piece)
+    own, other, piece = first_tiles(packed, other_packed, piece)
     ring_piece = across_the_ring(piece)
-    near_back = stepped(near_back, -near)
-    total, other_total, middle_back, far_back = later_tiles(own, other, (middle_piece, far_piece))
-    returned = (near_back, stepped(middle_back, -middle), stepped(far_back, -far))
-    from_other = swapped(ring_tiles((other_total, *other[1:]), ring_piece))
-    tiles = lax.all_to_all(joined(total, from_other, returned), "layer", 0, 0, tiled=True)
+    total, other_total, near_back, middle_back = shared_tiles(
+        own, other, (near_piece, middle_piece)
+    )
+    for_other, part = other_tiles((other_total, *other[1:]), (far_piece, ring_piece))
+    from_other = swapped(for_other)
+    total, far_back = own_tiles((total, *own[1:]), part, far_piece)
+    tiles = lax.all_to_all(joined(total, from_other), "layer", 0, 0, tiled=True)
+    returned = (
+        stepped(near_back, -near) + stepped(middle_back, -middle) + stepped(far_back, -far)
+    )
     normalizer = float(rows * (2 * layers - 1)) ** (-0.5)
-    return (jnp.sum(tiles, axis=0) * normalizer + noise_term).T
+    return ((jnp.sum(tiles, axis=0) + returned) * normalizer + noise_term).T
 
 
 def solution(mesh):

time: 46.1 us -> 36.8 us (0.80)
  blocking collectives: 16.3 us -> 0 us
  starting transfers between devices: 12.2 us -> 19.1 us
  waiting for transfers between devices: 8.63 us -> 6.32 us
  Pallas kernels: 8.05 us -> 10.2 us
    all_to_all x1 -> x0, blocking collectives: 16.3 us -> none  [per_device(): lax.all_to_all(joined(total, from_other, returned), 'layer', 0, 0, tiled=...]
    all_to_all x0 -> x1, starting transfers between devices: none -> 7.48 us  [per_device(): tiles = lax.all_to_all(joined(total, from_other), 'layer', 0, 0, tiled=True)]
    ppermute x9, waiting for transfers between devices: 8.63 us -> 1.95 us  [permuted(): return lax.ppermute(value, 'blk', pairs)]
    all_to_all x0 -> x1, waiting for transfers between devices: none -> 4.38 us  [per_device(): tiles = lax.all_to_all(joined(total, from_other), 'layer', 0, 0, tiled=True)]
    pallas_call x5 -> x6, Pallas kernels: 8.05 us -> 10.2 us  [local_call(): pl.pallas_call(body, out_shape=tuple((jax.ShapeDtypeStruct(shape, kind) f...]
    ppermute x9, starting transfers between devices: 12.2 us -> 11.6 us  [permuted(): return lax.ppermute(value, 'blk', pairs)]
  transfers between devices with their start and end apart: 9 -> 10, of which waited for: 6 -> 3; matrix products, arithmetic and copies ran while one was open for 0% -> 0% of each run, Pallas kernels for 12% -> 17%
where the time goes in v5:
time: 36.8 us; the launch traced here: 36.3 us
  starting transfers between devices  19.1 us (52%)
  Pallas kernels  10.2 us (28%)
  waiting for transfers between devices  6.32 us (17%)
  other arithmetic  0.65 us (2%)
    ppermute x9, starting transfers between devices, permuted(): return lax.ppermute(value, 'blk', pairs)  11.6 us
    pallas_call x6, Pallas kernels, local_call(): pl.pallas_call(body, out_shape=tuple((jax.ShapeDtypeStruct(shape, kind) f...  10.2 us
    all_to_all x1, starting transfers between devices, per_device(): tiles = lax.all_to_all(joined(total, from_other), 'layer', 0, 0, tiled=True)  7.48 us
    all_to_all x1, waiting for transfers between devices, per_device(): tiles = lax.all_to_all(joined(total, from_other), 'layer', 0, 0, tiled=True)  4.38 us
    ppermute x9, waiting for transfers between devices, permuted(): return lax.ppermute(value, 'blk', pairs)  1.95 us
  transfers between devices with their start and end apart: 10, of which 3 were waited for; matrix products, arithmetic and copies ran while one was open for 0% of the time, Pallas kernels for 17%

profile of v5, /device:TPU:0, one launch (start us, length us, event | category | flops | bytes accessed | tf_op | source)
XLA Modules:
  0.0 36.3 jit_solution(3898443138669641495)
XLA Ops:
  0.0 1.2 %shard_map.46 = (f32[1536,128]{1,0:T(8,128)S(1)}, f32[192,128]{1,0:T(8,128)S(1)}, f32[64,128]{1,0:T(8,128)S(1)}) custom-call(f32[1024,128]{1,0:T(8,128)} %points_hbm.1, f32[64,1024]{1,0:T(8,128)} %bitcast.5, f32[1,128]{1,0:T(1,128)} %bitcast.6, f32[1,128]{1,0:T(1,128)} %bitcast.7), custom_call_target="tpu_custom_call" | custom-call | bytes 1048576 | tf_op jit(solution)/shard_map/pallas_call | solution.py:66
  1.2 0.1 collective-permute-start
  1.3 4.1 %collective-permute-start.1 = (f32[192,128]{1,0:T(8,128)S(1)}, f32[192,128]{1,0:T(8,128)S(1)}, u32[]{:S(2)}, u32[]{:S(2)}) collective-permute-start(f32[192,128]{1,0:T(8,128)S(1)} %get-tuple-element.26.piece), channel_id=1, source_target_pairs={{0,112},{8,120},{16,0},{24,8},{32,16},{40,24},{48,32},{56,40},{64,... | collective-permute-start | bytes 294920 | tf_op jit(solution)/shard_map/ppermute | solution.py:24
  5.4 0.6 %collective-permute-start.2 = (f32[192,128]{1,0:T(8,128)S(1)}, f32[192,128]{1,0:T(8,128)S(1)}, u32[]{:S(2)}, u32[]{:S(2)}) collective-permute-start(f32[192,128]{1,0:T(8,128)S(1)} %get-tuple-element.26.piece), channel_id=1, source_target_pairs={{0,96},{8,104},{16,112},{24,120},{32,0},{40,8},{48,16},{56,24},{64... | collective-permute-start | bytes 294920 | tf_op jit(solution)/shard_map/ppermute | solution.py:24
  6.0 0.0 collective-permute-start.3
  6.1 0.0 collective-permute-done.other_packed
  6.1 2.2 %shard_map.47 = (f32[1024,128]{1,0:T(8,128)S(1)}, bf16[1024,768]{1,0:T(8,128)(2,1)S(1)}, f32[1024,128]{1,0:T(8,128)S(1)}, bf16[128,1024]{1,0:T(8,128)(2,1)S(1)},...) custom-call(f32[1536,128]{1,0:T(8,128)S(1)} %get-tuple-element.25.pa, ...), custom_call_target="tpu_custom_call" | custom-call | flops 671088640 | bytes 1048576 | tf_op jit(solution)/shard_map/pallas_call | solution.py:66
  8.3 1.7 %collective-permute-start.4 = (f32[192,128]{1,0:T(8,128)S(1)}, f32[192,128]{1,0:T(8,128)S(1)}, u32[]{:S(2)}, u32[]{:S(2)}) collective-permute-start(f32[192,128]{1,0:T(8,128)S(1)} %get-tuple-element.37), channel_id=1, source_target_pairs={{0,64},{8,72},{16,80},{24,88},{32,96},{40,104},{48,112},{56,120},{... | collective-permute-start | bytes 294920 | tf_op jit(solution)/shard_map/ppermute | solution.py:24
  9.9 0.0 collective-permute-done.1.refs_8_
  9.9 1.8 %collective-permute-done.2.refs_9_ = f32[192,128]{1,0:T(8,128)S(1)} collective-permute-done((f32[192,128]{1,0:T(8,128)S(1)}, f32[192,128]{1,0:T(8,128)S(1)}, u32[]{:S(2)}, u32[]{:S(2)}) %collective-permute-start.2) | collective-permute-done | bytes 98336 | tf_op jit(solution)/shard_map/ppermute | solution.py:24
  11.7 2.7 %shard_map.48 = (f32[1024,128]{1,0:T(8,128)S(1)}, f32[1024,128]{1,0:T(8,128)S(1)}, f32[64,128]{1,0:T(8,128)S(1)}, f32[64,128]{1,0:T(8,128)S(1)}) custom-call(f32[1024,128]{1,0:T(8,128)S(1)} %get-tuple-element.27.refs_0_, bf16[1024,768]{1,0:T(8,128)(2,1)S(1)} %get-tuple-element.28.refs_1_, f32[1024,128]{1,0:T(8,128)S(1)} %get-tuple-element.29.refs_2_, ...), custom_call_target="tpu_custom_call" | custom-call | flops 1342177280 | bytes 1048576 | tf_op jit(solution)/shard_map/pallas_call | solution.py:66
  14.4 0.0 collective-permute-done.3.refs_4_.refs_5_
  14.4 0.0 collective-permute-done.4.refs_5_
  14.4 1.8 %shard_map.49 = (f32[8,64,128]{2,1,0:T(8,128)S(1)}, f32[128,128]{1,0:T(8,128)S(1)}) custom-call(f32[1024,128]{1,0:T(8,128)S(1)} %get-tuple-element.36.refs_0_, bf16[1024,768]{1,0:T(8,128)(2,1)S(1)} %get-tuple-element.32.refs_5_.refs_1_, f32[1024,128]{1,0:T(8,128)S(1)} %get-tuple-element.33.refs_6_.refs_2_, ...), custom_call_target="tpu_custom_call" | custom-call | flops 671088640 | bytes 1048576 | tf_op jit(solution)/shard_map/pallas_call | solution.py:66
  16.3 0.1 collective-permute-start.5
  16.4 1.4 %shard_map.50 = (f32[1024,128]{1,0:T(8,128)S(1)}, f32[64,128]{1,0:T(8,128)S(1)}) custom-call(f32[1024,128]{1,0:T(8,128)S(1)} %get-tuple-element.35.refs_0_, bf16[1024,768]{1,0:T(8,128)(2,1)S(1)} %get-tuple-element.28.refs_1_, f32[1024,128]{1,0:T(8,128)S(1)} %get-tuple-element.29.refs_2_, bf16[128,1024]{1,0:T(8,128)(2,1)S(1)} %get-tuple-element.30.refs_3_, ...), custom_call_target="tpu_custom_call" | custom-call | flops 335544320 | bytes 1048576 | tf_op jit(solution)/shard_map/pallas_call | solution.py:66
  17.8 0.1 collective-permute-done.5.from_other
  17.9 0.9 %shard_map.51 = f32[8,64,128]{2,1,0:T(8,128)} custom-call(f32[1024,128]{1,0:T(8,128)S(1)} %get-tuple-element.39.total, f32[8,64,128]{2,1,0:T(8,128)S(1)} %collective-permute-done.5.from_other), custom_call_target="tpu_custom_call" | custom-call | bytes 1048576 | tf_op jit(solution)/shard_map/pallas_call | solution.py:66
  18.8 7.5 %all-to-all-start = ((f32[8,64,128]{2,1,0:T(8,128)}), f32[8,64,128]{2,1,0:T(8,128)S(1)}, u32[]{:S(2)}, u32[]{:S(2)}) async-start(f32[8,64,128]{2,1,0:T(8,128)} %shard_map.51), calls=%async_computation | async-start | bytes 524288 | tf_op jit(solution)/shard_map/all_to_all | solution.py:306
  26.3 1.0 %collective-permute-start.6 = (f32[64,128]{1,0:T(8,128)S(1)}, f32[64,128]{1,0:T(8,128)S(1)}, u32[]{:S(2)}, u32[]{:S(2)}) collective-permute-start(f32[64,128]{1,0:T(8,128)S(1)} %get-tuple-element.41), channel_id=1, source_target_pairs={{0,16},{8,24},{16,32},{24,40},{32,48},{40,56},{48,64},{56,72},{64,... | collective-permute-start | bytes 98312 | tf_op jit(solution)/shard_map/ppermute | solution.py:24
  27.3 2.9 %collective-permute-start.7 = (f32[64,128]{1,0:T(8,128)S(1)}, f32[64,128]{1,0:T(8,128)S(1)}, u32[]{:S(2)}, u32[]{:S(2)}) collective-permute-start(f32[64,128]{1,0:T(8,128)S(1)} %get-tuple-element.42), channel_id=1, source_target_pairs={{0,32},{8,40},{16,48},{24,56},{32,64},{40,72},{48,80},{56,88},{64,... | collective-permute-start | bytes 98312 | tf_op jit(solution)/shard_map/ppermute | solution.py:24
  30.2 1.1 %collective-permute-start.8 = (f32[64,128]{1,0:T(8,128)S(1)}, f32[64,128]{1,0:T(8,128)S(1)}, u32[]{:S(2)}, u32[]{:S(2)}) collective-permute-start(f32[64,128]{1,0:T(8,128)S(1)} %get-tuple-element.43), channel_id=1, source_target_pairs={{0,80},{8,88},{16,96},{24,104},{32,112},{40,120},{48,0},{56,8},{64... | collective-permute-start | bytes 98312 | tf_op jit(solution)/shard_map/ppermute | solution.py:24
  31.3 4.4 %all-to-all-done = f32[8,64,128]{2,1,0:T(8,128)S(1)} async-done(((f32[8,64,128]{2,1,0:T(8,128)}), f32[8,64,128]{2,1,0:T(8,128)S(1)}, u32[]{:S(2)}, u32[]{:S(2)}) %all-to-all-start) | async-done | bytes 262176 | tf_op jit(solution)/shard_map/all_to_all | solution.py:306
  35.7 0.0 collective-permute-done.6
  35.7 0.0 collective-permute-done.7
  35.7 0.0 collective-permute-done.8
  35.7 0.6 %add_bitcast_fusion = f32[128,64]{0,1:T(8,128)} fusion(f32[64,128]{1,0:T(8,128)S(1)} %get-tuple-element.44, f32[64,128]{1,0:T(8,128)S(1)} %reduce_sum.9, f32[64,128]{1,0:T(8,128)S(1)} %collective-permute-done.8, f32[64,128]{1,0:T(8,128)S(1)} %collective-permute-done.6, f32[64,128]{1,0:T(8,128)S(1)} %collective-permute-done.7), kind=kLoop, calls=%fused_computation | loop fusion | flops 40960 | bytes 196608 | tf_op jit(solution)/shard_map/transpose | solution.py:311
  (1 shorter events, 0.0 us)
Async XLA Ops:
  1.2 4.9 %collective-permute-start = (f32[1536,128]{1,0:T(8,128)S(1)}, f32[1536,128]{1,0:T(8,128)S(1)}, u32[]{:S(2)}, u32[]{:S(2)}) collective-permute-start(f32[1536,128]{1,0:T(8,128)S(1)} %get-tuple-element.25.packed), channel_id=1, source_target_pairs={{0,8},{8,0},{16,24},{24,16},{32,40},{40,32},{48,56},{56,48},{64,72... | collective-permute-start | bytes 2359304 | tf_op jit(solution)/shard_map/ppermute | solution.py:24
  1.3 8.6 %collective-permute-start.1 = (f32[192,128]{1,0:T(8,128)S(1)}, f32[192,128]{1,0:T(8,128)S(1)}, u32[]{:S(2)}, u32[]{:S(2)}) collective-permute-start(f32[192,128]{1,0:T(8,128)S(1)} %get-tuple-element.26.piece), channel_id=1, source_target_pairs={{0,112},{8,120},{16,0},{24,8},{32,16},{40,24},{48,32},{56,40},{64,... | collective-permute-start | bytes 294920 | tf_op jit(solution)/shard_map/ppermute | solution.py:24
  5.4 6.4 %collective-permute-start.2 = (f32[192,128]{1,0:T(8,128)S(1)}, f32[192,128]{1,0:T(8,128)S(1)}, u32[]{:S(2)}, u32[]{:S(2)}) collective-permute-start(f32[192,128]{1,0:T(8,128)S(1)} %get-tuple-element.26.piece), channel_id=1, source_target_pairs={{0,96},{8,104},{16,112},{24,120},{32,0},{40,8},{48,16},{56,24},{64... | collective-permute-start | bytes 294920 | tf_op jit(solution)/shard_map/ppermute | solution.py:24
  6.0 8.4 %collective-permute-start.3 = (f32[192,128]{1,0:T(8,128)S(1)}, f32[192,128]{1,0:T(8,128)S(1)}, u32[]{:S(2)}, u32[]{:S(2)}) collective-permute-start(f32[192,128]{1,0:T(8,128)S(1)} %get-tuple-element.26.piece), channel_id=1, source_target_pairs={{0,48},{8,56},{16,64},{24,72},{32,80},{40,88},{48,96},{56,104},{64... | collective-permute-start | bytes 294920 | tf_op jit(solution)/shard_map/ppermute | solution.py:24
  8.3 6.2 %collective-permute-start.4 = (f32[192,128]{1,0:T(8,128)S(1)}, f32[192,128]{1,0:T(8,128)S(1)}, u32[]{:S(2)}, u32[]{:S(2)}) collective-permute-start(f32[192,128]{1,0:T(8,128)S(1)} %get-tuple-element.37), channel_id=1, source_target_pairs={{0,64},{8,72},{16,80},{24,88},{32,96},{40,104},{48,112},{56,120},{... | collective-permute-start | bytes 294920 | tf_op jit(solution)/shard_map/ppermute | solution.py:24
  16.3 1.6 %collective-permute-start.5 = (f32[8,64,128]{2,1,0:T(8,128)S(1)}, f32[8,64,128]{2,1,0:T(8,128)S(1)}, u32[]{:S(2)}, u32[]{:S(2)}) collective-permute-start(f32[8,64,128]{2,1,0:T(8,128)S(1)} %get-tuple-element.40), channel_id=1, source_target_pairs={{0,8},{8,0},{16,24},{24,16},{32,40},{40,32},{48,56},{56,48},{64,72... | collective-permute-start | bytes 786440 | tf_op jit(solution)/shard_map/ppermute | solution.py:24
  18.8 16.9 %all-to-all-start = ((f32[8,64,128]{2,1,0:T(8,128)}), f32[8,64,128]{2,1,0:T(8,128)S(1)}, u32[]{:S(2)}, u32[]{:S(2)}) async-start(f32[8,64,128]{2,1,0:T(8,128)} %shard_map.51), calls=%async_computation | async-start | bytes 524288 | tf_op jit(solution)/shard_map/all_to_all | solution.py:306
  26.3 9.4 %collective-permute-start.6 = (f32[64,128]{1,0:T(8,128)S(1)}, f32[64,128]{1,0:T(8,128)S(1)}, u32[]{:S(2)}, u32[]{:S(2)}) collective-permute-start(f32[64,128]{1,0:T(8,128)S(1)} %get-tuple-element.41), channel_id=1, source_target_pairs={{0,16},{8,24},{16,32},{24,40},{32,48},{40,56},{48,64},{56,72},{64,... | collective-permute-start | bytes 98312 | tf_op jit(solution)/shard_map/ppermute | solution.py:24
  27.3 8.4 %collective-permute-start.7 = (f32[64,128]{1,0:T(8,128)S(1)}, f32[64,128]{1,0:T(8,128)S(1)}, u32[]{:S(2)}, u32[]{:S(2)}) collective-permute-start(f32[64,128]{1,0:T(8,128)S(1)} %get-tuple-element.42), channel_id=1, source_target_pairs={{0,32},{8,40},{16,48},{24,56},{32,64},{40,72},{48,80},{56,88},{64,... | collective-permute-start | bytes 98312 | tf_op jit(solution)/shard_map/ppermute | solution.py:24
  30.2 5.5 %collective-permute-start.8 = (f32[64,128]{1,0:T(8,128)S(1)}, f32[64,128]{1,0:T(8,128)S(1)}, u32[]{:S(2)}, u32[]{:S(2)}) collective-permute-start(f32[64,128]{1,0:T(8,128)S(1)} %get-tuple-element.43), channel_id=1, source_target_pairs={{0,80},{8,88},{16,96},{24,104},{32,112},{40,120},{48,0},{56,8},{64... | collective-permute-start | bytes 98312 | tf_op jit(solution)/shard_map/ppermute | solution.py:24

commit v6 on v5

--- a/solution.py
+++ b/solution.py
@@ -211,71 +211,66 @@
     )
 
 
-def first_tiles(packed, other_packed, piece):
+def first_sides(packed, other_packed, piece):
     feats = packed.shape[1]
     columns = piece.shape[0] - LANES
     rows = packed.shape[0] * LANES // (LANES + columns)
 
-    def body(packed, other_packed, piece, *refs):
-        own, other, again_ref = refs[:4], refs[4:8], refs[8]
-        again_ref[...] = piece[...]
-        loaded = load_right((piece,))
-        for source, (total, *side) in ((packed, own), (other_packed, other)):
-            load_left(source, *side)
-            tile_products(side, loaded, None, total, None, 0)
-
-    side = side_shapes(rows, feats, columns)
-    outs = side + side + ((piece.shape, F32),)
-    macs = macs_of(2 * rows, feats, columns, 1)
-    out = local_call(body, outs, (packed, other_packed, piece), macs=macs)
-    return out[:4], out[4:8], out[8]
-
-
-def shared_tiles(own, other, pieces):
-    rows, columns = own[1].shape[0], own[3].shape[0] // 2
+    def body(packed, other_packed, *refs):
+        load_left(packed, *refs[:3])
+        load_left(other_packed, *refs[3:])
+
+    side = side_shapes(rows, feats, columns)[1:]
+    out = local_call(body, side + side, (packed, other_packed))
+    return out[:3], out[3:]
+
+
+def near_tiles(own, other, piece, arrived):
+    rows, columns = own[0].shape[0], own[2].shape[0] // 2
 
     def body(*refs):
-        (own_in, *own_side), (other_in, *other_side) = refs[:4], refs[4:8]
-        arrived, total, other_total, first_ref, second_ref = refs[8:10], *refs[10:]
-        loaded = load_right(arrived)
-        mirrored = tile_products(own_side, loaded, own_in, total, None, 2)
-        mirrored = tile_products(other_side, loaded, other_in, other_total, mirrored, 2)
-        mirrored = folded(mirrored)
-        first_ref[...] = mirrored[:, :LANES]
-        second_ref[...] = mirrored[:, LANES:]
+        own_side, other_side = refs[:3], refs[3:6]
+        piece, arrived, total, other_total, back_ref = refs[6:]
+        loaded = load_right((arrived, piece))
+        mirrored = tile_products(own_side, loaded, None, total, None, 1)
+        mirrored = tile_products(other_side, loaded, None, other_total, mirrored, 1)
+        back_ref[...] = folded(mirrored)
 
     total_shape = ((rows, 2 * columns), F32)
-    back = ((columns, LANES), F32)
-    outs = (total_shape, total_shape, back, back)
-    macs = macs_of(2 * rows, own[1].shape[1] // 6, columns, 2)
-    return local_call(body, outs, (*own, *other, *pieces), macs=macs)
+    outs = (total_shape, total_shape, ((columns, LANES), F32))
+    macs = macs_of(2 * rows, own[0].shape[1] // 6, columns, 2)
+    return local_call(body, outs, (*own, *other, piece, arrived), macs=macs)
 
 
 def other_tiles(side, pieces):
     rows, columns = side[1].shape[0], side[3].shape[0] // 2
 
     def body(*refs):
-        (total_in, *side), arrived, turned_ref, part_ref, total = refs[:4], refs[4:6], *refs[6:]
-        part_ref[...] = tile_products(side, load_right(arrived), total_in, total, None, 1)
+        (total_in, *side), arrived, turned_ref, part_ref, total = refs[:4], refs[4:7], *refs[7:]
+        part_ref[...] = tile_products(side, load_right(arrived), total_in, total, None, 2)
         write_turned(total, turned_ref)
 
-    outs = (((rows // LANES, columns, LANES), F32), ((2 * columns, LANES), F32))
+    outs = (((rows // LANES, columns, LANES), F32), ((2 * columns, 2 * LANES), F32))
     scratch = (pltpu.VMEM((rows, 2 * columns), F32),)
     macs = macs_of(rows, side[1].shape[1] // 6, columns, 2)
     return local_call(body, outs, (*side, *pieces), scratch, macs=macs)
 
 
-def own_tiles(side, part, piece):
+def own_tiles(side, part, pieces):
     rows, columns = side[1].shape[0], side[3].shape[0] // 2
 
     def body(*refs):
-        (total_in, *side), part_ref, arrived, total, back_ref = refs[:4], *refs[4:]
-        loaded = load_right((arrived,))
-        back_ref[...] = folded(tile_products(side, loaded, total_in, total, part_ref[...], 1))
-
-    outs = (((rows, 2 * columns), F32), ((columns, LANES), F32))
-    macs = macs_of(rows, side[1].shape[1] // 6, columns, 1)
-    return local_call(body, outs, (*side, part, piece), macs=macs)
+        (total_in, *side), part_ref, arrived = refs[:4], refs[4], refs[5:7]
+        total, first_ref, second_ref = refs[7:]
+        loaded = load_right(arrived)
+        mirrored = folded(tile_products(side, loaded, total_in, total, part_ref[...], 2))
+        first_ref[...] = mirrored[:, :LANES]
+        second_ref[...] = mirrored[:, LANES:]
+
+    back = ((columns, LANES), F32)
+    outs = (((rows, 2 * columns), F32), back, back)
+    macs = macs_of(rows, side[1].shape[1] // 6, columns, 3)
+    return local_call(body, outs, (*side, part, *pieces), macs=macs)
 
 
 def joined(total, from_other):
@@ -295,14 +290,13 @@
     other_packed = swapped(packed)
     middle_piece = stepped(piece, middle)
     far_piece = stepped(piece, far)
-    own, other, piece = first_tiles(packed, other_packed, piece)
     ring_piece = across_the_ring(piece)
-    total, other_total, near_back, middle_back = shared_tiles(
-        own, other, (near_piece, middle_piece)
-    )
-    for_other, part = other_tiles((other_total, *other[1:]), (far_piece, ring_piece))
+    own, other = first_sides(packed, other_packed, piece)
+    total, other_total, near_back = near_tiles(own, other, piece, near_piece)
+    pieces = (middle_piece, far_piece)
+    for_other, part = other_tiles((other_total, *other), (*pieces, ring_piece))
     from_other = swapped(for_other)
-    total, far_back = own_tiles((total, *own[1:]), part, far_piece)
+    total, middle_back, far_back = own_tiles((total, *own), part, pieces)
     tiles = lax.all_to_all(joined(total, from_other), "layer", 0, 0, tiled=True)
     returned = (
         stepped(near_back, -near) + stepped(middle_back, -middle) + stepped(far_back, -far)

time: 36.8 us -> 36.5 us (level)
  Pallas kernels: 10.2 us -> 8.85 us
  waiting for transfers between devices: 6.32 us -> 7.43 us
    pallas_call x6, Pallas kernels: 10.2 us -> 8.85 us  [local_call(): pl.pallas_call(body, out_shape=tuple((jax.ShapeDtypeStruct(shape, kind) f...]
    all_to_all x1, waiting for transfers between devices: 4.38 us -> 4.94 us  [per_device(): tiles = lax.all_to_all(joined(total, from_other), 'layer', 0, 0, tiled=True)]
    ppermute x9, waiting for transfers between devices: 1.95 us -> 2.49 us  [permuted(): return lax.ppermute(value, 'blk', pairs)]
    ppermute x9, starting transfers between devices: 11.6 us -> 11.2 us  [permuted(): return lax.ppermute(value, 'blk', pairs)]
  transfers between devices with their start and end apart: 10 -> 10, of which waited for: 3 -> 6; matrix products, arithmetic and copies ran while one was open for 0% -> 0% of each run, Pallas kernels for 17% -> 13%
where the time goes in v6:
time: 36.5 us; the launch traced here: 36 us
  starting transfers between devices  19 us (52%)
  Pallas kernels  8.85 us (24%)
  waiting for transfers between devices  7.43 us (20%)
  other arithmetic  0.65 us (2%)
    ppermute x9, starting transfers between devices, permuted(): return lax.ppermute(value, 'blk', pairs)  11.2 us
    pallas_call x6, Pallas kernels, local_call(): pl.pallas_call(body, out_shape=tuple((jax.ShapeDtypeStruct(shape, kind) f...  8.85 us
    all_to_all x1, starting transfers between devices, per_device(): tiles = lax.all_to_all(joined(total, from_other), 'layer', 0, 0, tiled=True)  7.78 us
    all_to_all x1, waiting for transfers between devices, per_device(): tiles = lax.all_to_all(joined(total, from_other), 'layer', 0, 0, tiled=True)  4.94 us
    ppermute x9, waiting for transfers between devices, permuted(): return lax.ppermute(value, 'blk', pairs)  2.49 us
  transfers between devices with their start and end apart: 10, of which 6 were waited for; matrix products, arithmetic and copies ran while one was open for 0% of the time, Pallas kernels for 13%

profile of v6, /device:TPU:0, one launch (start us, length us, event | category | flops | bytes accessed | tf_op | source)
XLA Modules:
  0.0 36.0 jit_solution(1155713765932126503)
XLA Ops:
  0.0 1.2 %shard_map.46 = (f32[1536,128]{1,0:T(8,128)S(1)}, f32[192,128]{1,0:T(8,128)S(1)}, f32[64,128]{1,0:T(8,128)S(1)}) custom-call(f32[1024,128]{1,0:T(8,128)} %points_hbm.1, f32[64,1024]{1,0:T(8,128)} %bitcast.5, f32[1,128]{1,0:T(1,128)} %bitcast.6, f32[1,128]{1,0:T(1,128)} %bitcast.7), custom_call_target="tpu_custom_call" | custom-call | bytes 1048576 | tf_op jit(solution)/shard_map/pallas_call | solution.py:66
  1.2 0.1 collective-permute-start
  1.3 4.1 %collective-permute-start.1 = (f32[192,128]{1,0:T(8,128)S(1)}, f32[192,128]{1,0:T(8,128)S(1)}, u32[]{:S(2)}, u32[]{:S(2)}) collective-permute-start(f32[192,128]{1,0:T(8,128)S(1)} %get-tuple-element.29.refs_6_), channel_id=1, source_target_pairs={{0,112},{8,120},{16,0},{24,8},{32,16},{40,24},{48,32},{56,40},{64,... | collective-permute-start | bytes 294920 | tf_op jit(solution)/shard_map/ppermute | solution.py:24
  5.4 0.6 %collective-permute-start.2 = (f32[192,128]{1,0:T(8,128)S(1)}, f32[192,128]{1,0:T(8,128)S(1)}, u32[]{:S(2)}, u32[]{:S(2)}) collective-permute-start(f32[192,128]{1,0:T(8,128)S(1)} %get-tuple-element.29.refs_6_), channel_id=1, source_target_pairs={{0,96},{8,104},{16,112},{24,120},{32,0},{40,8},{48,16},{56,24},{64... | collective-permute-start | bytes 294920 | tf_op jit(solution)/shard_map/ppermute | solution.py:24
  6.0 0.0 collective-permute-start.3
  6.1 1.6 %collective-permute-start.4 = (f32[192,128]{1,0:T(8,128)S(1)}, f32[192,128]{1,0:T(8,128)S(1)}, u32[]{:S(2)}, u32[]{:S(2)}) collective-permute-start(f32[192,128]{1,0:T(8,128)S(1)} %get-tuple-element.29.refs_6_), channel_id=1, source_target_pairs={{0,64},{8,72},{16,80},{24,88},{32,96},{40,104},{48,112},{56,120},{... | collective-permute-start | bytes 294920 | tf_op jit(solution)/shard_map/ppermute | solution.py:24
  7.6 0.0 collective-permute-done.other_packed
  7.6 0.6 %shard_map.47 = (bf16[1024,768]{1,0:T(8,128)(2,1)S(1)}, f32[1024,128]{1,0:T(8,128)S(1)}, bf16[128,1024]{1,0:T(8,128)(2,1)S(1)}, bf16[1024,768]{1,0:T(8,128)(2,1)...) custom-call(f32[1536,128]{1,0:T(8,128)S(1)} %get-tuple-element.22.packed, ...), custom_call_target="tpu_custom_call" | custom-call | bytes 1048576 | tf_op jit(solution)/shard_map/pallas_call | solution.py:66
  8.2 0.3 collective-permute-done.1.refs_7_
  8.5 2.7 %shard_map.48 = (f32[1024,128]{1,0:T(8,128)S(1)}, f32[1024,128]{1,0:T(8,128)S(1)}, f32[64,128]{1,0:T(8,128)S(1)}) custom-call(bf16[1024,768]{1,0:T(8,128)(2,1)S(1)} %get-tuple-element.23.refs_0_.refs_1_, f32[1024,128]{1,0:T(8,128)S(1)} %get-tuple-element.24.refs_1_.refs_2_, bf16[128,1024]{1,0:T(8,128)(2,1)S(1)} %get-tuple-element.25.refs_2_.refs_3_, ...), custom_call_target="tpu_custom_call" | custom-call | flops 1342177280 | bytes 1048576 | tf_op jit(solution)/shard_map/pallas_call | solution.py:66
  11.2 0.5 %collective-permute-done.2.refs_4_.refs_5_ = f32[192,128]{1,0:T(8,128)S(1)} collective-permute-done((f32[192,128]{1,0:T(8,128)S(1)}, f32[192,128]{1,0:T(8,128)S(1)}, u32[]{:S(2)}, u32[]{:S(2)}) %collective-permute-start.2) | collective-permute-done | bytes 98336 | tf_op jit(solution)/shard_map/ppermute | solution.py:24
  11.7 1.3 %collective-permute-done.3.refs_5_.refs_6_ = f32[192,128]{1,0:T(8,128)S(1)} collective-permute-done((f32[192,128]{1,0:T(8,128)S(1)}, f32[192,128]{1,0:T(8,128)S(1)}, u32[]{:S(2)}, u32[]{:S(2)}) %collective-permute-start.3) | collective-permute-done | bytes 98336 | tf_op jit(solution)/shard_map/ppermute | solution.py:24
  13.1 0.2 collective-permute-done.4.refs_6_
  13.2 2.1 %shard_map.49 = (f32[8,64,128]{2,1,0:T(8,128)S(1)}, f32[128,256]{1,0:T(8,128)S(1)}) custom-call(f32[1024,128]{1,0:T(8,128)S(1)} %get-tuple-element.31.refs_0_, bf16[1024,768]{1,0:T(8,128)(2,1)S(1)} %get-tuple-element.26.refs_3_.refs_1_, f32[1024,128]{1,0:T(8,128)S(1)} %get-tuple-element.27.refs_4_.refs_2_, ...), custom_call_target="tpu_custom_call" | custom-call | flops 671088640 | bytes 1048576 | tf_op jit(solution)/shard_map/pallas_call | solution.py:66
  15.4 0.1 collective-permute-start.5
  15.5 1.4 %shard_map.50 = (f32[1024,128]{1,0:T(8,128)S(1)}, f32[64,128]{1,0:T(8,128)S(1)}, f32[64,128]{1,0:T(8,128)S(1)}) custom-call(f32[1024,128]{1,0:T(8,128)S(1)} %get-tuple-element.30.refs_0_, bf16[1024,768]{1,0:T(8,128)(2,1)S(1)} %get-tuple-element.23.refs_0_.refs_1_, f32[1024,128]{1,0:T(8,128)S(1)} %get-tuple-element.24.refs_1_.refs_2_, ...), custom_call_target="tpu_custom_call" | custom-call | flops 1006632960 | bytes 1048576 | tf_op jit(solution)/shard_map/pallas_call | solution.py:66
  16.9 0.2 collective-permute-done.5.from_other
  17.0 0.9 %shard_map.51 = f32[8,64,128]{2,1,0:T(8,128)} custom-call(f32[1024,128]{1,0:T(8,128)S(1)} %get-tuple-element.33.total, f32[8,64,128]{2,1,0:T(8,128)S(1)} %collective-permute-done.5.from_other), custom_call_target="tpu_custom_call" | custom-call | bytes 1048576 | tf_op jit(solution)/shard_map/pallas_call | solution.py:66
  17.9 7.8 %all-to-all-start = ((f32[8,64,128]{2,1,0:T(8,128)}), f32[8,64,128]{2,1,0:T(8,128)S(1)}, u32[]{:S(2)}, u32[]{:S(2)}) async-start(f32[8,64,128]{2,1,0:T(8,128)} %shard_map.51), calls=%async_computation | async-start | bytes 524288 | tf_op jit(solution)/shard_map/all_to_all | solution.py:300
  25.7 1.7 %collective-permute-start.8 = (f32[64,128]{1,0:T(8,128)S(1)}, f32[64,128]{1,0:T(8,128)S(1)}, u32[]{:S(2)}, u32[]{:S(2)}) collective-permute-start(f32[64,128]{1,0:T(8,128)S(1)} %get-tuple-element.37), channel_id=1, source_target_pairs={{0,80},{8,88},{16,96},{24,104},{32,112},{40,120},{48,0},{56,8},{64... | collective-permute-start | bytes 98312 | tf_op jit(solution)/shard_map/ppermute | solution.py:24
  27.4 0.1 collective-permute-start.6
  27.5 2.9 %collective-permute-start.7 = (f32[64,128]{1,0:T(8,128)S(1)}, f32[64,128]{1,0:T(8,128)S(1)}, u32[]{:S(2)}, u32[]{:S(2)}) collective-permute-start(f32[64,128]{1,0:T(8,128)S(1)} %get-tuple-element.36), channel_id=1, source_target_pairs={{0,32},{8,40},{16,48},{24,56},{32,64},{40,72},{48,80},{56,88},{64,... | collective-permute-start | bytes 98312 | tf_op jit(solution)/shard_map/ppermute | solution.py:24
  30.4 4.9 %all-to-all-done = f32[8,64,128]{2,1,0:T(8,128)S(1)} async-done(((f32[8,64,128]{2,1,0:T(8,128)}), f32[8,64,128]{2,1,0:T(8,128)S(1)}, u32[]{:S(2)}, u32[]{:S(2)}) %all-to-all-start) | async-done | bytes 262176 | tf_op jit(solution)/shard_map/all_to_all | solution.py:300
  35.3 0.0 collective-permute-done.8
  35.4 0.0 collective-permute-done.6
  35.4 0.0 collective-permute-done.7
  35.4 0.6 %add_bitcast_fusion = f32[128,64]{0,1:T(8,128)} fusion(f32[64,128]{1,0:T(8,128)S(1)} %get-tuple-element.38, f32[64,128]{1,0:T(8,128)S(1)} %reduce_sum.9, f32[64,128]{1,0:T(8,128)S(1)} %collective-permute-done.8, f32[64,128]{1,0:T(8,128)S(1)} %collective-permute-done.6, f32[64,128]{1,0:T(8,128)S(1)} %collective-permute-done.7), kind=kLoop, calls=%fused_computation | loop fusion | flops 40960 | bytes 196608 | tf_op jit(solution)/shard_map/transpose | solution.py:305
  (1 shorter events, 0.0 us)
Async XLA Ops:
  1.2 6.4 %collective-permute-start = (f32[1536,128]{1,0:T(8,128)S(1)}, f32[1536,128]{1,0:T(8,128)S(1)}, u32[]{:S(2)}, u32[]{:S(2)}) collective-permute-start(f32[1536,128]{1,0:T(8,128)S(1)} %get-tuple-element.22.packed), channel_id=1, source_target_pairs={{0,8},{8,0},{16,24},{24,16},{32,40},{40,32},{48,56},{56,48},{64,72... | collective-permute-start | bytes 2359304 | tf_op jit(solution)/shard_map/ppermute | solution.py:24
  1.3 7.2 %collective-permute-start.1 = (f32[192,128]{1,0:T(8,128)S(1)}, f32[192,128]{1,0:T(8,128)S(1)}, u32[]{:S(2)}, u32[]{:S(2)}) collective-permute-start(f32[192,128]{1,0:T(8,128)S(1)} %get-tuple-element.29.refs_6_), channel_id=1, source_target_pairs={{0,112},{8,120},{16,0},{24,8},{32,16},{40,24},{48,32},{56,40},{64,... | collective-permute-start | bytes 294920 | tf_op jit(solution)/shard_map/ppermute | solution.py:24
  5.4 6.4 %collective-permute-start.2 = (f32[192,128]{1,0:T(8,128)S(1)}, f32[192,128]{1,0:T(8,128)S(1)}, u32[]{:S(2)}, u32[]{:S(2)}) collective-permute-start(f32[192,128]{1,0:T(8,128)S(1)} %get-tuple-element.29.refs_6_), channel_id=1, source_target_pairs={{0,96},{8,104},{16,112},{24,120},{32,0},{40,8},{48,16},{56,24},{64... | collective-permute-start | bytes 294920 | tf_op jit(solution)/shard_map/ppermute | solution.py:24
  6.0 7.0 %collective-permute-start.3 = (f32[192,128]{1,0:T(8,128)S(1)}, f32[192,128]{1,0:T(8,128)S(1)}, u32[]{:S(2)}, u32[]{:S(2)}) collective-permute-start(f32[192,128]{1,0:T(8,128)S(1)} %get-tuple-element.29.refs_6_), channel_id=1, source_target_pairs={{0,48},{8,56},{16,64},{24,72},{32,80},{40,88},{48,96},{56,104},{64... | collective-permute-start | bytes 294920 | tf_op jit(solution)/shard_map/ppermute | solution.py:24
  6.1 7.2 %collective-permute-start.4 = (f32[192,128]{1,0:T(8,128)S(1)}, f32[192,128]{1,0:T(8,128)S(1)}, u32[]{:S(2)}, u32[]{:S(2)}) collective-permute-start(f32[192,128]{1,0:T(8,128)S(1)} %get-tuple-element.29.refs_6_), channel_id=1, source_target_pairs={{0,64},{8,72},{16,80},{24,88},{32,96},{40,104},{48,112},{56,120},{... | collective-permute-start | bytes 294920 | tf_op jit(solution)/shard_map/ppermute | solution.py:24
  15.4 1.6 %collective-permute-start.5 = (f32[8,64,128]{2,1,0:T(8,128)S(1)}, f32[8,64,128]{2,1,0:T(8,128)S(1)}, u32[]{:S(2)}, u32[]{:S(2)}) collective-permute-start(f32[8,64,128]{2,1,0:T(8,128)S(1)} %get-tuple-element.34), channel_id=1, source_target_pairs={{0,8},{8,0},{16,24},{24,16},{32,40},{40,32},{48,56},{56,48},{64,72... | collective-permute-start | bytes 786440 | tf_op jit(solution)/shard_map/ppermute | solution.py:24
  17.9 17.4 %all-to-all-start = ((f32[8,64,128]{2,1,0:T(8,128)}), f32[8,64,128]{2,1,0:T(8,128)S(1)}, u32[]{:S(2)}, u32[]{:S(2)}) async-start(f32[8,64,128]{2,1,0:T(8,128)} %shard_map.51), calls=%async_computation | async-start | bytes 524288 | tf_op jit(solution)/shard_map/all_to_all | solution.py:300
  25.7 9.7 %collective-permute-start.8 = (f32[64,128]{1,0:T(8,128)S(1)}, f32[64,128]{1,0:T(8,128)S(1)}, u32[]{:S(2)}, u32[]{:S(2)}) collective-permute-start(f32[64,128]{1,0:T(8,128)S(1)} %get-tuple-element.37), channel_id=1, source_target_pairs={{0,80},{8,88},{16,96},{24,104},{32,112},{40,120},{48,0},{56,8},{64... | collective-permute-start | bytes 98312 | tf_op jit(solution)/shard_map/ppermute | solution.py:24
  27.4 8.0 %collective-permute-start.6 = (f32[64,128]{1,0:T(8,128)S(1)}, f32[64,128]{1,0:T(8,128)S(1)}, u32[]{:S(2)}, u32[]{:S(2)}) collective-permute-start(f32[64,128]{1,0:T(8,128)S(1)} %get-tuple-element.35), channel_id=1, source_target_pairs={{0,16},{8,24},{16,32},{24,40},{32,48},{40,56},{48,64},{56,72},{64,... | collective-permute-start | bytes 98312 | tf_op jit(solution)/shard_map/ppermute | solution.py:24
  27.5 7.8 %collective-permute-start.7 = (f32[64,128]{1,0:T(8,128)S(1)}, f32[64,128]{1,0:T(8,128)S(1)}, u32[]{:S(2)}, u32[]{:S(2)}) collective-permute-start(f32[64,128]{1,0:T(8,128)S(1)} %get-tuple-element.36), channel_id=1, source_target_pairs={{0,32},{8,40},{16,48},{24,56},{32,64},{40,72},{48,80},{56,88},{64,... | collective-permute-start | bytes 98312 | tf_op jit(solution)/shard_map/ppermute | solution.py:24

commit v7 on v6

--- a/solution.py
+++ b/solution.py
@@ -15,26 +15,29 @@
 CHUNK = 256
 VMEM_BYTES = 32 * 1024 * 1024
 
-CHIP_STEPS = (-1, -2, 3)
-
-
-def permuted(value, target_of):
-    count = lax.axis_size("blk")
-    pairs = [(block, target_of(block) % count) for block in range(count)]
+NEAR = lambda x, y: (x, y + 1)
+MIDDLE = lambda x, y: (x + 1, y - 1)
+FAR = lambda x, y: (x + (y >= 2), y + 2)
+ACROSS = lambda x, y: (x + 1, y)
+
+
+def permuted(value, pairs, back=False):
+    if back:
+        pairs = [(target, source) for source, target in pairs]
     return lax.ppermute(value, "blk", pairs)
 
 
 def swapped(value):
-    return permuted(value, lambda block: block ^ 1)
-
-
-def stepped(value, chips):
-    return permuted(value, lambda block: block + 2 * chips)
-
-
-def across_the_ring(value):
-    count = lax.axis_size("blk")
-    return permuted(value, lambda block: block + count // 2)
+    return permuted(value, [(block, block ^ 1) for block in range(lax.axis_size("blk"))])
+
+
+def stepped(value, step, back=False):
+    half = lax.axis_size("blk") // 2
+    pairs = []
+    for block in range(2 * half):
+        x, y = step(block // half, block % half // 2)
+        pairs.append((block, x % 2 * half + y % (half // 2) * 2 + block % 2))
+    return permuted(value, pairs, back)
 
 
 def two_parts(x):
@@ -211,9 +214,8 @@
     )
 
 
-def first_sides(packed, other_packed, piece):
+def first_sides(packed, other_packed, columns):
     feats = packed.shape[1]
-    columns = piece.shape[0] - LANES
     rows = packed.shape[0] * LANES // (LANES + columns)
 
     def body(packed, other_packed, *refs):
@@ -242,35 +244,47 @@
     return local_call(body, outs, (*own, *other, piece, arrived), macs=macs)
 
 
+def middle_tile(side, piece):
+    rows, columns = side[1].shape[0], side[3].shape[0] // 2
+
+    def body(*refs):
+        (total_in, *side), arrived, total, part_ref = refs[:4], *refs[4:]
+        part_ref[...] = tile_products(side, load_right((arrived,)), total_in, total, None, 1)
+
+    outs = (((rows, 2 * columns), F32), ((2 * columns, LANES), F32))
+    macs = macs_of(rows, side[1].shape[1] // 6, columns, 1)
+    return local_call(body, outs, (*side, piece), macs=macs)
+
+
 def other_tiles(side, pieces):
     rows, columns = side[1].shape[0], side[3].shape[0] // 2
 
     def body(*refs):
-        (total_in, *side), arrived, turned_ref, part_ref, total = refs[:4], refs[4:7], *refs[7:]
-        part_ref[...] = tile_products(side, load_right(arrived), total_in, total, None, 2)
+        (total_in, *side), arrived, turned_ref, part_ref, total = refs[:4], refs[4:6], *refs[6:]
+        part_ref[...] = tile_products(side, load_right(arrived), total_in, total, None, 1)
         write_turned(total, turned_ref)
 
-    outs = (((rows // LANES, columns, LANES), F32), ((2 * columns, 2 * LANES), F32))
+    outs = (((rows // LANES, columns, LANES), F32), ((2 * columns, LANES), F32))
     scratch = (pltpu.VMEM((rows, 2 * columns), F32),)
     macs = macs_of(rows, side[1].shape[1] // 6, columns, 2)
     return local_call(body, outs, (*side, *pieces), scratch, macs=macs)
 
 
-def own_tiles(side, part, pieces):
+def own_tiles(side, parts, pieces):
     rows, columns = side[1].shape[0], side[3].shape[0] // 2
 
     def body(*refs):
-        (total_in, *side), part_ref, arrived = refs[:4], refs[4], refs[5:7]
-        total, first_ref, second_ref = refs[7:]
-        loaded = load_right(arrived)
-        mirrored = folded(tile_products(side, loaded, total_in, total, part_ref[...], 2))
+        (total_in, *side), parts, arrived = refs[:4], refs[4:6], refs[6:8]
+        total, first_ref, second_ref = refs[8:]
+        begun = side_by_side(parts[0][...], parts[1][...])
+        mirrored = folded(tile_products(side, load_right(arrived), total_in, total, begun, 2))
         first_ref[...] = mirrored[:, :LANES]
         second_ref[...] = mirrored[:, LANES:]
 
     back = ((columns, LANES), F32)
     outs = (((rows, 2 * columns), F32), back, back)
-    macs = macs_of(rows, side[1].shape[1] // 6, columns, 3)
-    return local_call(body, outs, (*side, part, *pieces), macs=macs)
+    macs = macs_of(rows, side[1].shape[1] // 6, columns, 2)
+    return local_call(body, outs, (*side, *parts, *pieces), macs=macs)
 
 
 def joined(total, from_other):
@@ -285,21 +299,21 @@
     layers = lax.axis_size("layer")
     rows = points.shape[0]
     packed, piece, noise_term = prepare(points, inv_scale[None, :], vectors.T, noise[None, :])
-    near, middle, far = CHIP_STEPS
-    near_piece = stepped(piece, near)
+    near_piece = stepped(piece, NEAR)
     other_packed = swapped(packed)
-    middle_piece = stepped(piece, middle)
-    far_piece = stepped(piece, far)
-    ring_piece = across_the_ring(piece)
-    own, other = first_sides(packed, other_packed, piece)
+    middle_piece = stepped(piece, MIDDLE)
+    far_piece = stepped(piece, FAR)
+    ring_piece = stepped(piece, ACROSS)
+    own, other = first_sides(packed, other_packed, vectors.shape[1])
     total, other_total, near_back = near_tiles(own, other, piece, near_piece)
-    pieces = (middle_piece, far_piece)
-    for_other, part = other_tiles((other_total, *other), (*pieces, ring_piece))
+    other_total, middle_part = middle_tile((other_total, *other), middle_piece)
+    for_other, far_part = other_tiles((other_total, *other), (far_piece, ring_piece))
     from_other = swapped(for_other)
-    total, middle_back, far_back = own_tiles((total, *own), part, pieces)
+    parts, pieces = (middle_part, far_part), (middle_piece, far_piece)
+    total, middle_back, far_back = own_tiles((total, *own), parts, pieces)
     tiles = lax.all_to_all(joined(total, from_other), "layer", 0, 0, tiled=True)
     returned = (
-        stepped(near_back, -near) + stepped(middle_back, -middle) + stepped(far_back, -far)
+        stepped(near_back, NEAR, True) + stepped(middle_back, MIDDLE, True) + stepped(far_back, FAR, True)
     )
     normalizer = float(rows * (2 * layers - 1)) ** (-0.5)
     return ((jnp.sum(tiles, axis=0) + returned) * normalizer + noise_term).T

time: 36.5 us -> 36.1 us (0.989)
  waiting for transfers between devices: 7.43 us -> 6 us
  Pallas kernels: 8.85 us -> 9.9 us
    ppermute x9, waiting for transfers between devices: 2.49 us -> 1.07 us  [permuted(): return lax.ppermute(value, 'blk', pairs)]
    pallas_call x6 -> x7, Pallas kernels: 8.85 us -> 9.9 us  [local_call(): pl.pallas_call(body, out_shape=tuple((jax.ShapeDtypeStruct(shape, kind) f...]
    ppermute x9, starting transfers between devices: 11.2 us -> 11.7 us  [permuted(): return lax.ppermute(value, 'blk', pairs)]
  transfers between devices with their start and end apart: 10 -> 10, of which waited for: 6 -> 3; matrix products, arithmetic and copies ran while one was open for 0% -> 0% of each run, Pallas kernels for 13% -> 17%
where the time goes in v7:
time: 36.1 us; the launch traced here: 35.9 us
  starting transfers between devices  19.2 us (53%)
  Pallas kernels  9.9 us (27%)
  waiting for transfers between devices  6 us (17%)
  other arithmetic  0.65 us (2%)
    ppermute x9, starting transfers between devices, permuted(): return lax.ppermute(value, 'blk', pairs)  11.7 us
    pallas_call x7, Pallas kernels, local_call(): pl.pallas_call(body, out_shape=tuple((jax.ShapeDtypeStruct(shape, kind) f...  9.9 us
    all_to_all x1, starting transfers between devices, per_device(): tiles = lax.all_to_all(joined(total, from_other), 'layer', 0, 0, tiled=True)  7.48 us
    all_to_all x1, waiting for transfers between devices, per_device(): tiles = lax.all_to_all(joined(total, from_other), 'layer', 0, 0, tiled=True)  4.93 us
    ppermute x9, waiting for transfers between devices, permuted(): return lax.ppermute(value, 'blk', pairs)  1.07 us
  transfers between devices with their start and end apart: 10, of which 3 were waited for; matrix products, arithmetic and copies ran while one was open for 0% of the time, Pallas kernels for 17%

profile of v7, /device:TPU:0, one launch (start us, length us, event | category | flops | bytes accessed | tf_op | source)
XLA Modules:
  0.0 35.9 jit_solution(16669469464159842649)
XLA Ops:
  0.0 1.2 %shard_map.46 = (f32[1536,128]{1,0:T(8,128)S(1)}, f32[192,128]{1,0:T(8,128)S(1)}, f32[64,128]{1,0:T(8,128)S(1)}) custom-call(f32[1024,128]{1,0:T(8,128)} %points_hbm.1, f32[64,1024]{1,0:T(8,128)} %bitcast.5, f32[1,128]{1,0:T(1,128)} %bitcast.6, f32[1,128]{1,0:T(1,128)} %bitcast.7), custom_call_target="tpu_custom_call" | custom-call | bytes 1048576 | tf_op jit(solution)/shard_map/pallas_call | solution.py:69
  1.2 0.1 collective-permute-start
  1.3 1.7 %collective-permute-start.1 = (f32[192,128]{1,0:T(8,128)S(1)}, f32[192,128]{1,0:T(8,128)S(1)}, u32[]{:S(2)}, u32[]{:S(2)}) collective-permute-start(f32[192,128]{1,0:T(8,128)S(1)} %get-tuple-element.31.refs_6_), channel_id=1, source_target_pairs={{0,16},{8,24},{16,32},{24,40},{32,48},{40,56},{48,0},{56,8},{64,80... | collective-permute-start | bytes 294920 | tf_op jit(solution)/shard_map/ppermute | solution.py:27
  3.0 2.6 %collective-permute-start.2 = (f32[192,128]{1,0:T(8,128)S(1)}, f32[192,128]{1,0:T(8,128)S(1)}, u32[]{:S(2)}, u32[]{:S(2)}) collective-permute-start(f32[192,128]{1,0:T(8,128)S(1)} %get-tuple-element.31.refs_6_), channel_id=1, source_target_pairs={{0,112},{8,120},{16,64},{24,72},{32,80},{40,88},{48,96},{56,104},{... | collective-permute-start | bytes 294920 | tf_op jit(solution)/shard_map/ppermute | solution.py:27
  5.6 2.0 %collective-permute-start.3 = (f32[192,128]{1,0:T(8,128)S(1)}, f32[192,128]{1,0:T(8,128)S(1)}, u32[]{:S(2)}, u32[]{:S(2)}) collective-permute-start(f32[192,128]{1,0:T(8,128)S(1)} %get-tuple-element.31.refs_6_), channel_id=1, source_target_pairs={{0,32},{8,40},{16,48},{24,56},{32,64},{40,72},{48,80},{56,88},{64,... | collective-permute-start | bytes 294920 | tf_op jit(solution)/shard_map/ppermute | solution.py:27
  7.6 0.5 %collective-permute-start.4 = (f32[192,128]{1,0:T(8,128)S(1)}, f32[192,128]{1,0:T(8,128)S(1)}, u32[]{:S(2)}, u32[]{:S(2)}) collective-permute-start(f32[192,128]{1,0:T(8,128)S(1)} %get-tuple-element.31.refs_6_), channel_id=1, source_target_pairs={{0,64},{8,72},{16,80},{24,88},{32,96},{40,104},{48,112},{56,120},{... | collective-permute-start | bytes 294920 | tf_op jit(solution)/shard_map/ppermute | solution.py:27
  8.1 0.0 collective-permute-done.other_packed
  8.1 0.6 %shard_map.47 = (bf16[1024,768]{1,0:T(8,128)(2,1)S(1)}, f32[1024,128]{1,0:T(8,128)S(1)}, bf16[128,1024]{1,0:T(8,128)(2,1)S(1)}, bf16[1024,768]{1,0:T(8,128)(2,1)...) custom-call(f32[1536,128]{1,0:T(8,128)S(1)} %get-tuple-element.24.packed, ...), custom_call_target="tpu_custom_call" | custom-call | bytes 1048576 | tf_op jit(solution)/shard_map/pallas_call | solution.py:69
  8.7 0.0 collective-permute-done.1.refs_7_
  8.7 2.7 %shard_map.48 = (f32[1024,128]{1,0:T(8,128)S(1)}, f32[1024,128]{1,0:T(8,128)S(1)}, f32[64,128]{1,0:T(8,128)S(1)}) custom-call(bf16[1024,768]{1,0:T(8,128)(2,1)S(1)} %get-tuple-element.25.refs_0_.refs_1_, f32[1024,128]{1,0:T(8,128)S(1)} %get-tuple-element.26.refs_1_.refs_2_, bf16[128,1024]{1,0:T(8,128)(2,1)S(1)} %get-tuple-element.27.refs_2_.refs_3_, ...), custom_call_target="tpu_custom_call" | custom-call | flops 1342177280 | bytes 1048576 | tf_op jit(solution)/shard_map/pallas_call | solution.py:69
  11.4 0.0 collective-permute-done.2.refs_4_.refs_6_
  11.4 1.3 %shard_map.49 = (f32[1024,128]{1,0:T(8,128)S(1)}, f32[128,128]{1,0:T(8,128)S(1)}) custom-call(f32[1024,128]{1,0:T(8,128)S(1)} %get-tuple-element.33.refs_0_, bf16[1024,768]{1,0:T(8,128)(2,1)S(1)} %get-tuple-element.28.refs_3_.refs_1_, f32[1024,128]{1,0:T(8,128)S(1)} %get-tuple-element.29.refs_4_.refs_2_, ...), custom_call_target="tpu_custom_call" | custom-call | flops 335544320 | bytes 1048576 | tf_op jit(solution)/shard_map/pallas_call | solution.py:69
  12.8 0.9 %collective-permute-done.3.refs_4_.refs_7_ = f32[192,128]{1,0:T(8,128)S(1)} collective-permute-done((f32[192,128]{1,0:T(8,128)S(1)}, f32[192,128]{1,0:T(8,128)S(1)}, u32[]{:S(2)}, u32[]{:S(2)}) %collective-permute-start.3) | collective-permute-done | bytes 98336 | tf_op jit(solution)/shard_map/ppermute | solution.py:27
  13.7 0.0 collective-permute-done.4.refs_5_
  13.7 1.8 %shard_map.50 = (f32[8,64,128]{2,1,0:T(8,128)S(1)}, f32[128,128]{1,0:T(8,128)S(1)}) custom-call(f32[1024,128]{1,0:T(8,128)S(1)} %get-tuple-element.35.refs_0_, bf16[1024,768]{1,0:T(8,128)(2,1)S(1)} %get-tuple-element.28.refs_3_.refs_1_, f32[1024,128]{1,0:T(8,128)S(1)} %get-tuple-element.29.refs_4_.refs_2_, ...), custom_call_target="tpu_custom_call" | custom-call | flops 671088640 | bytes 1048576 | tf_op jit(solution)/shard_map/pallas_call | solution.py:69
  15.5 0.1 collective-permute-start.5
  15.6 1.4 %shard_map.51 = (f32[1024,128]{1,0:T(8,128)S(1)}, f32[64,128]{1,0:T(8,128)S(1)}, f32[64,128]{1,0:T(8,128)S(1)}) custom-call(f32[1024,128]{1,0:T(8,128)S(1)} %get-tuple-element.32.refs_0_, bf16[1024,768]{1,0:T(8,128)(2,1)S(1)} %get-tuple-element.25.refs_0_.refs_1_, f32[1024,128]{1,0:T(8,128)S(1)} %get-tuple-element.26.refs_1_.refs_2_, ...), custom_call_target="tpu_custom_call" | custom-call | flops 671088640 | bytes 1048576 | tf_op jit(solution)/shard_map/pallas_call | solution.py:69
  17.0 0.2 collective-permute-done.5.from_other
  17.1 0.9 %shard_map.52 = f32[8,64,128]{2,1,0:T(8,128)} custom-call(f32[1024,128]{1,0:T(8,128)S(1)} %get-tuple-element.37.total, f32[8,64,128]{2,1,0:T(8,128)S(1)} %collective-permute-done.5.from_other), custom_call_target="tpu_custom_call" | custom-call | bytes 1048576 | tf_op jit(solution)/shard_map/pallas_call | solution.py:69
  18.1 7.5 %all-to-all-start = ((f32[8,64,128]{2,1,0:T(8,128)}), f32[8,64,128]{2,1,0:T(8,128)S(1)}, u32[]{:S(2)}, u32[]{:S(2)}) async-start(f32[8,64,128]{2,1,0:T(8,128)} %shard_map.52), calls=%async_computation | async-start | bytes 524288 | tf_op jit(solution)/shard_map/all_to_all | solution.py:314
  25.5 1.8 %collective-permute-start.8 = (f32[64,128]{1,0:T(8,128)S(1)}, f32[64,128]{1,0:T(8,128)S(1)}, u32[]{:S(2)}, u32[]{:S(2)}) collective-permute-start(f32[64,128]{1,0:T(8,128)S(1)} %get-tuple-element.41), channel_id=1, source_target_pairs={{32,0},{40,8},{48,16},{56,24},{64,32},{72,40},{80,48},{88,56},{96,... | collective-permute-start | bytes 98312 | tf_op jit(solution)/shard_map/ppermute | solution.py:27
  27.3 1.2 %collective-permute-start.6 = (f32[64,128]{1,0:T(8,128)S(1)}, f32[64,128]{1,0:T(8,128)S(1)}, u32[]{:S(2)}, u32[]{:S(2)}) collective-permute-start(f32[64,128]{1,0:T(8,128)S(1)} %get-tuple-element.39), channel_id=1, source_target_pairs={{16,0},{24,8},{32,16},{40,24},{48,32},{56,40},{0,48},{8,56},{80,64... | collective-permute-start | bytes 98312 | tf_op jit(solution)/shard_map/ppermute | solution.py:27
  28.6 1.7 %collective-permute-start.7 = (f32[64,128]{1,0:T(8,128)S(1)}, f32[64,128]{1,0:T(8,128)S(1)}, u32[]{:S(2)}, u32[]{:S(2)}) collective-permute-start(f32[64,128]{1,0:T(8,128)S(1)} %get-tuple-element.40), channel_id=1, source_target_pairs={{112,0},{120,8},{64,16},{72,24},{80,32},{88,40},{96,48},{104,56},{... | collective-permute-start | bytes 98312 | tf_op jit(solution)/shard_map/ppermute | solution.py:27
  30.2 4.9 %all-to-all-done = f32[8,64,128]{2,1,0:T(8,128)S(1)} async-done(((f32[8,64,128]{2,1,0:T(8,128)}), f32[8,64,128]{2,1,0:T(8,128)S(1)}, u32[]{:S(2)}, u32[]{:S(2)}) %all-to-all-start) | async-done | bytes 262176 | tf_op jit(solution)/shard_map/all_to_all | solution.py:314
  35.2 0.0 collective-permute-done.8
  35.2 0.0 collective-permute-done.6
  35.2 0.0 collective-permute-done.7
  35.2 0.6 %add_bitcast_fusion = f32[128,64]{0,1:T(8,128)} fusion(f32[64,128]{1,0:T(8,128)S(1)} %get-tuple-element.42, f32[64,128]{1,0:T(8,128)S(1)} %reduce_sum.9, f32[64,128]{1,0:T(8,128)S(1)} %collective-permute-done.8, f32[64,128]{1,0:T(8,128)S(1)} %collective-permute-done.6, f32[64,128]{1,0:T(8,128)S(1)} %collective-permute-done.7), kind=kLoop, calls=%fused_computation | loop fusion | flops 40960 | bytes 196608 | tf_op jit(solution)/shard_map/transpose | solution.py:319
  (1 shorter events, 0.0 us)
Async XLA Ops:
  1.2 6.9 %collective-permute-start = (f32[1536,128]{1,0:T(8,128)S(1)}, f32[1536,128]{1,0:T(8,128)S(1)}, u32[]{:S(2)}, u32[]{:S(2)}) collective-permute-start(f32[1536,128]{1,0:T(8,128)S(1)} %get-tuple-element.24.packed), channel_id=1, source_target_pairs={{0,8},{8,0},{16,24},{24,16},{32,40},{40,32},{48,56},{56,48},{64,72... | collective-permute-start | bytes 2359304 | tf_op jit(solution)/shard_map/ppermute | solution.py:27
  1.3 7.4 %collective-permute-start.1 = (f32[192,128]{1,0:T(8,128)S(1)}, f32[192,128]{1,0:T(8,128)S(1)}, u32[]{:S(2)}, u32[]{:S(2)}) collective-permute-start(f32[192,128]{1,0:T(8,128)S(1)} %get-tuple-element.31.refs_6_), channel_id=1, source_target_pairs={{0,16},{8,24},{16,32},{24,40},{32,48},{40,56},{48,0},{56,8},{64,80... | collective-permute-start | bytes 294920 | tf_op jit(solution)/shard_map/ppermute | solution.py:27
  3.0 8.4 %collective-permute-start.2 = (f32[192,128]{1,0:T(8,128)S(1)}, f32[192,128]{1,0:T(8,128)S(1)}, u32[]{:S(2)}, u32[]{:S(2)}) collective-permute-start(f32[192,128]{1,0:T(8,128)S(1)} %get-tuple-element.31.refs_6_), channel_id=1, source_target_pairs={{0,112},{8,120},{16,64},{24,72},{32,80},{40,88},{48,96},{56,104},{... | collective-permute-start | bytes 294920 | tf_op jit(solution)/shard_map/ppermute | solution.py:27
  5.6 8.1 %collective-permute-start.3 = (f32[192,128]{1,0:T(8,128)S(1)}, f32[192,128]{1,0:T(8,128)S(1)}, u32[]{:S(2)}, u32[]{:S(2)}) collective-permute-start(f32[192,128]{1,0:T(8,128)S(1)} %get-tuple-element.31.refs_6_), channel_id=1, source_target_pairs={{0,32},{8,40},{16,48},{24,56},{32,64},{40,72},{48,80},{56,88},{64,... | collective-permute-start | bytes 294920 | tf_op jit(solution)/shard_map/ppermute | solution.py:27
  7.6 6.1 %collective-permute-start.4 = (f32[192,128]{1,0:T(8,128)S(1)}, f32[192,128]{1,0:T(8,128)S(1)}, u32[]{:S(2)}, u32[]{:S(2)}) collective-permute-start(f32[192,128]{1,0:T(8,128)S(1)} %get-tuple-element.31.refs_6_), channel_id=1, source_target_pairs={{0,64},{8,72},{16,80},{24,88},{32,96},{40,104},{48,112},{56,120},{... | collective-permute-start | bytes 294920 | tf_op jit(solution)/shard_map/ppermute | solution.py:27
  15.5 1.6 %collective-permute-start.5 = (f32[8,64,128]{2,1,0:T(8,128)S(1)}, f32[8,64,128]{2,1,0:T(8,128)S(1)}, u32[]{:S(2)}, u32[]{:S(2)}) collective-permute-start(f32[8,64,128]{2,1,0:T(8,128)S(1)} %get-tuple-element.38), channel_id=1, source_target_pairs={{0,8},{8,0},{16,24},{24,16},{32,40},{40,32},{48,56},{56,48},{64,72... | collective-permute-start | bytes 786440 | tf_op jit(solution)/shard_map/ppermute | solution.py:27
  18.1 17.1 %all-to-all-start = ((f32[8,64,128]{2,1,0:T(8,128)}), f32[8,64,128]{2,1,0:T(8,128)S(1)}, u32[]{:S(2)}, u32[]{:S(2)}) async-start(f32[8,64,128]{2,1,0:T(8,128)} %shard_map.52), calls=%async_computation | async-start | bytes 524288 | tf_op jit(solution)/shard_map/all_to_all | solution.py:314
  25.5 9.7 %collective-permute-start.8 = (f32[64,128]{1,0:T(8,128)S(1)}, f32[64,128]{1,0:T(8,128)S(1)}, u32[]{:S(2)}, u32[]{:S(2)}) collective-permute-start(f32[64,128]{1,0:T(8,128)S(1)} %get-tuple-element.41), channel_id=1, source_target_pairs={{32,0},{40,8},{48,16},{56,24},{64,32},{72,40},{80,48},{88,56},{96,... | collective-permute-start | bytes 98312 | tf_op jit(solution)/shard_map/ppermute | solution.py:27
  27.3 7.9 %collective-permute-start.6 = (f32[64,128]{1,0:T(8,128)S(1)}, f32[64,128]{1,0:T(8,128)S(1)}, u32[]{:S(2)}, u32[]{:S(2)}) collective-permute-start(f32[64,128]{1,0:T(8,128)S(1)} %get-tuple-element.39), channel_id=1, source_target_pairs={{16,0},{24,8},{32,16},{40,24},{48,32},{56,40},{0,48},{8,56},{80,64... | collective-permute-start | bytes 98312 | tf_op jit(solution)/shard_map/ppermute | solution.py:27
  28.6 6.6 %collective-permute-start.7 = (f32[64,128]{1,0:T(8,128)S(1)}, f32[64,128]{1,0:T(8,128)S(1)}, u32[]{:S(2)}, u32[]{:S(2)}) collective-permute-start(f32[64,128]{1,0:T(8,128)S(1)} %get-tuple-element.40), channel_id=1, source_target_pairs={{112,0},{120,8},{64,16},{72,24},{80,32},{88,40},{96,48},{104,56},{... | collective-permute-start | bytes 98312 | tf_op jit(solution)/shard_map/ppermute | solution.py:27

commit v8 on v7

--- a/solution.py
+++ b/solution.py
@@ -214,34 +214,25 @@
     )
 
 
-def first_sides(packed, other_packed, columns):
+def near_tiles(packed, other_packed, piece, arrived):
     feats = packed.shape[1]
+    columns = piece.shape[0] - LANES
     rows = packed.shape[0] * LANES // (LANES + columns)
 
-    def body(packed, other_packed, *refs):
-        load_left(packed, *refs[:3])
-        load_left(other_packed, *refs[3:])
-
-    side = side_shapes(rows, feats, columns)[1:]
-    out = local_call(body, side + side, (packed, other_packed))
-    return out[:3], out[3:]
-
-
-def near_tiles(own, other, piece, arrived):
-    rows, columns = own[0].shape[0], own[2].shape[0] // 2
-
-    def body(*refs):
-        own_side, other_side = refs[:3], refs[3:6]
-        piece, arrived, total, other_total, back_ref = refs[6:]
+    def body(packed, other_packed, piece, arrived, *refs):
+        (total, *own), (other_total, *other), back_ref = refs[:4], refs[4:8], refs[8]
+        load_left(packed, *own)
+        load_left(other_packed, *other)
         loaded = load_right((arrived, piece))
-        mirrored = tile_products(own_side, loaded, None, total, None, 1)
-        mirrored = tile_products(other_side, loaded, None, other_total, mirrored, 1)
+        mirrored = tile_products(own, loaded, None, total, None, 1)
+        mirrored = tile_products(other, loaded, None, other_total, mirrored, 1)
         back_ref[...] = folded(mirrored)
 
-    total_shape = ((rows, 2 * columns), F32)
-    outs = (total_shape, total_shape, ((columns, LANES), F32))
-    macs = macs_of(2 * rows, own[0].shape[1] // 6, columns, 2)
-    return local_call(body, outs, (*own, *other, piece, arrived), macs=macs)
+    side = side_shapes(rows, feats, columns)
+    outs = side + side + (((columns, LANES), F32),)
+    macs = macs_of(2 * rows, feats, columns, 2)
+    out = local_call(body, outs, (packed, other_packed, piece, arrived), macs=macs)
+    return out[:4], out[4:8], out[8]
 
 
 def middle_tile(side, piece):
@@ -304,8 +295,9 @@
     middle_piece = stepped(piece, MIDDLE)
     far_piece = stepped(piece, FAR)
     ring_piece = stepped(piece, ACROSS)
-    own, other = first_sides(packed, other_packed, vectors.shape[1])
-    total, other_total, near_back = near_tiles(own, other, piece, near_piece)
+    (total, *own), (other_total, *other), near_back = near_tiles(
+        packed, other_packed, piece, near_piece
+    )
     other_total, middle_part = middle_tile((other_total, *other), middle_piece)
     for_other, far_part = other_tiles((other_total, *other), (far_piece, ring_piece))
     from_other = swapped(for_other)

time: 36.1 us -> 36.1 us (level)
  waiting for transfers between devices: 6 us -> 6.39 us
  Pallas kernels: 9.9 us -> 9.53 us
    ppermute x9, waiting for transfers between devices: 1.07 us -> 1.46 us  [permuted(): return lax.ppermute(value, 'blk', pairs)]
    pallas_call x7 -> x6, Pallas kernels: 9.9 us -> 9.53 us  [local_call(): pl.pallas_call(body, out_shape=tuple((jax.ShapeDtypeStruct(shape, kind) f...]
  transfers between devices with their start and end apart: 10 -> 10, of which waited for: 3 -> 3; matrix products, arithmetic and copies ran while one was open for 0% -> 0% of each run, Pallas kernels for 17% -> 16%
where the time goes in v8:
time: 36.1 us; the launch traced here: 35.8 us
  starting transfers between devices  19.2 us (53%)
  Pallas kernels  9.53 us (26%)
  waiting for transfers between devices  6.39 us (18%)
  other arithmetic  0.65 us (2%)
    ppermute x9, starting transfers between devices, permuted(): return lax.ppermute(value, 'blk', pairs)  11.7 us
    pallas_call x6, Pallas kernels, local_call(): pl.pallas_call(body, out_shape=tuple((jax.ShapeDtypeStruct(shape, kind) f...  9.53 us
    all_to_all x1, starting transfers between devices, per_device(): tiles = lax.all_to_all(joined(total, from_other), 'layer', 0, 0, tiled=True)  7.48 us
    all_to_all x1, waiting for transfers between devices, per_device(): tiles = lax.all_to_all(joined(total, from_other), 'layer', 0, 0, tiled=True)  4.93 us
    ppermute x9, waiting for transfers between devices, permuted(): return lax.ppermute(value, 'blk', pairs)  1.46 us
  transfers between devices with their start and end apart: 10, of which 3 were waited for; matrix products, arithmetic and copies ran while one was open for 0% of the time, Pallas kernels for 16%

profile of v8, /device:TPU:0, one launch (start us, length us, event | category | flops | bytes accessed | tf_op | source)
XLA Modules:
  0.0 35.8 jit_solution(16858941131945824158)
XLA Ops:
  0.0 1.2 %shard_map.46 = (f32[1536,128]{1,0:T(8,128)S(1)}, f32[192,128]{1,0:T(8,128)S(1)}, f32[64,128]{1,0:T(8,128)S(1)}) custom-call(f32[1024,128]{1,0:T(8,128)} %points_hbm.1, f32[64,1024]{1,0:T(8,128)} %bitcast.5, f32[1,128]{1,0:T(1,128)} %bitcast.6, f32[1,128]{1,0:T(1,128)} %bitcast.7), custom_call_target="tpu_custom_call" | custom-call | bytes 1048576 | tf_op jit(solution)/shard_map/pallas_call | solution.py:69
  1.2 0.1 collective-permute-start
  1.3 1.7 %collective-permute-start.1 = (f32[192,128]{1,0:T(8,128)S(1)}, f32[192,128]{1,0:T(8,128)S(1)}, u32[]{:S(2)}, u32[]{:S(2)}) collective-permute-start(f32[192,128]{1,0:T(8,128)S(1)} %get-tuple-element.25.piece), channel_id=1, source_target_pairs={{0,16},{8,24},{16,32},{24,40},{32,48},{40,56},{48,0},{56,8},{64,80... | collective-permute-start | bytes 294920 | tf_op jit(solution)/shard_map/ppermute | solution.py:27
  3.0 2.6 %collective-permute-start.2 = (f32[192,128]{1,0:T(8,128)S(1)}, f32[192,128]{1,0:T(8,128)S(1)}, u32[]{:S(2)}, u32[]{:S(2)}) collective-permute-start(f32[192,128]{1,0:T(8,128)S(1)} %get-tuple-element.25.piece), channel_id=1, source_target_pairs={{0,112},{8,120},{16,64},{24,72},{32,80},{40,88},{48,96},{56,104},{... | collective-permute-start | bytes 294920 | tf_op jit(solution)/shard_map/ppermute | solution.py:27
  5.6 2.0 %collective-permute-start.3 = (f32[192,128]{1,0:T(8,128)S(1)}, f32[192,128]{1,0:T(8,128)S(1)}, u32[]{:S(2)}, u32[]{:S(2)}) collective-permute-start(f32[192,128]{1,0:T(8,128)S(1)} %get-tuple-element.25.piece), channel_id=1, source_target_pairs={{0,32},{8,40},{16,48},{24,56},{32,64},{40,72},{48,80},{56,88},{64,... | collective-permute-start | bytes 294920 | tf_op jit(solution)/shard_map/ppermute | solution.py:27
  7.6 0.5 %collective-permute-start.4 = (f32[192,128]{1,0:T(8,128)S(1)}, f32[192,128]{1,0:T(8,128)S(1)}, u32[]{:S(2)}, u32[]{:S(2)}) collective-permute-start(f32[192,128]{1,0:T(8,128)S(1)} %get-tuple-element.25.piece), channel_id=1, source_target_pairs={{0,64},{8,72},{16,80},{24,88},{32,96},{40,104},{48,112},{56,120},{... | collective-permute-start | bytes 294920 | tf_op jit(solution)/shard_map/ppermute | solution.py:27
  8.1 0.0 collective-permute-done.1.arrived
  8.1 0.0 collective-permute-done.other_packed
  8.1 2.9 %shard_map.47 = (f32[1024,128]{1,0:T(8,128)S(1)}, bf16[1024,768]{1,0:T(8,128)(2,1)S(1)}, f32[1024,128]{1,0:T(8,128)S(1)}, bf16[128,1024]{1,0:T(8,128)(2,1)S(1)},...) custom-call(f32[1536,128]{1,0:T(8,128)S(1)} %get-tuple-element.24.pa, ...), custom_call_target="tpu_custom_call" | custom-call | flops 1342177280 | bytes 1048576 | tf_op jit(solution)/shard_map/pallas_call | solution.py:69
  11.0 0.0 collective-permute-done.2.refs_4_.refs_6_
  11.0 1.3 %shard_map.48 = (f32[1024,128]{1,0:T(8,128)S(1)}, f32[128,128]{1,0:T(8,128)S(1)}) custom-call(f32[1024,128]{1,0:T(8,128)S(1)} %get-tuple-element.30.refs_0_, bf16[1024,768]{1,0:T(8,128)(2,1)S(1)} %get-tuple-element.31.refs_1_, f32[1024,128]{1,0:T(8,128)S(1)} %get-tuple-element.32.refs_2_, bf16[128,1024]{1,0:T(8,128)(2,1)S(1)} %get-tuple-element.33.refs_3_, ...), custom_call_target="tpu_custom_call" | custom-call | flops 335544320 | bytes 1048576 | tf_op jit(solution)/shard_map/pallas_call | solution.py:69
  12.4 1.3 %collective-permute-done.3.refs_4_.refs_7_ = f32[192,128]{1,0:T(8,128)S(1)} collective-permute-done((f32[192,128]{1,0:T(8,128)S(1)}, f32[192,128]{1,0:T(8,128)S(1)}, u32[]{:S(2)}, u32[]{:S(2)}) %collective-permute-start.3) | collective-permute-done | bytes 98336 | tf_op jit(solution)/shard_map/ppermute | solution.py:27
  13.7 0.0 collective-permute-done.4.refs_5_
  13.7 1.8 %shard_map.49 = (f32[8,64,128]{2,1,0:T(8,128)S(1)}, f32[128,128]{1,0:T(8,128)S(1)}) custom-call(f32[1024,128]{1,0:T(8,128)S(1)} %get-tuple-element.35.refs_0_, bf16[1024,768]{1,0:T(8,128)(2,1)S(1)} %get-tuple-element.31.refs_1_, f32[1024,128]{1,0:T(8,128)S(1)} %get-tuple-element.32.refs_2_, bf16[128,1024]{1,0:T(8,128)(2,1)S(1)} %get-tuple-element.33.refs_3_, ...), custom_call_target="tpu_custom_call" | custom-call | flops 671088640 | bytes 1048576 | tf_op jit(solution)/shard_map/pallas_call | solution.py:69
  15.5 0.1 collective-permute-start.5
  15.6 1.4 %shard_map.50 = (f32[1024,128]{1,0:T(8,128)S(1)}, f32[64,128]{1,0:T(8,128)S(1)}, f32[64,128]{1,0:T(8,128)S(1)}) custom-call(f32[1024,128]{1,0:T(8,128)S(1)} %get-tuple-element.26.refs_0_, bf16[1024,768]{1,0:T(8,128)(2,1)S(1)} %get-tuple-element.27.refs_1_, f32[1024,128]{1,0:T(8,128)S(1)} %get-tuple-element.28.refs_2_, ...), custom_call_target="tpu_custom_call" | custom-call | flops 671088640 | bytes 1048576 | tf_op jit(solution)/shard_map/pallas_call | solution.py:69
  17.0 0.2 collective-permute-done.5.from_other
  17.1 0.9 %shard_map.51 = f32[8,64,128]{2,1,0:T(8,128)} custom-call(f32[1024,128]{1,0:T(8,128)S(1)} %get-tuple-element.37.total, f32[8,64,128]{2,1,0:T(8,128)S(1)} %collective-permute-done.5.from_other), custom_call_target="tpu_custom_call" | custom-call | bytes 1048576 | tf_op jit(solution)/shard_map/pallas_call | solution.py:69
  18.0 7.5 %all-to-all-start = ((f32[8,64,128]{2,1,0:T(8,128)}), f32[8,64,128]{2,1,0:T(8,128)S(1)}, u32[]{:S(2)}, u32[]{:S(2)}) async-start(f32[8,64,128]{2,1,0:T(8,128)} %shard_map.51), calls=%async_computation | async-start | bytes 524288 | tf_op jit(solution)/shard_map/all_to_all | solution.py:306
  25.5 1.8 %collective-permute-start.8 = (f32[64,128]{1,0:T(8,128)S(1)}, f32[64,128]{1,0:T(8,128)S(1)}, u32[]{:S(2)}, u32[]{:S(2)}) collective-permute-start(f32[64,128]{1,0:T(8,128)S(1)} %get-tuple-element.41), channel_id=1, source_target_pairs={{32,0},{40,8},{48,16},{56,24},{64,32},{72,40},{80,48},{88,56},{96,... | collective-permute-start | bytes 98312 | tf_op jit(solution)/shard_map/ppermute | solution.py:27
  27.3 1.2 %collective-permute-start.6 = (f32[64,128]{1,0:T(8,128)S(1)}, f32[64,128]{1,0:T(8,128)S(1)}, u32[]{:S(2)}, u32[]{:S(2)}) collective-permute-start(f32[64,128]{1,0:T(8,128)S(1)} %get-tuple-element.39), channel_id=1, source_target_pairs={{16,0},{24,8},{32,16},{40,24},{48,32},{56,40},{0,48},{8,56},{80,64... | collective-permute-start | bytes 98312 | tf_op jit(solution)/shard_map/ppermute | solution.py:27
  28.6 1.7 %collective-permute-start.7 = (f32[64,128]{1,0:T(8,128)S(1)}, f32[64,128]{1,0:T(8,128)S(1)}, u32[]{:S(2)}, u32[]{:S(2)}) collective-permute-start(f32[64,128]{1,0:T(8,128)S(1)} %get-tuple-element.40), channel_id=1, source_target_pairs={{112,0},{120,8},{64,16},{72,24},{80,32},{88,40},{96,48},{104,56},{... | collective-permute-start | bytes 98312 | tf_op jit(solution)/shard_map/ppermute | solution.py:27
  30.2 4.9 %all-to-all-done = f32[8,64,128]{2,1,0:T(8,128)S(1)} async-done(((f32[8,64,128]{2,1,0:T(8,128)}), f32[8,64,128]{2,1,0:T(8,128)S(1)}, u32[]{:S(2)}, u32[]{:S(2)}) %all-to-all-start) | async-done | bytes 262176 | tf_op jit(solution)/shard_map/all_to_all | solution.py:306
  35.2 0.0 collective-permute-done.8
  35.2 0.0 collective-permute-done.6
  35.2 0.0 collective-permute-done.7
  35.2 0.6 %add_bitcast_fusion = f32[128,64]{0,1:T(8,128)} fusion(f32[64,128]{1,0:T(8,128)S(1)} %get-tuple-element.42, f32[64,128]{1,0:T(8,128)S(1)} %reduce_sum.9, f32[64,128]{1,0:T(8,128)S(1)} %collective-permute-done.8, f32[64,128]{1,0:T(8,128)S(1)} %collective-permute-done.6, f32[64,128]{1,0:T(8,128)S(1)} %collective-permute-done.7), kind=kLoop, calls=%fused_computation | loop fusion | flops 40960 | bytes 196608 | tf_op jit(solution)/shard_map/transpose | solution.py:311
  (1 shorter events, 0.0 us)
Async XLA Ops:
  1.2 6.9 %collective-permute-start = (f32[1536,128]{1,0:T(8,128)S(1)}, f32[1536,128]{1,0:T(8,128)S(1)}, u32[]{:S(2)}, u32[]{:S(2)}) collective-permute-start(f32[1536,128]{1,0:T(8,128)S(1)} %get-tuple-element.24.packed), channel_id=1, source_target_pairs={{0,8},{8,0},{16,24},{24,16},{32,40},{40,32},{48,56},{56,48},{64,72... | collective-permute-start | bytes 2359304 | tf_op jit(solution)/shard_map/ppermute | solution.py:27
  1.3 6.8 %collective-permute-start.1 = (f32[192,128]{1,0:T(8,128)S(1)}, f32[192,128]{1,0:T(8,128)S(1)}, u32[]{:S(2)}, u32[]{:S(2)}) collective-permute-start(f32[192,128]{1,0:T(8,128)S(1)} %get-tuple-element.25.piece), channel_id=1, source_target_pairs={{0,16},{8,24},{16,32},{24,40},{32,48},{40,56},{48,0},{56,8},{64,80... | collective-permute-start | bytes 294920 | tf_op jit(solution)/shard_map/ppermute | solution.py:27
  3.0 8.0 %collective-permute-start.2 = (f32[192,128]{1,0:T(8,128)S(1)}, f32[192,128]{1,0:T(8,128)S(1)}, u32[]{:S(2)}, u32[]{:S(2)}) collective-permute-start(f32[192,128]{1,0:T(8,128)S(1)} %get-tuple-element.25.piece), channel_id=1, source_target_pairs={{0,112},{8,120},{16,64},{24,72},{32,80},{40,88},{48,96},{56,104},{... | collective-permute-start | bytes 294920 | tf_op jit(solution)/shard_map/ppermute | solution.py:27
  5.6 8.1 %collective-permute-start.3 = (f32[192,128]{1,0:T(8,128)S(1)}, f32[192,128]{1,0:T(8,128)S(1)}, u32[]{:S(2)}, u32[]{:S(2)}) collective-permute-start(f32[192,128]{1,0:T(8,128)S(1)} %get-tuple-element.25.piece), channel_id=1, source_target_pairs={{0,32},{8,40},{16,48},{24,56},{32,64},{40,72},{48,80},{56,88},{64,... | collective-permute-start | bytes 294920 | tf_op jit(solution)/shard_map/ppermute | solution.py:27
  7.6 6.1 %collective-permute-start.4 = (f32[192,128]{1,0:T(8,128)S(1)}, f32[192,128]{1,0:T(8,128)S(1)}, u32[]{:S(2)}, u32[]{:S(2)}) collective-permute-start(f32[192,128]{1,0:T(8,128)S(1)} %get-tuple-element.25.piece), channel_id=1, source_target_pairs={{0,64},{8,72},{16,80},{24,88},{32,96},{40,104},{48,112},{56,120},{... | collective-permute-start | bytes 294920 | tf_op jit(solution)/shard_map/ppermute | solution.py:27
  15.5 1.6 %collective-permute-start.5 = (f32[8,64,128]{2,1,0:T(8,128)S(1)}, f32[8,64,128]{2,1,0:T(8,128)S(1)}, u32[]{:S(2)}, u32[]{:S(2)}) collective-permute-start(f32[8,64,128]{2,1,0:T(8,128)S(1)} %get-tuple-element.38), channel_id=1, source_target_pairs={{0,8},{8,0},{16,24},{24,16},{32,40},{40,32},{48,56},{56,48},{64,72... | collective-permute-start | bytes 786440 | tf_op jit(solution)/shard_map/ppermute | solution.py:27
  18.0 17.1 %all-to-all-start = ((f32[8,64,128]{2,1,0:T(8,128)}), f32[8,64,128]{2,1,0:T(8,128)S(1)}, u32[]{:S(2)}, u32[]{:S(2)}) async-start(f32[8,64,128]{2,1,0:T(8,128)} %shard_map.51), calls=%async_computation | async-start | bytes 524288 | tf_op jit(solution)/shard_map/all_to_all | solution.py:306
  25.5 9.7 %collective-permute-start.8 = (f32[64,128]{1,0:T(8,128)S(1)}, f32[64,128]{1,0:T(8,128)S(1)}, u32[]{:S(2)}, u32[]{:S(2)}) collective-permute-start(f32[64,128]{1,0:T(8,128)S(1)} %get-tuple-element.41), channel_id=1, source_target_pairs={{32,0},{40,8},{48,16},{56,24},{64,32},{72,40},{80,48},{88,56},{96,... | collective-permute-start | bytes 98312 | tf_op jit(solution)/shard_map/ppermute | solution.py:27
  27.3 7.9 %collective-permute-start.6 = (f32[64,128]{1,0:T(8,128)S(1)}, f32[64,128]{1,0:T(8,128)S(1)}, u32[]{:S(2)}, u32[]{:S(2)}) collective-permute-start(f32[64,128]{1,0:T(8,128)S(1)} %get-tuple-element.39), channel_id=1, source_target_pairs={{16,0},{24,8},{32,16},{40,24},{48,32},{56,40},{0,48},{8,56},{80,64... | collective-permute-start | bytes 98312 | tf_op jit(solution)/shard_map/ppermute | solution.py:27
  28.6 6.6 %collective-permute-start.7 = (f32[64,128]{1,0:T(8,128)S(1)}, f32[64,128]{1,0:T(8,128)S(1)}, u32[]{:S(2)}, u32[]{:S(2)}) collective-permute-start(f32[64,128]{1,0:T(8,128)S(1)} %get-tuple-element.40), channel_id=1, source_target_pairs={{112,0},{120,8},{64,16},{72,24},{80,32},{88,40},{96,48},{104,56},{... | collective-permute-start | bytes 98312 | tf_op jit(solution)/shard_map/ppermute | solution.py:27
